TPU v7x, 32 devices: a whole 2x2x4 slice. The times are simulated.
32 devices in a mesh: dp: 16 (over z, x, core), tensor: 2 (over y).
Axes of the slice: x: 2, y: 2, z: 4, core: 2. Of those that a mesh axis runs over, the one named last changes fastest.
Arguments:
- block_input: bfloat16 [16384, 1024], P(('dp', 'tensor')), may hold values from -6 to 6
- segment_ids: int32 [16, 1024], P('dp'), may hold values from 0 to 3, never falling along the last dimension, each value on 1 to 512 neighbouring positions
- out_grad: bfloat16 [16384, 1024], P(('dp', 'tensor')), may hold values from -6 to 6
- gating_weight: bfloat16 [1024, 1536], P(None, 'tensor'), may hold values from -0.1875 to 0.1875
- inner_weight: bfloat16 [1024, 1536], P(None, 'tensor'), may hold values from -0.1875 to 0.1875
- state_weight: bfloat16 [1024, 256], replicated, may hold values from -0.1875 to 0.1875
- step_weight: bfloat16 [1024, 24], P(None, 'tensor'), may hold values from -0.1875 to 0.1875
- step_bias: float32 [24], P('tensor'), may hold values from -6.5 to -2.5
- decay_log: float32 [24], P('tensor'), may hold values from 0 to 2.77
- skip_scale: float32 [24], P('tensor'), may hold values from 0.5 to 1.5
- inner_conv: bfloat16 [4, 1536], P(None, 'tensor'), may hold values from -3 to 3
- state_conv: bfloat16 [4, 256], replicated, may hold values from -3 to 3
- mixer_gain: bfloat16 [1536], P('tensor'), may hold values from 0.5 to 1.5
- mixer_proj: bfloat16 [1536, 1024], P('tensor'), may hold values from -0.15625 to 0.15625
- query_weight: bfloat16 [1024, 512], P(None, 'tensor'), may hold values from -0.1875 to 0.1875
- key_weight: bfloat16 [1024, 128], P(None, 'tensor'), may hold values from -0.1875 to 0.1875
- value_weight: bfloat16 [1024, 128], P(None, 'tensor'), may hold values from -0.1875 to 0.1875
- attention_out: bfloat16 [512, 1024], P('tensor'), may hold values from -1 to 1
- first_gain: bfloat16 [1024], replicated, may hold values from 0.5 to 1.5
- second_gain: bfloat16 [1024], replicated, may hold values from 0.5 to 1.5
- gate_weight: bfloat16 [1024, 2048], P(None, 'tensor'), may hold values from -0.1875 to 0.1875
- up_weight: bfloat16 [1024, 2048], P(None, 'tensor'), may hold values from -0.1875 to 0.1875
- down_projection_weight: bfloat16 [2048, 1024], P('tensor'), may hold values from -0.125 to 0.125
Outputs:
- block_output: bfloat16 [16384, 1024], P(('dp', 'tensor'))
- input_grad: float32 [16384, 1024], P(('dp', 'tensor'))
- grad_gating: float32 [1024, 1536], P(None, 'tensor')
- grad_inner: float32 [1024, 1536], P(None, 'tensor')
- grad_state: float32 [1024, 256], replicated
- grad_step: float32 [1024, 24], P(None, 'tensor')
- grad_step_bias: float32 [24], P('tensor')
- grad_decay_log: float32 [24], P('tensor')
- grad_skip_scale: float32 [24], P('tensor')
- grad_inner_conv: float32 [4, 1536], P(None, 'tensor')
- grad_state_conv: float32 [4, 256], replicated
- grad_mixer_gain: float32 [1536], P('tensor')
- grad_mixer_proj: float32 [1536, 1024], P('tensor')
- grad_query: float32 [1024, 512], P(None, 'tensor')
- grad_key: float32 [1024, 128], P(None, 'tensor')
- grad_value: float32 [1024, 128], P(None, 'tensor')
- attention_output_gradient: float32 [512, 1024], P('tensor')
- grad_first_gain: float32 [1024], replicated
- grad_second_gain: float32 [1024], replicated
- grad_gate: float32 [1024, 2048], P(None, 'tensor')
- grad_up: float32 [1024, 2048], P(None, 'tensor')
- grad_down: float32 [2048, 1024], P('tensor')
Inputs may be any that keep to these rules, and one draw needn't show every extreme that they name: `segment_ids`: segment numbers never fall along a sequence; each segment has at most 512 tokens.
All inputs are finite; a program needn't handle non-finite values.
Results may differ from a plain program's by a relative error of at most 0.014.
Values may be sent and summed in bfloat16 or wider, within the bound.
No kernel may reach another device: no remote copies, remote signals or barrier semaphores. Data moves between devices by JAX's collectives and lax.ppermute only.
A program may use at most 192 MiB of HBM per device.

v0:
```python
import jax
import jax.numpy as jnp
from jax import lax
from jax.sharding import PartitionSpec as P

H_SSM = 24
P_SIZE = 64
HD = 64
SPAN = 128
ATT_BLOCK = 512


epsilon = 1e-05
rope_base = 100000000000.0
top_precision = lax.Precision.HIGHEST


def dense(left_side, right_side):
    return jnp.dot(left_side, right_side, preferred_element_type=jnp.float32)


def row_dot(left_side, right_side):
    return lax.dot_general(
        left_side, right_side, (((0,), (0,)), ((), ())), preferred_element_type=jnp.float32
    )


def back_dot(left_side, right_side):
    return lax.dot_general(
        left_side, right_side, (((1,), (1,)), ((), ())), preferred_element_type=jnp.float32
    )


def causal_conv(value_tensor, kernel):
    tap_count = kernel.shape[0]
    length = value_tensor.shape[1]
    padded = jnp.pad(value_tensor, ((0, 0), (tap_count - 1, 0), (0, 0)))
    result = padded[:, 0:length] * kernel[0]
    for offset in range(1, tap_count):
        result = result + padded[:, offset : offset + length] * kernel[offset]
    return result


def rope_tables(length, head_size):
    positions = jnp.arange(length, dtype=jnp.float32)
    frequency = rope_base ** (-jnp.arange(0, head_size, 2, dtype=jnp.float32) / head_size)
    angles = positions[:, None] * frequency[None, :]
    angles = jnp.concatenate([angles, angles], axis=-1)
    return (jnp.cos(angles)[:, None, :], jnp.sin(angles)[:, None, :])


def rotate(value_tensor, cosine, sine_table):
    half_size = value_tensor.shape[-1] // 2
    turned = jnp.concatenate(
        [-value_tensor[..., half_size:], value_tensor[..., :half_size]], axis=-1
    )
    return value_tensor * cosine + turned * sine_table


def unrotate(grad_values, cosine, sine_table):
    half_size = grad_values.shape[-1] // 2
    product = grad_values * sine_table
    turned = jnp.concatenate([product[..., half_size:], -product[..., :half_size]], axis=-1)
    return grad_values * cosine + turned


def norm_back(grad_values, value_tensor, inverse, gain_vector):
    scaled = grad_values * gain_vector
    return inverse * scaled - value_tensor * inverse**3 * jnp.mean(
        value_tensor * scaled, axis=-1, keepdims=True
    )


def ssd_spans(inner, in_vec, out_vec, step_sizes, decay_rate):
    seq_count, length, head_count, head_size = inner.shape
    state_size = in_vec.shape[-1]
    block_count = length // SPAN

    def to_blocks(value_tensor):
        return jnp.swapaxes(
            value_tensor.reshape((seq_count, block_count, SPAN) + value_tensor.shape[2:]), 0, 1
        )

    lower_mask = jnp.arange(SPAN)[:, None] >= jnp.arange(SPAN)[None, :]

    def one_block(carry_state, pieces):
        inner_block, in_block, out_block, step_block = pieces
        cumulative = jnp.cumsum(step_block * decay_rate, axis=1)
        log_gaps = cumulative[:, :, None, :] - cumulative[:, None, :, :]
        within = jnp.exp(jnp.where(lower_mask[None, :, :, None], log_gaps, -1e30))
        scores = jnp.einsum("stn,sun->stu", out_block, in_block, precision=top_precision)
        mixing = scores[..., None] * within * step_block[:, None, :, :]
        within_block = jnp.einsum("stuh,suhp->sthp", mixing, inner_block, precision=top_precision)
        from_state = (
            jnp.einsum("stn,shpn->sthp", out_block, carry_state, precision=top_precision)
            * jnp.exp(cumulative)[..., None]
        )
        tail_weight = jnp.exp(cumulative[:, -1:, :] - cumulative) * step_block
        carry_state = carry_state * jnp.exp(cumulative[:, -1, :])[:, :, None, None] + jnp.einsum(
            "suh,suhp,sun->shpn", tail_weight, inner_block, in_block, precision=top_precision
        )
        return (carry_state, within_block + from_state)

    initial = jnp.zeros((seq_count, head_count, head_size, state_size), inner.dtype)
    final_state, outputs = lax.scan(
        jax.checkpoint(one_block),
        initial,
        (to_blocks(inner), to_blocks(in_vec), to_blocks(out_vec), to_blocks(step_sizes)),
    )
    return jnp.swapaxes(outputs, 0, 1).reshape(seq_count, length, head_count, head_size)


def state_piece(pre_values, conv_kernel):
    return jax.nn.silu(causal_conv(pre_values, conv_kernel))


def mixer_piece(
    inner_pre, state_act, step_pre, gating_pre, inner_conv, step_bias, decay_log, skip_scale
):
    seq_count, length, channels = inner_pre.shape
    head_count = step_pre.shape[-1]
    state_size = state_act.shape[-1] // 2
    inner_act = jax.nn.silu(causal_conv(inner_pre, inner_conv))
    step_sizes = jax.nn.softplus(step_pre + step_bias)
    decay_rate = -jnp.exp(decay_log)
    split_act = inner_act.reshape(seq_count, length, head_count, channels // head_count)
    scanned = ssd_spans(
        split_act, state_act[..., :state_size], state_act[..., state_size:], step_sizes, decay_rate
    )
    scanned = scanned + skip_scale[:, None] * split_act
    return scanned.reshape(seq_count, length, channels) * jax.nn.silu(gating_pre)


def on_device(
    block_input,
    segment_ids,
    out_grad,
    gating_weight,
    inner_weight,
    state_weight,
    step_weight,
    step_bias,
    decay_log,
    skip_scale,
    inner_conv,
    state_conv,
    mixer_gain,
    mixer_proj,
    query_weight,
    key_weight,
    value_weight,
    attention_out,
    first_gain,
    second_gain,
    gate_weight,
    up_weight,
    down_projection_weight,
):
    seq_count, seq_len = segment_ids.shape
    token_count = seq_count * seq_len
    channels = inner_weight.shape[1]
    head_local = step_weight.shape[1]
    query_heads = query_weight.shape[1] // HD
    kv_heads = key_weight.shape[1] // HD
    group_width = query_heads // kv_heads
    scale_factor = HD ** (-0.5)
    mixer_width = H_SSM * P_SIZE
    dp_count = lax.axis_size("dp")
    tensor_place = lax.axis_index("tensor")

    def as_sequences(value_tensor):
        return value_tensor.reshape(seq_count, seq_len, value_tensor.shape[-1])

    def to_rows(value_tensor):
        return value_tensor.reshape(token_count, -1).astype(jnp.bfloat16)

    def flat_rows(value_tensor):
        return value_tensor.reshape(dp_count, -1)

    def widen_piece(part_values, full_width):
        offset_col = tensor_place * part_values.shape[-1]
        zeros_full = jnp.zeros(part_values.shape[:-1] + (full_width,), jnp.float32)
        return lax.dynamic_update_slice_in_dim(
            zeros_full, part_values, offset_col, part_values.ndim - 1
        )

    def narrow_piece(whole_sum, part_width):
        return lax.dynamic_slice_in_dim(
            whole_sum, tensor_place * part_width, part_width, whole_sum.ndim - 1
        )

    tokens = block_input.astype(jnp.float32)
    first_inverse = lax.rsqrt(jnp.mean(tokens * tokens, axis=-1, keepdims=True) + epsilon)
    first_vector = first_gain.astype(jnp.float32)
    normed_share = (tokens * first_inverse * first_vector).astype(jnp.bfloat16)
    normed = lax.all_gather(normed_share, "tensor", axis=0, tiled=True)
    gating_pre = dense(normed, gating_weight)
    inner_pre = dense(normed, inner_weight)
    state_pre = dense(normed, state_weight)
    step_pre = dense(normed, step_weight)
    state_act, state_back = jax.vjp(
        state_piece, as_sequences(state_pre), state_conv.astype(jnp.float32)
    )
    gated, mixer_back = jax.vjp(
        mixer_piece,
        as_sequences(inner_pre),
        state_act,
        as_sequences(step_pre),
        as_sequences(gating_pre),
        inner_conv.astype(jnp.float32),
        step_bias,
        decay_log,
        skip_scale,
    )
    gated_squares = lax.psum(jnp.sum(gated * gated, axis=-1), "tensor")
    mixer_inverse = lax.rsqrt(gated_squares / mixer_width + epsilon)[..., None]
    mixer_vector = mixer_gain.astype(jnp.float32)
    mixer_normed = (
        (gated * mixer_inverse * mixer_vector).astype(jnp.bfloat16).reshape(token_count, channels)
    )
    mixer_part = dense(mixer_normed, mixer_proj)
    cosine, sine_table = rope_tables(seq_len, HD)
    query_pre = dense(normed, query_weight).reshape(seq_count, seq_len, query_heads, HD)
    key_pre = dense(normed, key_weight).reshape(seq_count, seq_len, kv_heads, HD)
    value_pre = dense(normed, value_weight)
    queries = (
        rotate(query_pre, cosine, sine_table)
        .astype(jnp.bfloat16)
        .reshape(seq_count, seq_len, kv_heads, group_width, HD)
    )
    key_rows = rotate(key_pre, cosine, sine_table).astype(jnp.bfloat16)
    value_rows = value_pre.astype(jnp.bfloat16).reshape(seq_count, seq_len, kv_heads, HD)
    positions = jnp.arange(seq_len)

    def block_scores(block_start):
        query_block = queries[:, block_start : block_start + ATT_BLOCK]
        seg_block = segment_ids[:, block_start : block_start + ATT_BLOCK]
        row_index = block_start + jnp.arange(ATT_BLOCK)
        allowed = (positions[None, :] <= row_index[:, None])[None] & (
            seg_block[:, :, None] == segment_ids[:, None, :]
        )
        scores = (
            jnp.einsum(
                "sqkgd,slkd->skgql", query_block, key_rows, preferred_element_type=jnp.float32
            )
            * scale_factor
        )
        return (query_block, jnp.where(allowed[:, None, None], scores, -1e30))

    block_starts = list(range(0, seq_len, ATT_BLOCK))
    attended_blocks = []
    log_totals = []
    for block_start in block_starts:
        query_block, scores = block_scores(block_start)
        row_max = jnp.max(scores, axis=-1, keepdims=True)
        exponents = jnp.exp(scores - row_max)
        row_total = jnp.sum(exponents, axis=-1, keepdims=True)
        attn_probs = (exponents / row_total).astype(jnp.bfloat16)
        log_totals.append(row_max + jnp.log(row_total))
        attended_blocks.append(
            jnp.einsum(
                "skgql,slkd->sqkgd", attn_probs, value_rows, preferred_element_type=jnp.float32
            )
        )
    attended = (
        jnp.concatenate(attended_blocks, axis=1)
        .astype(jnp.bfloat16)
        .reshape(token_count, query_heads * HD)
    )
    attn_part = dense(attended, attention_out)
    branch_share = lax.psum_scatter(
        mixer_part + attn_part, "tensor", scatter_dimension=0, tiled=True
    )
    residual = tokens + branch_share
    second_inverse = lax.rsqrt(jnp.mean(residual * residual, axis=-1, keepdims=True) + epsilon)
    second_vector = second_gain.astype(jnp.float32)
    normed_two_share = (residual * second_inverse * second_vector).astype(jnp.bfloat16)
    normed_two, full_grad = (
        lax.all_gather(normed_two_share, "tensor", axis=0, tiled=True),
        lax.all_gather(out_grad, "tensor", axis=0, tiled=True),
    )
    gate_pre = dense(normed_two, gate_weight)
    up_pre = dense(normed_two, up_weight)
    gate_sigmoid = jax.nn.sigmoid(gate_pre)
    gate_act = gate_pre * gate_sigmoid
    hidden = (gate_act * up_pre).astype(jnp.bfloat16)
    ffn_share = lax.psum_scatter(
        dense(hidden, down_projection_weight).astype(jnp.bfloat16),
        "tensor",
        scatter_dimension=0,
        tiled=True,
    ).astype(jnp.float32)
    block_output = (residual + ffn_share).astype(jnp.bfloat16)
    grad_down = row_dot(hidden, full_grad)
    grad_hidden = back_dot(full_grad, down_projection_weight)
    grad_gate_pre = (
        grad_hidden * up_pre * gate_sigmoid * (1.0 + gate_pre * (1.0 - gate_sigmoid))
    ).astype(jnp.bfloat16)
    grad_up_pre = (grad_hidden * gate_act).astype(jnp.bfloat16)
    grad_gate = row_dot(normed_two, grad_gate_pre)
    grad_up = row_dot(normed_two, grad_up_pre)
    second_back = back_dot(grad_gate_pre, gate_weight) + back_dot(grad_up_pre, up_weight)
    grad_normed_two = lax.psum_scatter(second_back, "tensor", scatter_dimension=0, tiled=True)
    grad_second_gain = jnp.sum(grad_normed_two * residual * second_inverse, axis=0)
    grad_residual = out_grad.astype(jnp.float32) + norm_back(
        grad_normed_two, residual, second_inverse, second_vector
    )
    branch_grad = lax.all_gather(grad_residual.astype(jnp.bfloat16), "tensor", axis=0, tiled=True)
    grad_mixer_proj = row_dot(mixer_normed, branch_grad)
    grad_mixer_normed = back_dot(branch_grad, mixer_proj).reshape(seq_count, seq_len, channels)
    grad_mixer_gain = jnp.sum(grad_mixer_normed * gated * mixer_inverse, axis=(0, 1))
    mixer_scaled = grad_mixer_normed * mixer_vector
    cross_sum = lax.psum(jnp.sum(gated * mixer_scaled, axis=-1), "tensor")
    grad_gated = (
        mixer_inverse * mixer_scaled
        - gated * mixer_inverse**3 * (cross_sum / mixer_width)[..., None]
    )
    (
        grad_inner_pre,
        grad_state_act,
        grad_step_pre,
        grad_gating_pre,
        grad_inner_conv,
        grad_step_bias,
        grad_decay_log,
        grad_skip_scale,
    ) = mixer_back(grad_gated)
    state_total = lax.psum(grad_state_act.astype(jnp.bfloat16), "tensor").astype(jnp.float32)
    grad_state_pre, grad_state_conv = state_back(state_total)
    gating_rows = to_rows(grad_gating_pre)
    inner_rows = to_rows(grad_inner_pre)
    state_rows = to_rows(grad_state_pre)
    step_rows = to_rows(grad_step_pre)
    grad_gating = row_dot(normed, gating_rows)
    grad_inner = row_dot(normed, inner_rows)
    grad_state = row_dot(normed, state_rows)
    grad_step = row_dot(normed, step_rows)
    grad_attended = (
        back_dot(branch_grad, attention_out)
        .astype(jnp.bfloat16)
        .reshape(seq_count, seq_len, kv_heads, group_width, HD)
    )
    attention_output_gradient = row_dot(attended, branch_grad)
    key_gradients = jnp.zeros((seq_count, seq_len, kv_heads, HD), jnp.float32)
    grad_values = jnp.zeros((seq_count, seq_len, kv_heads, HD), jnp.float32)
    query_grads = []
    for block_index in range(len(block_starts)):
        block_start = block_starts[block_index]
        query_block, scores = block_scores(block_start)
        attn_probs = jnp.exp(scores - log_totals[block_index])
        grad_block = grad_attended[:, block_start : block_start + ATT_BLOCK]
        grad_probs = jnp.einsum(
            "sqkgd,slkd->skgql", grad_block, value_rows, preferred_element_type=jnp.float32
        )
        row_delta = jnp.sum(attn_probs * grad_probs, axis=-1, keepdims=True)
        grad_scores = (attn_probs * (grad_probs - row_delta)).astype(jnp.bfloat16)
        query_grads.append(
            jnp.einsum(
                "skgql,slkd->sqkgd", grad_scores, key_rows, preferred_element_type=jnp.float32
            )
            * scale_factor
        )
        key_gradients = (
            key_gradients
            + jnp.einsum(
                "skgql,sqkgd->slkd", grad_scores, query_block, preferred_element_type=jnp.float32
            )
            * scale_factor
        )
        grad_values = grad_values + jnp.einsum(
            "skgql,sqkgd->slkd",
            attn_probs.astype(jnp.bfloat16),
            grad_block,
            preferred_element_type=jnp.float32,
        )
    grad_query_pre = unrotate(
        jnp.concatenate(query_grads, axis=1).reshape(seq_count, seq_len, query_heads, HD),
        cosine,
        sine_table,
    )
    grad_key_pre = unrotate(key_gradients, cosine, sine_table)
    query_rows = to_rows(grad_query_pre)
    key_grad_rows = to_rows(grad_key_pre)
    value_grad_rows = to_rows(grad_values)
    grad_query = row_dot(normed, query_rows)
    grad_key = row_dot(normed, key_grad_rows)
    grad_value = row_dot(normed, value_grad_rows)
    first_back = (
        back_dot(gating_rows, gating_weight)
        + back_dot(inner_rows, inner_weight)
        + back_dot(step_rows, step_weight)
        + 0.5 * back_dot(state_rows, state_weight)
    )
    first_back = (
        first_back
        + back_dot(query_rows, query_weight)
        + back_dot(key_grad_rows, key_weight)
        + back_dot(value_grad_rows, value_weight)
    )
    grad_normed = lax.psum_scatter(
        first_back.astype(jnp.bfloat16), "tensor", scatter_dimension=0, tiled=True
    ).astype(jnp.float32)
    grad_first_gain = jnp.sum(grad_normed * tokens * first_inverse, axis=0)
    input_grad = grad_residual + norm_back(grad_normed, tokens, first_inverse, first_vector)
    small_sums = lax.psum(
        (
            widen_piece(grad_step_bias, H_SSM),
            widen_piece(grad_decay_log, H_SSM),
            widen_piece(grad_skip_scale, H_SSM),
            widen_piece(grad_inner_conv, mixer_width),
            0.5 * grad_state_conv,
            widen_piece(grad_mixer_gain, mixer_width),
            grad_first_gain,
            grad_second_gain,
        ),
        ("dp", "tensor"),
    )
    shares = (
        lax.psum_scatter(flat_rows(grad_gating), "dp", scatter_dimension=0, tiled=True),
        lax.psum_scatter(flat_rows(grad_inner), "dp", scatter_dimension=0, tiled=True),
        lax.psum_scatter(flat_rows(grad_state), "dp", scatter_dimension=0, tiled=True),
        lax.psum_scatter(flat_rows(grad_step), "dp", scatter_dimension=0, tiled=True),
        lax.psum_scatter(flat_rows(grad_mixer_proj), "dp", scatter_dimension=0, tiled=True),
        lax.psum_scatter(flat_rows(grad_query), "dp", scatter_dimension=0, tiled=True),
        lax.psum_scatter(flat_rows(grad_key), "dp", scatter_dimension=0, tiled=True),
        lax.psum_scatter(flat_rows(grad_value), "dp", scatter_dimension=0, tiled=True),
        lax.psum_scatter(
            flat_rows(attention_output_gradient), "dp", scatter_dimension=0, tiled=True
        ),
        lax.psum_scatter(flat_rows(grad_gate), "dp", scatter_dimension=0, tiled=True),
        lax.psum_scatter(flat_rows(grad_up), "dp", scatter_dimension=0, tiled=True),
        lax.psum_scatter(flat_rows(grad_down), "dp", scatter_dimension=0, tiled=True),
    )
    summed = (
        lax.all_gather(shares[0].astype(jnp.bfloat16), "dp", axis=0, tiled=True).astype(
            jnp.float32
        ),
        lax.all_gather(shares[1].astype(jnp.bfloat16), "dp", axis=0, tiled=True).astype(
            jnp.float32
        ),
        lax.all_gather(shares[2].astype(jnp.bfloat16), "dp", axis=0, tiled=True).astype(
            jnp.float32
        ),
        lax.all_gather(shares[3].astype(jnp.bfloat16), "dp", axis=0, tiled=True).astype(
            jnp.float32
        ),
        lax.all_gather(shares[4].astype(jnp.bfloat16), "dp", axis=0, tiled=True).astype(
            jnp.float32
        ),
        lax.all_gather(shares[5].astype(jnp.bfloat16), "dp", axis=0, tiled=True).astype(
            jnp.float32
        ),
        lax.all_gather(shares[6].astype(jnp.bfloat16), "dp", axis=0, tiled=True).astype(
            jnp.float32
        ),
        lax.all_gather(shares[7].astype(jnp.bfloat16), "dp", axis=0, tiled=True).astype(
            jnp.float32
        ),
        lax.all_gather(shares[8].astype(jnp.bfloat16), "dp", axis=0, tiled=True).astype(
            jnp.float32
        ),
        lax.all_gather(shares[9].astype(jnp.bfloat16), "dp", axis=0, tiled=True).astype(
            jnp.float32
        ),
        lax.all_gather(shares[10].astype(jnp.bfloat16), "dp", axis=0, tiled=True).astype(
            jnp.float32
        ),
        lax.all_gather(shares[11].astype(jnp.bfloat16), "dp", axis=0, tiled=True).astype(
            jnp.float32
        ),
    )
    return (
        block_output,
        input_grad,
        summed[0].reshape(gating_weight.shape),
        summed[1].reshape(inner_weight.shape),
        summed[2].reshape(state_weight.shape),
        summed[3].reshape(step_weight.shape),
        narrow_piece(small_sums[0], head_local),
        narrow_piece(small_sums[1], head_local),
        narrow_piece(small_sums[2], head_local),
        narrow_piece(small_sums[3], channels),
        small_sums[4],
        narrow_piece(small_sums[5], channels),
        summed[4].reshape(mixer_proj.shape),
        summed[5].reshape(query_weight.shape),
        summed[6].reshape(key_weight.shape),
        summed[7].reshape(value_weight.shape),
        summed[8].reshape(attention_out.shape),
        small_sums[6],
        small_sums[7],
        summed[9].reshape(gate_weight.shape),
        summed[10].reshape(up_weight.shape),
        summed[11].reshape(down_projection_weight.shape),
    )


def solution(mesh):
    placed = (
        P(("dp", "tensor"), None),
        P("dp", None),
        P(("dp", "tensor"), None),
        P(None, "tensor"),
        P(None, "tensor"),
        P(),
        P(None, "tensor"),
        P("tensor"),
        P("tensor"),
        P("tensor"),
        P(None, "tensor"),
        P(),
        P("tensor"),
        P("tensor", None),
        P(None, "tensor"),
        P(None, "tensor"),
        P(None, "tensor"),
        P("tensor", None),
        P(),
        P(),
        P(None, "tensor"),
        P(None, "tensor"),
        P("tensor", None),
    )
    return jax.shard_map(
        on_device,
        mesh=mesh,
        in_specs=placed,
        out_specs=(
            P(("dp", "tensor"), None),
            P(("dp", "tensor"), None),
            P(None, "tensor"),
            P(None, "tensor"),
            P(),
            P(None, "tensor"),
            P("tensor"),
            P("tensor"),
            P("tensor"),
            P(None, "tensor"),
            P(),
            P("tensor"),
            P("tensor", None),
            P(None, "tensor"),
            P(None, "tensor"),
            P(None, "tensor"),
            P("tensor", None),
            P(),
            P(),
            P(None, "tensor"),
            P(None, "tensor"),
            P("tensor", None),
        ),
        check_vma=False,
    )
```

profile of v0, /device:TPU:0, one launch (start us, length us, event | category | flops | bytes accessed | tf_op | source)
XLA Modules:
  0.0 1886.2 jit_solution(8115387187553326907)
XLA Ops:
  19.1 30.2 %all-gather.23.cloned.1.call-done = bf16[1024,1024]{1,0:T(8,128)(2,1)} async-done(((bf16[512,1024]{1,0:T(8,128)(2,1)}), bf16[1024,1024]{1,0:T(8,128)(2,1)}) %all-gather.23.cloned.1.call-update) | async-done | bytes 2097168 | tf_op jit(solution)/shard_map/all_gather | solution.py:196
  83.3 166.5 %while.41 = (s32[]{:T(128)}, f32[1,12,64,128]{3,2,1,0:T(8,128)S(1)}, f32[8,1,128,12,64]{2,0,4,3,1:T(8,128)}, f32[8,1,12,64,128]{4,3,2,1,0:T(8,128)}, f32[8,1,128...) while((s32[]{:T(128)}, ...), condition=%wide.region_3.4_spmd.clone, body=%wide.region_1.3_spmd.clone.sunk | while | flops 479923200 | bytes 5272572 | solution.py:105
  293.5 53.8 %reduce-scatter.5.cloned.1.call-done = f32[512,1024]{1,0:T(8,128)} async-done(((f32[1024,1024]{1,0:T(8,128)}), f32[512,1024]{1,0:T(8,128)}) %reduce-scatter.5.cloned.1.call-update) | async-done | bytes 2097168 | tf_op jit(solution)/shard_map/reduce_scatter | solution.py:271
  352.4 32.6 %all-gather.25.cloned.1.call-done = bf16[1024,1024]{1,0:T(8,128)(2,1)} async-done(((bf16[512,1024]{1,0:T(8,128)(2,1)}), bf16[1024,1024]{1,0:T(8,128)(2,1)}) %all-gather.25.cloned.1.call-update) | async-done | bytes 2097168 | tf_op jit(solution)/shard_map/all_gather | solution.py:279
  396.1 23.5 %all-gather.27.cloned.1.call-done = bf16[1024,1024]{1,0:T(8,128)(2,1)} async-done(((bf16[512,1024]{1,0:T(8,128)(2,1)}), bf16[1024,1024]{1,0:T(8,128)(2,1)}) %all-gather.27.cloned.1.call-update) | async-done | bytes 2097168 | tf_op jit(solution)/shard_map/all_gather | solution.py:280
  442.0 48.1 %reduce-scatter.9.cloned.1.call-done = f32[512,1024]{1,0:T(8,128)} async-done(((f32[1024,1024]{1,0:T(8,128)}), f32[512,1024]{1,0:T(8,128)}) %reduce-scatter.9.cloned.1.call-update) | async-done | bytes 2097168 | tf_op jit(solution)/shard_map/reduce_scatter | solution.py:303
  492.8 31.8 %reduce-scatter.7.cloned.1.call-done = bf16[512,1024]{1,0:T(8,128)(2,1)} async-done(((bf16[1024,1024]{1,0:T(8,128)(2,1)}), bf16[512,1024]{1,0:T(8,128)(2,1)}) %reduce-scatter.7.cloned.1.call-update) | async-done | bytes 1048592 | tf_op jit(solution)/shard_map/reduce_scatter | solution.py:287
  637.8 227.3 %while.42 = (s32[]{:T(128)}, f32[12]{0:T(128)S(1)}, f32[1,12,64,128]{3,2,1,0:T(8,128)S(1)}, f32[8,1,128,12,64]{2,0,4,3,1:T(8,128)}, f32[8,1,128,128]{3,2,0,1:T(8...) while((s32[]{:T(128)}, f32[12]{0:T(128)S(1)}, ...), condition=%wide.region_28.29_spmd.clone, body=%wide.region_17.28_spmd.clone.sunk | while | flops 1137632768 | bytes 13644976 | solution.py:105
  950.2 535.7 %all-reduce.40 = (bf16[16,49152]{1,0:T(8,128)(2,1)}, bf16[16,49152]{1,0:T(8,128)(2,1)}, bf16[16,16384]{1,0:T(8,128)(2,1)}, bf16[16,768]{1,0:T(8,128)(2,1)}, bf16...) all-reduce(f32[16,49152]{1,0:T(8,128)} %reshape.1568, ...), channel_id=6, replica_groups=mesh['dp'=16,'tensor'=2] {'dp'}, use_global_device_ids=true, to_apply=%region_34.35.clone | all-reduce | flops 6434816 | bytes 38608896
  1501.4 28.6 %all-gather.3 = bf16[16,1,768]{2,1,0:T(2,128)(2,1)} all-gather(bf16[1,1,768]{2,1,0:T(2,128)(2,1)S(1)} %fusion.218), channel_id=1, replica_groups=mesh['dp'=16,'tensor'=2] {'dp'}, dimensions={0}, use_global_device_ids=true | all-gather | bytes 26112 | tf_op jit(solution)/shard_map/all_gather | solution.py:444
  1531.6 18.4 all-gather.7
  1554.5 20.0 %all-gather.6 = bf16[16,1,4096]{2,1,0:T(2,128)(2,1)S(1)} all-gather(bf16[1,1,4096]{2,1,0:T(2,128)(2,1)S(1)} %fusion.212), channel_id=1, replica_groups=mesh['dp'=16,'tensor'=2] {'dp'}, dimensions={0}, use_global_device_ids=true | all-gather | bytes 139264 | tf_op jit(solution)/shard_map/all_gather | solution.py:453
  1577.6 23.4 %all-gather.8 = bf16[16,1,16384]{2,1,0:T(2,128)(2,1)S(1)} all-gather(bf16[1,1,16384]{2,1,0:T(2,128)(2,1)S(1)} %fusion.207), channel_id=1, replica_groups=mesh['dp'=16,'tensor'=2] {'dp'}, dimensions={0}, use_global_device_ids=true | all-gather | bytes 557056 | tf_op jit(solution)/shard_map/all_gather | solution.py:459
  1604.0 22.9 %all-gather.5 = bf16[16,1,16384]{2,1,0:T(2,128)(2,1)S(1)} all-gather(bf16[1,1,16384]{2,1,0:T(2,128)(2,1)S(1)} %fusion.208), channel_id=1, replica_groups=mesh['dp'=16,'tensor'=2] {'dp'}, dimensions={0}, use_global_device_ids=true | all-gather | bytes 557056 | tf_op jit(solution)/shard_map/all_gather | solution.py:450
  1647.6 25.6 %all-gather.2 = bf16[16,1,16384]{2,1,0:T(2,128)(2,1)S(1)} all-gather(bf16[1,1,16384]{2,1,0:T(2,128)(2,1)S(1)} %fusion.209), channel_id=1, replica_groups=mesh['dp'=16,'tensor'=2] {'dp'}, dimensions={0}, use_global_device_ids=true | all-gather | bytes 557056 | tf_op jit(solution)/shard_map/all_gather | solution.py:441
  1677.3 12.7 convert_reduce_fusion.5
  1693.4 12.5 convert_reduce_fusion.4
  1709.4 12.5 convert_reduce_fusion.3
  1725.2 15.0 convert_reduce_fusion.2
  1745.4 15.0 convert_reduce_fusion
  1764.4 32.1 %all-gather.39.cloned.1.call-done = bf16[16,1,65536]{2,1,0:T(2,128)(2,1)} async-done(((bf16[1,1,65536]{2,1,0:T(2,128)(2,1)}), bf16[16,1,65536]{2,1,0:T(2,128)(2,1)}) %all-gather.39.cloned.1.call-update) | async-done | bytes 2097168 | tf_op jit(solution)/shard_map/all_gather | solution.py:465
  1796.5 15.0 convert_reduce_fusion.1
  1815.6 13.9 reduce-scatter.11.cloned.1.call-done
  1831.7 40.6 %all-reduce.34 = (f32[24]{0:T(128)S(1)}, f32[24]{0:T(128)S(1)}, f32[24]{0:T(128)S(1)}, f32[4,1536]{1,0:T(4,128)S(1)}, f32[4,256]{1,0:T(4,128)}, /*index=5*/f32[1536]{0:T(1024)S(1)}, f32[1024]{0:T(1024)}, f32[1024]{0:T(1024)}) all-reduce(f32[24]{0:T(128)S(1)} %copy-done.133, ...), channel_id=1, replica_groups=mesh['dp'=16,'tensor'=2] {'dp','tensor'}, use_global_device_ids=true, to_apply=%region_39.40 | all-reduce | flops 10824 | bytes 86592 | tf_op jit(solution)/shard_map/psum | solution.py:405
  (986 shorter events, 804.5 us)
Async XLA Ops:
  7.2 412.5 %copy-start = (bf16[1024,1024]{1,0:T(8,128)(2,1)S(1)}, bf16[1024,1024]{1,0:T(8,128)(2,1)}, u32[]{:S(2)}) copy-start(bf16[1024,1024]{1,0:T(8,128)(2,1)} %param.49) | copy-start | bytes 6291460
  7.3 42.1 %all-gather.23.cloned.1.call-start = ((), (), s32[]{:S(2)}) async-start(), calls=%async_computation.4 | async-start | bytes 3145728 | tf_op jit(solution)/shard_map/all_gather | solution.py:196
  13.4 333.8 %reduce-scatter.5.cloned.1.call-start = ((), (), s32[]{:S(2)}) async-start(), calls=%async_computation.5 | async-start | bytes 6291456 | tf_op jit(solution)/shard_map/reduce_scatter | solution.py:271
  292.8 54.5 %copy-start.14 = (bf16[512,1024]{1,0:T(8,128)(2,1)S(1)}, bf16[512,1024]{1,0:T(8,128)(2,1)}, u32[]{:S(2)}) copy-start(bf16[512,1024]{1,0:T(8,128)(2,1)} %param.27) | copy-start | bytes 3145732
  292.8 92.3 %all-gather.25.cloned.1.call-start = ((), (), s32[]{:S(2)}) async-start(), calls=%async_computation.6 | async-start | bytes 3145728 | tf_op jit(solution)/shard_map/all_gather | solution.py:279
  293.5 58.3 %copy-start.69 = (f32[1024]{0:T(1024)}, f32[1024]{0:T(1024)S(1)}, u32[]{:S(2)}) copy-start(f32[1024]{0:T(1024)S(1)} %convert_element_type.207) | copy-start | bytes 12292
  351.8 67.9 %all-gather.27.cloned.1.call-start = ((), (), s32[]{:S(2)}) async-start(), calls=%async_computation.8 | async-start | bytes 3145728 | tf_op jit(solution)/shard_map/all_gather | solution.py:280
  352.4 137.7 %reduce-scatter.9.cloned.1.call-start = ((), (), s32[]{:S(2)}) async-start(), calls=%async_computation.9 | async-start | bytes 6291456 | tf_op jit(solution)/shard_map/reduce_scatter | solution.py:303
  435.6 89.0 %reduce-scatter.7.cloned.1.call-start = ((), (), s32[]{:S(2)}) async-start(), calls=%async_computation.7 | async-start | bytes 3145728 | tf_op jit(solution)/shard_map/reduce_scatter | solution.py:287
  435.7 54.4 %copy-start.70 = (f32[1024]{0:T(1024)S(1)}, f32[1024]{0:T(1024)}, u32[]{:S(2)}) copy-start(f32[1024]{0:T(1024)} %copy-done.69) | copy-start | bytes 12292
  441.0 121.9 %all-gather.29.cloned.1.call-start = ((), (), s32[]{:S(2)}) async-start(), calls=%async_computation.10 | async-start | bytes 3145728 | tf_op jit(solution)/shard_map/all_gather | solution.py:308
  529.6 413.3 %all-reduce.39.cloned.1.call-start = ((), (), s32[]{:S(2)}) async-start(), calls=%async_computation.11 | async-start | bytes 1048576 | tf_op jit(solution)/shard_map/psum | solution.py:328
  637.8 230.8 %copy-start.65 = (f32[1024,12]{0,1:T(8,128)S(1)}, f32[1024,12]{0,1:T(8,128)}, u32[]{:S(2)}) copy-start(f32[1024,12]{0,1:T(8,128)} %get-tuple-element.836) | copy-start | bytes 147460
  637.8 231.5 %copy-start.68 = (bf16[1024,12]{0,1:T(8,128)(2,1)S(1)}, bf16[1024,12]{0,1:T(8,128)(2,1)}, u32[]{:S(2)}) copy-start(bf16[1024,12]{0,1:T(8,128)(2,1)} %param.33) | copy-start | bytes 73732
  867.2 810.1 %all-gather.31.cloned.1.call-start = ((), (), s32[]{:S(2)}) async-start(), calls=%async_computation.13 | async-start | bytes 3342336 | tf_op jit(solution)/shard_map/all_gather | solution.py:435
  1488.7 204.7 %all-gather.33.cloned.1.call-start = ((), (), s32[]{:S(2)}) async-start(), calls=%async_computation.14 | async-start | bytes 3342336 | tf_op jit(solution)/shard_map/all_gather | solution.py:438
  1494.3 215.1 %all-gather.35.cloned.1.call-start = ((), (), s32[]{:S(2)}) async-start(), calls=%async_computation.15 | async-start | bytes 3342336 | tf_op jit(solution)/shard_map/all_gather | solution.py:447
  1497.1 228.1 %all-gather.37.cloned.1.call-start = ((), (), s32[]{:S(2)}) async-start(), calls=%async_computation.16 | async-start | bytes 4456448 | tf_op jit(solution)/shard_map/all_gather | solution.py:462
  1551.5 193.9 %all-gather.41.cloned.1.call-start = ((), (), s32[]{:S(2)}) async-start(), calls=%async_computation.18 | async-start | bytes 4456448 | tf_op jit(solution)/shard_map/all_gather | solution.py:468
  1554.4 72.5 %copy-start.37 = (bf16[1024,256]{1,0:T(8,128)(2,1)S(1)}, bf16[1024,256]{1,0:T(8,128)(2,1)}, u32[]{:S(2)}) copy-start(bf16[1024,256]{1,0:T(8,128)(2,1)} %copy-done.36) | copy-start | bytes 1572868
  1554.5 242.0 %all-gather.39.cloned.1.call-start = ((), (), s32[]{:S(2)}) async-start(), calls=%async_computation.17 | async-start | bytes 4456448 | tf_op jit(solution)/shard_map/all_gather | solution.py:465
  1576.7 52.0 %copy-start.57 = (bf16[1024,64]{0,1:T(8,128)(2,1)S(1)}, bf16[1024,64]{0,1:T(8,128)(2,1)}, u32[]{:S(2)}) copy-start(bf16[1024,64]{0,1:T(8,128)(2,1)} %param.43) | copy-start | bytes 393220
  1577.6 252.0 %reduce-scatter.11.cloned.1.call-start = ((), (), s32[]{:S(2)}) async-start(), calls=%async_computation.12 | async-start | bytes 3145728 | tf_op jit(solution)/shard_map/reduce_scatter | solution.py:400
  1811.5 63.8 %copy-start.118 = (f32[512]{0:T(512)S(1)}, f32[512]{0:T(512)}, u32[]{:S(2)}) copy-start(f32[512]{0:T(512)} %get-tuple-element.823) | copy-start | bytes 6148
  (142 other events, 1182.8 us)
Sparse Core Ops, SparseCore 0:
  13.5 35.8 all-gather.22
  292.9 54.2 reduce-scatter.4
  351.9 33.1 all-gather.24
  386.5 33.1 all-gather.26
  435.7 54.3 reduce-scatter.8
  492.7 31.8 reduce-scatter.6
  529.7 33.1 all-gather.28
  867.3 28.5 all-reduce.38
  1488.8 51.7 all-gather.30
  1542.7 45.9 all-gather.32
  1591.0 48.1 all-gather.34
  1641.3 52.7 all-gather.36
  1696.3 49.0 all-gather.40
  1747.4 49.0 all-gather.38
  1799.2 30.3 reduce-scatter.10
where the time goes:
time: 1900 us; the launch traced here: 1890 us
  blocking collectives  726 us (38%)
  local copies, waits for them, and re-layouts  389 us (20%)
  waiting for transfers between devices  269 us (14%)
  matrix products  269 us (14%)
  other arithmetic  215 us (11%)
    unnamed x1, blocking collectives  536 us
    dynamic_update_slice x32, local copies, waits for them, and re-layouts, ssd_spans(): lax.scan(jax.checkpoint(one_block), initial, (to_blocks(inner), to_blocks...  181 us
    unnamed x323, local copies, waits for them, and re-layouts  58 us
    reduce_scatter x1, waiting for transfers between devices, on_device(): lax.psum_scatter(mixer_part + attn_part, 'tensor', scatter_dimension=0, t...  53.8 us
    dot_general x12, matrix products, back_dot(): lax.dot_general(left_side, right_side, (((1,), (1,)), ((), ())), preferre...  50.8 us
    reduce_scatter x1, waiting for transfers between devices, on_device(): lax.psum_scatter(second_back, 'tensor', scatter_dimension=0, tiled=True)  48.1 us
    dot_general x24, matrix products, one_block(): jnp.einsum('stuh,suhp->sthp', mixing, inner_block, precision=top_precision)  44.7 us
    psum x1, blocking collectives, on_device(): lax.psum((widen_piece(grad_step_bias, H_SSM), widen_piece(grad_decay_log,...  40.6 us
  transfers between devices with their start and end apart: 15, of which 10 were waited for; matrix products, arithmetic and copies ran while one was open for 15% of the time, Pallas kernels for 0%

commit v1 on v0

--- a/solution.py
+++ b/solution.py
@@ -71,6 +71,87 @@
     )
 
 
+def swap_tensor(value):
+    return lax.ppermute(value, "tensor", [(0, 1), (1, 0)])
+
+
+def both(value):
+    return value + swap_tensor(value)
+
+
+def in_order(place, own, other):
+    first = jnp.where(place == 0, own, other)
+    second = jnp.where(place == 0, other, own)
+    return jnp.concatenate([first, second], axis=0)
+
+
+def gather_rows(share):
+    return in_order(lax.axis_index("tensor"), share, swap_tensor(share))
+
+
+def half_of(value, place):
+    half = value.shape[0] // 2
+    return lax.dynamic_slice_in_dim(value, place * half, half, 0)
+
+
+def scatter_rows(partial):
+    place = lax.axis_index("tensor")
+    got = swap_tensor(half_of(partial, 1 - place).astype(jnp.bfloat16))
+    return half_of(partial, place).astype(jnp.float32) + got.astype(jnp.float32)
+
+
+def flip(value, bit):
+    size = lax.axis_size("dp")
+    return lax.ppermute(value, "dp", [(i, i ^ bit) for i in range(size)])
+
+
+def bits_in_order(far_first):
+    count = lax.axis_size("dp").bit_length() - 1
+    bits = [1 << i for i in range(count)]
+    return bits[:1] + bits[2:] + bits[1:2] if far_first else bits
+
+
+def sum_over_dp(arrays, far_first, over_tensor=False):
+    index = lax.axis_index("dp")
+    bits = bits_in_order(far_first)
+    places = [(index // bit) % 2 for bit in bits]
+
+    def joined(parts):
+        return parts[0] if len(parts) == 1 else jnp.concatenate(parts, axis=0)
+
+    current = None
+    for bit, place in zip(bits, places):
+        if current is None:
+            keep = joined([half_of(a, place).astype(jnp.bfloat16) for a in arrays])
+            send = joined([half_of(a, 1 - place).astype(jnp.bfloat16) for a in arrays])
+        else:
+            keep, send = half_of(current, place), half_of(current, 1 - place)
+        got = flip(send, bit)
+        current = (keep.astype(jnp.float32) + got.astype(jnp.float32)).astype(jnp.bfloat16)
+    if over_tensor:
+        current = (current.astype(jnp.float32) + swap_tensor(current).astype(jnp.float32)).astype(jnp.bfloat16)
+    for bit, place in list(zip(bits, places))[:0:-1]:
+        current = in_order(place, current, flip(current, bit))
+    other = flip(current, bits[0])
+    results, start = [], 0
+    for a in arrays:
+        rows = a.shape[0] // 2
+        results.append(
+            in_order(places[0], current[start : start + rows], other[start : start + rows]).astype(jnp.float32)
+        )
+        start += rows
+    return results
+
+
+def sum_small(value):
+    size = lax.axis_size("dp")
+    bit = 1
+    while bit < size:
+        value = value + flip(value, bit)
+        bit *= 2
+    return value
+
+
 def ssd_spans(inner, in_vec, out_vec, step_sizes, decay_rate):
     seq_count, length, head_count, head_size = inner.shape
     state_size = in_vec.shape[-1]
@@ -85,7 +166,9 @@
 
     def one_block(carry_state, pieces):
         inner_block, in_block, out_block, step_block = pieces
-        cumulative = jnp.cumsum(step_block * decay_rate, axis=1)
+        cumulative = jnp.einsum(
+            "ts,bsh->bth", lower_mask.astype(jnp.float32), step_block * decay_rate, precision=top_precision
+        )
         log_gaps = cumulative[:, :, None, :] - cumulative[:, None, :, :]
         within = jnp.exp(jnp.where(lower_mask[None, :, :, None], log_gaps, -1e30))
         scores = jnp.einsum("stn,sun->stu", out_block, in_block, precision=top_precision)
@@ -165,35 +248,18 @@
     group_width = query_heads // kv_heads
     scale_factor = HD ** (-0.5)
     mixer_width = H_SSM * P_SIZE
-    dp_count = lax.axis_size("dp")
-    tensor_place = lax.axis_index("tensor")
 
     def as_sequences(value_tensor):
         return value_tensor.reshape(seq_count, seq_len, value_tensor.shape[-1])
 
     def to_rows(value_tensor):
         return value_tensor.reshape(token_count, -1).astype(jnp.bfloat16)
-
-    def flat_rows(value_tensor):
-        return value_tensor.reshape(dp_count, -1)
-
-    def widen_piece(part_values, full_width):
-        offset_col = tensor_place * part_values.shape[-1]
-        zeros_full = jnp.zeros(part_values.shape[:-1] + (full_width,), jnp.float32)
-        return lax.dynamic_update_slice_in_dim(
-            zeros_full, part_values, offset_col, part_values.ndim - 1
-        )
-
-    def narrow_piece(whole_sum, part_width):
-        return lax.dynamic_slice_in_dim(
-            whole_sum, tensor_place * part_width, part_width, whole_sum.ndim - 1
-        )
 
     tokens = block_input.astype(jnp.float32)
     first_inverse = lax.rsqrt(jnp.mean(tokens * tokens, axis=-1, keepdims=True) + epsilon)
     first_vector = first_gain.astype(jnp.float32)
     normed_share = (tokens * first_inverse * first_vector).astype(jnp.bfloat16)
-    normed = lax.all_gather(normed_share, "tensor", axis=0, tiled=True)
+    normed = gather_rows(normed_share)
     gating_pre = dense(normed, gating_weight)
     inner_pre = dense(normed, inner_weight)
     state_pre = dense(normed, state_weight)
@@ -212,7 +278,7 @@
         decay_log,
         skip_scale,
     )
-    gated_squares = lax.psum(jnp.sum(gated * gated, axis=-1), "tensor")
+    gated_squares = both(jnp.sum(gated * gated, axis=-1))
     mixer_inverse = lax.rsqrt(gated_squares / mixer_width + epsilon)[..., None]
     mixer_vector = mixer_gain.astype(jnp.float32)
     mixer_normed = (
@@ -268,28 +334,19 @@
         .reshape(token_count, query_heads * HD)
     )
     attn_part = dense(attended, attention_out)
-    branch_share = lax.psum_scatter(
-        mixer_part + attn_part, "tensor", scatter_dimension=0, tiled=True
-    )
+    branch_share = scatter_rows(mixer_part + attn_part)
     residual = tokens + branch_share
     second_inverse = lax.rsqrt(jnp.mean(residual * residual, axis=-1, keepdims=True) + epsilon)
     second_vector = second_gain.astype(jnp.float32)
     normed_two_share = (residual * second_inverse * second_vector).astype(jnp.bfloat16)
-    normed_two, full_grad = (
-        lax.all_gather(normed_two_share, "tensor", axis=0, tiled=True),
-        lax.all_gather(out_grad, "tensor", axis=0, tiled=True),
-    )
+    normed_two = gather_rows(normed_two_share)
+    full_grad = gather_rows(out_grad)
     gate_pre = dense(normed_two, gate_weight)
     up_pre = dense(normed_two, up_weight)
     gate_sigmoid = jax.nn.sigmoid(gate_pre)
     gate_act = gate_pre * gate_sigmoid
     hidden = (gate_act * up_pre).astype(jnp.bfloat16)
-    ffn_share = lax.psum_scatter(
-        dense(hidden, down_projection_weight).astype(jnp.bfloat16),
-        "tensor",
-        scatter_dimension=0,
-        tiled=True,
-    ).astype(jnp.float32)
+    ffn_share = scatter_rows(dense(hidden, down_projection_weight))
     block_output = (residual + ffn_share).astype(jnp.bfloat16)
     grad_down = row_dot(hidden, full_grad)
     grad_hidden = back_dot(full_grad, down_projection_weight)
@@ -300,17 +357,17 @@
     grad_gate = row_dot(normed_two, grad_gate_pre)
     grad_up = row_dot(normed_two, grad_up_pre)
     second_back = back_dot(grad_gate_pre, gate_weight) + back_dot(grad_up_pre, up_weight)
-    grad_normed_two = lax.psum_scatter(second_back, "tensor", scatter_dimension=0, tiled=True)
+    grad_normed_two = scatter_rows(second_back)
     grad_second_gain = jnp.sum(grad_normed_two * residual * second_inverse, axis=0)
     grad_residual = out_grad.astype(jnp.float32) + norm_back(
         grad_normed_two, residual, second_inverse, second_vector
     )
-    branch_grad = lax.all_gather(grad_residual.astype(jnp.bfloat16), "tensor", axis=0, tiled=True)
+    branch_grad = gather_rows(grad_residual.astype(jnp.bfloat16))
     grad_mixer_proj = row_dot(mixer_normed, branch_grad)
     grad_mixer_normed = back_dot(branch_grad, mixer_proj).reshape(seq_count, seq_len, channels)
     grad_mixer_gain = jnp.sum(grad_mixer_normed * gated * mixer_inverse, axis=(0, 1))
     mixer_scaled = grad_mixer_normed * mixer_vector
-    cross_sum = lax.psum(jnp.sum(gated * mixer_scaled, axis=-1), "tensor")
+    cross_sum = both(jnp.sum(gated * mixer_scaled, axis=-1))
     grad_gated = (
         mixer_inverse * mixer_scaled
         - gated * mixer_inverse**3 * (cross_sum / mixer_width)[..., None]
@@ -325,16 +382,11 @@
         grad_decay_log,
         grad_skip_scale,
     ) = mixer_back(grad_gated)
-    state_total = lax.psum(grad_state_act.astype(jnp.bfloat16), "tensor").astype(jnp.float32)
-    grad_state_pre, grad_state_conv = state_back(state_total)
+    grad_state_pre, grad_state_conv = state_back(grad_state_act)
     gating_rows = to_rows(grad_gating_pre)
     inner_rows = to_rows(grad_inner_pre)
     state_rows = to_rows(grad_state_pre)
     step_rows = to_rows(grad_step_pre)
-    grad_gating = row_dot(normed, gating_rows)
-    grad_inner = row_dot(normed, inner_rows)
-    grad_state = row_dot(normed, state_rows)
-    grad_step = row_dot(normed, step_rows)
     grad_attended = (
         back_dot(branch_grad, attention_out)
         .astype(jnp.bfloat16)
@@ -382,14 +434,11 @@
     query_rows = to_rows(grad_query_pre)
     key_grad_rows = to_rows(grad_key_pre)
     value_grad_rows = to_rows(grad_values)
-    grad_query = row_dot(normed, query_rows)
-    grad_key = row_dot(normed, key_grad_rows)
-    grad_value = row_dot(normed, value_grad_rows)
     first_back = (
         back_dot(gating_rows, gating_weight)
         + back_dot(inner_rows, inner_weight)
         + back_dot(step_rows, step_weight)
-        + 0.5 * back_dot(state_rows, state_weight)
+        + back_dot(state_rows, state_weight)
     )
     first_back = (
         first_back
@@ -397,101 +446,80 @@
         + back_dot(key_grad_rows, key_weight)
         + back_dot(value_grad_rows, value_weight)
     )
-    grad_normed = lax.psum_scatter(
-        first_back.astype(jnp.bfloat16), "tensor", scatter_dimension=0, tiled=True
-    ).astype(jnp.float32)
+    grad_normed = scatter_rows(first_back)
     grad_first_gain = jnp.sum(grad_normed * tokens * first_inverse, axis=0)
     input_grad = grad_residual + norm_back(grad_normed, tokens, first_inverse, first_vector)
-    small_sums = lax.psum(
-        (
-            widen_piece(grad_step_bias, H_SSM),
-            widen_piece(grad_decay_log, H_SSM),
-            widen_piece(grad_skip_scale, H_SSM),
-            widen_piece(grad_inner_conv, mixer_width),
-            0.5 * grad_state_conv,
-            widen_piece(grad_mixer_gain, mixer_width),
-            grad_first_gain,
-            grad_second_gain,
-        ),
-        ("dp", "tensor"),
-    )
-    shares = (
-        lax.psum_scatter(flat_rows(grad_gating), "dp", scatter_dimension=0, tiled=True),
-        lax.psum_scatter(flat_rows(grad_inner), "dp", scatter_dimension=0, tiled=True),
-        lax.psum_scatter(flat_rows(grad_state), "dp", scatter_dimension=0, tiled=True),
-        lax.psum_scatter(flat_rows(grad_step), "dp", scatter_dimension=0, tiled=True),
-        lax.psum_scatter(flat_rows(grad_mixer_proj), "dp", scatter_dimension=0, tiled=True),
-        lax.psum_scatter(flat_rows(grad_query), "dp", scatter_dimension=0, tiled=True),
-        lax.psum_scatter(flat_rows(grad_key), "dp", scatter_dimension=0, tiled=True),
-        lax.psum_scatter(flat_rows(grad_value), "dp", scatter_dimension=0, tiled=True),
-        lax.psum_scatter(
-            flat_rows(attention_output_gradient), "dp", scatter_dimension=0, tiled=True
-        ),
-        lax.psum_scatter(flat_rows(grad_gate), "dp", scatter_dimension=0, tiled=True),
-        lax.psum_scatter(flat_rows(grad_up), "dp", scatter_dimension=0, tiled=True),
-        lax.psum_scatter(flat_rows(grad_down), "dp", scatter_dimension=0, tiled=True),
-    )
-    summed = (
-        lax.all_gather(shares[0].astype(jnp.bfloat16), "dp", axis=0, tiled=True).astype(
-            jnp.float32
-        ),
-        lax.all_gather(shares[1].astype(jnp.bfloat16), "dp", axis=0, tiled=True).astype(
-            jnp.float32
-        ),
-        lax.all_gather(shares[2].astype(jnp.bfloat16), "dp", axis=0, tiled=True).astype(
-            jnp.float32
-        ),
-        lax.all_gather(shares[3].astype(jnp.bfloat16), "dp", axis=0, tiled=True).astype(
-            jnp.float32
-        ),
-        lax.all_gather(shares[4].astype(jnp.bfloat16), "dp", axis=0, tiled=True).astype(
-            jnp.float32
-        ),
-        lax.all_gather(shares[5].astype(jnp.bfloat16), "dp", axis=0, tiled=True).astype(
-            jnp.float32
-        ),
-        lax.all_gather(shares[6].astype(jnp.bfloat16), "dp", axis=0, tiled=True).astype(
-            jnp.float32
-        ),
-        lax.all_gather(shares[7].astype(jnp.bfloat16), "dp", axis=0, tiled=True).astype(
-            jnp.float32
-        ),
-        lax.all_gather(shares[8].astype(jnp.bfloat16), "dp", axis=0, tiled=True).astype(
-            jnp.float32
-        ),
-        lax.all_gather(shares[9].astype(jnp.bfloat16), "dp", axis=0, tiled=True).astype(
-            jnp.float32
-        ),
-        lax.all_gather(shares[10].astype(jnp.bfloat16), "dp", axis=0, tiled=True).astype(
-            jnp.float32
-        ),
-        lax.all_gather(shares[11].astype(jnp.bfloat16), "dp", axis=0, tiled=True).astype(
-            jnp.float32
-        ),
+    model_width = normed.shape[1]
+    step_padded = jnp.pad(step_rows, ((0, 0), (0, 128 - head_local)))
+    input_rows = jnp.concatenate(
+        [gating_rows, inner_rows, query_rows, key_grad_rows, value_grad_rows, step_padded], axis=1
+    )
+    grad_inputs = row_dot(normed, input_rows)
+    grad_state = row_dot(normed, state_rows)
+    grad_gate, grad_up, grad_down = sum_over_dp([grad_gate, grad_up, grad_down], False)
+    grad_mixer_proj, attention_output_gradient = sum_over_dp(
+        [grad_mixer_proj, attention_output_gradient], True
+    )
+    (grad_inputs,) = sum_over_dp([grad_inputs], False)
+    (grad_state,) = sum_over_dp([grad_state], True, over_tensor=True)
+    grad_gating, grad_inner, grad_query, grad_key, grad_value, grad_step = jnp.split(
+        grad_inputs,
+        [
+            channels,
+            2 * channels,
+            2 * channels + query_heads * HD,
+            2 * channels + (query_heads + kv_heads) * HD,
+            2 * channels + (query_heads + 2 * kv_heads) * HD,
+        ],
+        axis=1,
+    )
+    state_width = state_weight.shape[1]
+    shared_small = jnp.concatenate(
+        [grad_state_conv.reshape(-1), grad_first_gain, grad_second_gain]
+    )
+    own_small = jnp.concatenate(
+        [
+            grad_inner_conv.reshape(-1),
+            grad_mixer_gain,
+            grad_step_bias,
+            grad_decay_log,
+            grad_skip_scale,
+        ]
+    )
+    small = sum_small(jnp.concatenate([both(shared_small), own_small]))
+    shared_small, own_small = small[: shared_small.shape[0]], small[shared_small.shape[0] :]
+    taps = inner_conv.shape[0]
+    grad_state_conv, grad_first_gain, grad_second_gain = jnp.split(
+        shared_small, [taps * state_width, taps * state_width + model_width]
+    )
+    starts = [taps * channels, (taps + 1) * channels]
+    starts = starts + [starts[1] + head_local, starts[1] + 2 * head_local]
+    grad_inner_conv, grad_mixer_gain, grad_step_bias, grad_decay_log, grad_skip_scale = jnp.split(
+        own_small, starts
     )
     return (
         block_output,
         input_grad,
-        summed[0].reshape(gating_weight.shape),
-        summed[1].reshape(inner_weight.shape),
-        summed[2].reshape(state_weight.shape),
-        summed[3].reshape(step_weight.shape),
-        narrow_piece(small_sums[0], head_local),
-        narrow_piece(small_sums[1], head_local),
-        narrow_piece(small_sums[2], head_local),
-        narrow_piece(small_sums[3], channels),
-        small_sums[4],
-        narrow_piece(small_sums[5], channels),
-        summed[4].reshape(mixer_proj.shape),
-        summed[5].reshape(query_weight.shape),
-        summed[6].reshape(key_weight.shape),
-        summed[7].reshape(value_weight.shape),
-        summed[8].reshape(attention_out.shape),
-        small_sums[6],
-        small_sums[7],
-        summed[9].reshape(gate_weight.shape),
-        summed[10].reshape(up_weight.shape),
-        summed[11].reshape(down_projection_weight.shape),
+        grad_gating,
+        grad_inner,
+        grad_state,
+        grad_step[:, :head_local],
+        grad_step_bias,
+        grad_decay_log,
+        grad_skip_scale,
+        grad_inner_conv.reshape(taps, channels),
+        grad_state_conv.reshape(taps, state_width),
+        grad_mixer_gain,
+        grad_mixer_proj,
+        grad_query,
+        grad_key,
+        grad_value,
+        attention_output_gradient,
+        grad_first_gain,
+        grad_second_gain,
+        grad_gate,
+        grad_up,
+        grad_down,
     )
 
 

time: 1900 us -> 1160 us (0.61)
  blocking collectives: 726 us -> 0 us
  waiting for transfers between devices: 269 us -> 339 us
  other arithmetic: 215 us -> 162 us
  starting transfers between devices: 1 us -> 40.1 us
  local copies, waits for them, and re-layouts: 389 us -> 354 us
  matrix products: 269 us -> 249 us
    unnamed x1 -> x0, blocking collectives: 536 us -> none
    ppermute x0 -> x48, waiting for transfers between devices: none -> 339 us  [the longest x36 211 us: flip(): return lax.ppermute(value, 'dp', [(i, i ^ bit) for i in range(size)])]
    reduce_scatter x4 -> x0, waiting for transfers between devices: 148 us -> none  [the longest x1 53.8 us: on_device(): lax.psum_scatter(mixer_part + attn_part, 'tensor', scatter_dimension=0, t...]
    all_gather x6 -> x0, blocking collectives: 139 us -> none  [the longest x1 28.6 us: on_device(): lax.all_gather(shares[3].astype(jnp.bfloat16), 'dp', axis=0, tiled=True)]
    all_gather x10 -> x0, waiting for transfers between devices: 121 us -> none  [the longest x1 32.6 us: on_device(): lax.all_gather(normed_two_share, 'tensor', axis=0, tiled=True)]
    reshape x12 -> x0, other arithmetic: 93 us -> none  [the longest x1 15 us: on_device(): summed[9].reshape(gate_weight.shape)]
    reshape x24 -> x13, local copies, waits for them, and re-layouts: 56.9 us -> 2.32 us  [the longest x8 0.76 us: one_block(): tail_weight = jnp.exp(cumulative[:, -1:, :] - cumulative) * step_block]
    psum x3 -> x0, blocking collectives: 50.8 us -> none  [the longest x1 40.6 us: on_device(): lax.psum((widen_piece(grad_step_bias, H_SSM), widen_piece(grad_decay_log,...]
  transfers between devices with their start and end apart: 15 -> 48, of which waited for: 10 -> 27; matrix products, arithmetic and copies ran while one was open for 15% -> 43% of each run, Pallas kernels for 0% -> 0%
where the time goes in v1:
time: 1160 us; the launch traced here: 1150 us
  local copies, waits for them, and re-layouts  354 us (31%)
  waiting for transfers between devices  339 us (29%)
  matrix products  249 us (21%)
  other arithmetic  162 us (14%)
  starting transfers between devices  40.1 us (3%)
    ppermute x36, waiting for transfers between devices, flip(): return lax.ppermute(value, 'dp', [(i, i ^ bit) for i in range(size)])  211 us
    dynamic_update_slice x48, local copies, waits for them, and re-layouts, ssd_spans(): lax.scan(jax.checkpoint(one_block), initial, (to_blocks(inner), to_blocks...  193 us
    ppermute x12, waiting for transfers between devices, swap_tensor(): return lax.ppermute(value, 'tensor', [(0, 1), (1, 0)])  128 us
    dot_general x24, matrix products, one_block(): jnp.einsum('stuh,suhp->sthp', mixing, inner_block, precision=top_precision)  50.8 us
    dot_general x12, matrix products, back_dot(): lax.dot_general(left_side, right_side, (((1,), (1,)), ((), ())), preferre...  37.7 us
    squeeze x40, local copies, waits for them, and re-layouts, ssd_spans(): lax.scan(jax.checkpoint(one_block), initial, (to_blocks(inner), to_blocks...  34.7 us
    unnamed x347, local copies, waits for them, and re-layouts  33.7 us
    dot_general x32, matrix products, one_block(): jnp.einsum('stn,shpn->sthp', out_block, carry_state, precision=top_precis...  30.1 us
  transfers between devices with their start and end apart: 48, of which 27 were waited for; matrix products, arithmetic and copies ran while one was open for 43% of the time, Pallas kernels for 0%

profile of v1, /device:TPU:0, one launch (start us, length us, event | category | flops | bytes accessed | tf_op | source)
XLA Modules:
  0.0 1148.3 jit_solution(4132277636215112424)
XLA Ops:
  21.4 11.2 collective-permute-done
  66.4 170.1 %while.41 = (s32[]{:T(128)}, f32[1,12,64,128]{3,2,1,0:T(8,128)S(1)}, f32[8,1,128,12,64]{2,0,4,3,1:T(8,128)}, f32[8,1,12,64,128]{4,3,2,1,0:T(8,128)}, f32[8,1,128...) while((s32[]{:T(128)}, ...), condition=%wide.region_2.3_spmd.clone, body=%wide.region_1.2_spmd.clone.sunk | while | flops 482120192 | bytes 5217264 | solution.py:188
  74.3 11.0 dynamic_update_slice.66
  95.5 11.0 dynamic_update_slice.66
  116.8 11.0 dynamic_update_slice.66
  138.1 11.0 dynamic_update_slice.66
  159.3 11.0 dynamic_update_slice.66
  180.6 11.0 dynamic_update_slice.66
  201.9 11.0 dynamic_update_slice.66
  273.7 24.4 %collective-permute-done.2 = bf16[512,1024]{1,0:T(8,128)(2,1)} collective-permute-done((bf16[512,1024]{1,0:T(8,128)(2,1)}, bf16[512,1024]{1,0:T(8,128)(2,1)}, u32[]{:S(2)}, u32[]{:S(2)}) %collective-permute-start.2) | collective-permute-done | bytes 1048608 | tf_op jit(solution)/shard_map/ppermute | solution.py:75
  307.1 13.4 %collective-permute-done.5 = bf16[512,1024]{1,0:T(8,128)(2,1)} collective-permute-done((bf16[512,1024]{1,0:T(8,128)(2,1)}, bf16[512,1024]{1,0:T(8,128)(2,1)}, u32[]{:S(2)}, u32[]{:S(2)}) %collective-permute-start.5) | collective-permute-done | bytes 1048608 | tf_op jit(solution)/shard_map/ppermute | solution.py:75
  322.8 17.8 %collective-permute-done.3 = bf16[512,1024]{1,0:T(8,128)(2,1)} collective-permute-done((bf16[512,1024]{1,0:T(8,128)(2,1)}, bf16[512,1024]{1,0:T(8,128)(2,1)}, u32[]{:S(2)}, u32[]{:S(2)}) %collective-permute-start.3) | collective-permute-done | bytes 1048608 | tf_op jit(solution)/shard_map/ppermute | solution.py:75
  374.3 32.2 %collective-permute-done.6 = bf16[512,1024]{1,0:T(8,128)(2,1)S(1)} collective-permute-done((bf16[512,1024]{1,0:T(8,128)(2,1)S(1)}, bf16[512,1024]{1,0:T(8,128)(2,1)S(1)}, u32[]{:S(2)}, u32[]{:S(2)}) %collective-permute-start.6) | collective-permute-done | bytes 1048608 | tf_op jit(solution)/shard_map/ppermute | solution.py:75
  419.5 14.4 %collective-permute-done.7 = bf16[512,1024]{1,0:T(8,128)(2,1)S(1)} collective-permute-done((bf16[512,1024]{1,0:T(8,128)(2,1)S(1)}, bf16[512,1024]{1,0:T(8,128)(2,1)S(1)}, u32[]{:S(2)}, u32[]{:S(2)}) %collective-permute-start.7) | collective-permute-done | bytes 1048608 | tf_op jit(solution)/shard_map/ppermute | solution.py:75
  511.3 251.1 %while.42 = (s32[]{:T(128)}, f32[12]{0:T(128)}, f32[1,12,64,128]{3,2,1,0:T(8,128)S(1)}, f32[8,1,128,12,64]{2,0,4,3,1:T(8,128)}, f32[8,1,128,128]{3,2,0,1:T(8,128...) while((s32[]{:T(128)}, f32[12]{0:T(128)}, ...), condition=%wide.region_20.21_spmd.clone, body=%wide.region_11.20_spmd.clone.sunk | while | flops 1141961216 | bytes 13464880 | solution.py:188
  770.2 11.1 multiply_reduce_fusion.7
  852.2 14.4 %collective-permute-done.9 = bf16[512,1024]{1,0:T(8,128)(2,1)} collective-permute-done((bf16[512,1024]{1,0:T(8,128)(2,1)}, bf16[512,1024]{1,0:T(8,128)(2,1)}, u32[]{:S(2)}, u32[]{:S(2)}) %collective-permute-start.9) | collective-permute-done | bytes 1048608 | tf_op jit(solution)/shard_map/ppermute | solution.py:75
  884.6 55.7 %collective-permute-done.29 = f32[6948]{0:T(1024)S(1)} collective-permute-done((f32[6948]{0:T(1024)S(1)}, f32[6948]{0:T(1024)S(1)}, u32[]{:S(2)}, u32[]{:S(2)}) %collective-permute-start.29) | collective-permute-done | bytes 27824 | tf_op jit(solution)/shard_map/ppermute | solution.py:105
  950.9 13.7 %collective-permute-done.12 = bf16[128,2048]{1,0:T(8,128)(2,1)S(1)} collective-permute-done((bf16[128,2048]{1,0:T(8,128)(2,1)S(1)}, bf16[128,2048]{1,0:T(8,128)(2,1)S(1)}, u32[]{:S(2)}, u32[]{:S(2)}) %collective-permute-start.12) | collective-permute-done | bytes 524320 | tf_op jit(solution)/shard_map/ppermute | solution.py:105
  964.8 16.6 %collective-permute-done.42 = bf16[384,1024]{1,0:T(8,128)(2,1)S(1)} collective-permute-done((bf16[384,1024]{1,0:T(8,128)(2,1)S(1)}, bf16[384,1024]{1,0:T(8,128)(2,1)S(1)}, u32[]{:S(2)}, u32[]{:S(2)}) %collective-permute-start.42) | collective-permute-done | bytes 786464 | tf_op jit(solution)/shard_map/ppermute | solution.py:105
  985.1 25.2 %collective-permute-done.43 = bf16[192,1024]{1,0:T(8,128)(2,1)S(1)} collective-permute-done((bf16[192,1024]{1,0:T(8,128)(2,1)S(1)}, bf16[192,1024]{1,0:T(8,128)(2,1)S(1)}, u32[]{:S(2)}, u32[]{:S(2)}) %collective-permute-start.43) | collective-permute-done | bytes 393248 | tf_op jit(solution)/shard_map/ppermute | solution.py:105
  1010.5 13.8 %collective-permute-done.14 = bf16[64,2048]{1,0:T(8,128)(2,1)S(1)} collective-permute-done((bf16[64,2048]{1,0:T(8,128)(2,1)S(1)}, bf16[64,2048]{1,0:T(8,128)(2,1)S(1)}, u32[]{:S(2)}, u32[]{:S(2)}) %collective-permute-start.14) | collective-permute-done | bytes 262176 | tf_op jit(solution)/shard_map/ppermute | solution.py:105
  1052.2 14.2 %collective-permute-done.45 = bf16[384,1024]{1,0:T(8,128)(2,1)S(1)} collective-permute-done((bf16[384,1024]{1,0:T(8,128)(2,1)S(1)}, bf16[384,1024]{1,0:T(8,128)(2,1)S(1)}, u32[]{:S(2)}, u32[]{:S(2)}) %collective-permute-start.45) | collective-permute-done | bytes 786464 | tf_op jit(solution)/shard_map/ppermute | solution.py:105
  1083.2 26.9 %collective-permute-done.46 = bf16[768,1024]{1,0:T(8,128)(2,1)} collective-permute-done((bf16[768,1024]{1,0:T(8,128)(2,1)}, bf16[768,1024]{1,0:T(8,128)(2,1)}, u32[]{:S(2)}, u32[]{:S(2)}) %collective-permute-start.46) | collective-permute-done | bytes 1572896 | tf_op jit(solution)/shard_map/ppermute | solution.py:105
  (991 shorter events, 761.9 us)
Async XLA Ops:
  6.2 26.4 %collective-permute-start = (bf16[512,1024]{1,0:T(8,128)(2,1)}, bf16[512,1024]{1,0:T(8,128)(2,1)}, u32[]{:S(2)}, u32[]{:S(2)}) collective-permute-start(bf16[512,1024]{1,0:T(8,128)(2,1)} %fusion.152), channel_id=1, source_target_pairs={{0,1},{1,0},{2,3},{3,2},{4,5},{5,4},{6,7},{7,6},{8,9},{9,8},{10,11... | collective-permute-start | bytes 3145736 | tf_op jit(solution)/shard_map/ppermute | solution.py:75
  271.9 48.6 %collective-permute-start.5 = (bf16[512,1024]{1,0:T(8,128)(2,1)}, bf16[512,1024]{1,0:T(8,128)(2,1)}, u32[]{:S(2)}, u32[]{:S(2)}) collective-permute-start(bf16[512,1024]{1,0:T(8,128)(2,1)} %param.29), channel_id=1, source_target_pairs={{0,1},{1,0},{2,3},{3,2},{4,5},{5,4},{6,7},{7,6},{8,9},{9,8},{10,11... | collective-permute-start | bytes 3145736 | tf_op jit(solution)/shard_map/ppermute | solution.py:75
  303.0 37.7 %collective-permute-start.3 = (bf16[512,1024]{1,0:T(8,128)(2,1)}, bf16[512,1024]{1,0:T(8,128)(2,1)}, u32[]{:S(2)}, u32[]{:S(2)}) collective-permute-start(bf16[512,1024]{1,0:T(8,128)(2,1)} %multiply_convert_fusion.4), channel_id=1, source_target_pairs={{0,1},{1,0},{2,3},{3,2},{4,5},{5,4},{6,7},{7,6},{8,9},{9,8},{10,11... | collective-permute-start | bytes 3145736 | tf_op jit(solution)/shard_map/ppermute | solution.py:75
  361.1 46.7 %collective-permute-start.4 = (bf16[512,1024]{1,0:T(8,128)(2,1)S(1)}, bf16[512,1024]{1,0:T(8,128)(2,1)S(1)}, u32[]{:S(2)}, u32[]{:S(2)}) collective-permute-start(bf16[512,1024]{1,0:T(8,128)(2,1)S(1)} %dynamic-slice_convert_fusion.10), channel_id=1, source_target_pairs={{0,1},{1,0},{2,3},{3,2},{4,5},{5,4},{6,7},{7,6},{8,9},{9,8},{10,11... | collective-permute-start | bytes 3145736 | tf_op jit(solution)/shard_map/ppermute | solution.py:75
  366.8 39.8 %collective-permute-start.6 = (bf16[512,1024]{1,0:T(8,128)(2,1)S(1)}, bf16[512,1024]{1,0:T(8,128)(2,1)S(1)}, u32[]{:S(2)}, u32[]{:S(2)}) collective-permute-start(bf16[512,1024]{1,0:T(8,128)(2,1)S(1)} %dynamic-slice_convert_fusion.9), channel_id=1, source_target_pairs={{0,1},{1,0},{2,3},{3,2},{4,5},{5,4},{6,7},{7,6},{8,9},{9,8},{10,11... | collective-permute-start | bytes 3145736 | tf_op jit(solution)/shard_map/ppermute | solution.py:75
  419.5 449.7 %collective-permute-start.40 = (bf16[1536,1024]{1,0:T(8,128)(2,1)}, bf16[1536,1024]{1,0:T(8,128)(2,1)}, u32[]{:S(2)}, u32[]{:S(2)}) collective-permute-start(bf16[1536,1024]{1,0:T(8,128)(2,1)} %pad_maximum_fusion.1), channel_id=1, source_target_pairs={{0,2},{2,0},{4,6},{6,4},{8,10},{10,8},{12,14},{14,12},{16,18},{18,... | collective-permute-start | bytes 9437192 | tf_op jit(solution)/shard_map/ppermute | solution.py:105
  478.4 370.8 %collective-permute-start.32 = (bf16[512,1024]{1,0:T(8,128)(2,1)}, bf16[512,1024]{1,0:T(8,128)(2,1)}, u32[]{:S(2)}, u32[]{:S(2)}) collective-permute-start(bf16[512,1024]{1,0:T(8,128)(2,1)} %pad_maximum_fusion.14), channel_id=1, source_target_pairs={{0,2},{2,0},{4,6},{6,4},{8,10},{10,8},{12,14},{14,12},{16,18},{18,... | collective-permute-start | bytes 3145736 | tf_op jit(solution)/shard_map/ppermute | solution.py:105
  847.0 30.5 %collective-permute-start.10 = (bf16[512,2048]{1,0:T(8,128)(2,1)}, bf16[512,2048]{1,0:T(8,128)(2,1)}, u32[]{:S(2)}, u32[]{:S(2)}) collective-permute-start(bf16[512,2048]{1,0:T(8,128)(2,1)} %dynamic-slice_convert_fusion), channel_id=1, source_target_pairs={{0,2},{2,0},{4,6},{6,4},{8,10},{10,8},{12,14},{14,12},{16,18},{18,... | collective-permute-start | bytes 6291464 | tf_op jit(solution)/shard_map/ppermute | solution.py:105
  874.8 65.8 %collective-permute-start.34 = (bf16[128,1024]{1,0:T(8,128)(2,1)S(1)}, bf16[128,1024]{1,0:T(8,128)(2,1)S(1)}, u32[]{:S(2)}, u32[]{:S(2)}) collective-permute-start(bf16[128,1024]{1,0:T(8,128)(2,1)S(1)} %constant_dynamic-slice_fusion.5), channel_id=1, source_target_pairs={{0,16},{2,18},{4,20},{6,22},{8,24},{10,26},{12,28},{14,30},{16,0},... | collective-permute-start | bytes 786440 | tf_op jit(solution)/shard_map/ppermute | solution.py:105
  880.7 65.7 %collective-permute-start.11 = (bf16[256,2048]{1,0:T(8,128)(2,1)S(1)}, bf16[256,2048]{1,0:T(8,128)(2,1)S(1)}, u32[]{:S(2)}, u32[]{:S(2)}) collective-permute-start(bf16[256,2048]{1,0:T(8,128)(2,1)S(1)} %constant_dynamic-slice_fusion.12), channel_id=1, source_target_pairs={{0,4},{2,6},{4,0},{6,2},{8,12},{10,14},{12,8},{14,10},{16,20},{18,... | collective-permute-start | bytes 3145736 | tf_op jit(solution)/shard_map/ppermute | solution.py:105
  881.4 67.3 %collective-permute-start.41 = (bf16[768,1024]{1,0:T(8,128)(2,1)S(1)}, bf16[768,1024]{1,0:T(8,128)(2,1)S(1)}, u32[]{:S(2)}, u32[]{:S(2)}) collective-permute-start(bf16[768,1024]{1,0:T(8,128)(2,1)S(1)} %constant_dynamic-slice_fusion.3), channel_id=1, source_target_pairs={{0,4},{2,6},{4,0},{6,2},{8,12},{10,14},{12,8},{14,10},{16,20},{18,... | collective-permute-start | bytes 4718600 | tf_op jit(solution)/shard_map/ppermute | solution.py:105
  883.0 57.4 %collective-permute-start.29 = (f32[6948]{0:T(1024)S(1)}, f32[6948]{0:T(1024)S(1)}, u32[]{:S(2)}, u32[]{:S(2)}) collective-permute-start(f32[6948]{0:T(1024)S(1)} %add.551), channel_id=1, source_target_pairs={{0,4},{2,6},{4,0},{6,2},{8,12},{10,14},{12,8},{14,10},{16,20},{18,... | collective-permute-start | bytes 83384 | tf_op jit(solution)/shard_map/ppermute | solution.py:105
  944.2 129.1 %collective-permute-start.31 = (f32[6948]{0:T(1024)S(1)}, f32[6948]{0:T(1024)S(1)}, u32[]{:S(2)}, u32[]{:S(2)}) collective-permute-start(f32[6948]{0:T(1024)S(1)} %add.553), channel_id=1, source_target_pairs={{0,16},{2,18},{4,20},{6,22},{8,24},{10,26},{12,28},{14,30},{16,0},... | collective-permute-start | bytes 83384 | tf_op jit(solution)/shard_map/ppermute | solution.py:105
  949.4 32.1 %collective-permute-start.42 = (bf16[384,1024]{1,0:T(8,128)(2,1)S(1)}, bf16[384,1024]{1,0:T(8,128)(2,1)S(1)}, u32[]{:S(2)}, u32[]{:S(2)}) collective-permute-start(bf16[384,1024]{1,0:T(8,128)(2,1)S(1)} %constant_dynamic-slice_fusion.2), channel_id=1, source_target_pairs={{0,8},{2,10},{4,12},{6,14},{8,0},{10,2},{12,4},{14,6},{16,24},{18,... | collective-permute-start | bytes 2359304 | tf_op jit(solution)/shard_map/ppermute | solution.py:105
  981.8 28.4 %collective-permute-start.43 = (bf16[192,1024]{1,0:T(8,128)(2,1)S(1)}, bf16[192,1024]{1,0:T(8,128)(2,1)S(1)}, u32[]{:S(2)}, u32[]{:S(2)}) collective-permute-start(bf16[192,1024]{1,0:T(8,128)(2,1)S(1)} %constant_dynamic-slice_fusion.1), channel_id=1, source_target_pairs={{0,16},{2,18},{4,20},{6,22},{8,24},{10,26},{12,28},{14,30},{16,0},... | collective-permute-start | bytes 1179656 | tf_op jit(solution)/shard_map/ppermute | solution.py:105
  982.0 42.3 %collective-permute-start.14 = (bf16[64,2048]{1,0:T(8,128)(2,1)S(1)}, bf16[64,2048]{1,0:T(8,128)(2,1)S(1)}, u32[]{:S(2)}, u32[]{:S(2)}) collective-permute-start(bf16[64,2048]{1,0:T(8,128)(2,1)S(1)} %add_convert_fusion.13), channel_id=1, source_target_pairs={{0,16},{2,18},{4,20},{6,22},{8,24},{10,26},{12,28},{14,30},{16,0},... | collective-permute-start | bytes 786440 | tf_op jit(solution)/shard_map/ppermute | solution.py:105
  985.0 45.0 %collective-permute-start.37 = (bf16[128,1024]{1,0:T(8,128)(2,1)S(1)}, bf16[128,1024]{1,0:T(8,128)(2,1)S(1)}, u32[]{:S(2)}, u32[]{:S(2)}) collective-permute-start(bf16[128,1024]{1,0:T(8,128)(2,1)S(1)} %pad_maximum_fusion.24), channel_id=1, source_target_pairs={{0,16},{2,18},{4,20},{6,22},{8,24},{10,26},{12,28},{14,30},{16,0},... | collective-permute-start | bytes 786440 | tf_op jit(solution)/shard_map/ppermute | solution.py:105
  1010.4 28.0 %collective-permute-start.44 = (bf16[192,1024]{1,0:T(8,128)(2,1)S(1)}, bf16[192,1024]{1,0:T(8,128)(2,1)S(1)}, u32[]{:S(2)}, u32[]{:S(2)}) collective-permute-start(bf16[192,1024]{1,0:T(8,128)(2,1)S(1)} %add_convert_fusion.10), channel_id=1, source_target_pairs={{0,16},{2,18},{4,20},{6,22},{8,24},{10,26},{12,28},{14,30},{16,0},... | collective-permute-start | bytes 1179656 | tf_op jit(solution)/shard_map/ppermute | solution.py:105
  1038.5 28.0 %collective-permute-start.45 = (bf16[384,1024]{1,0:T(8,128)(2,1)S(1)}, bf16[384,1024]{1,0:T(8,128)(2,1)S(1)}, u32[]{:S(2)}, u32[]{:S(2)}) collective-permute-start(bf16[384,1024]{1,0:T(8,128)(2,1)S(1)} %pad_maximum_fusion.15), channel_id=1, source_target_pairs={{0,8},{2,10},{4,12},{6,14},{8,0},{10,2},{12,4},{14,6},{16,24},{18,... | collective-permute-start | bytes 2359304 | tf_op jit(solution)/shard_map/ppermute | solution.py:105
  1039.4 38.2 %collective-permute-start.38 = (bf16[256,1024]{1,0:T(8,128)(2,1)}, bf16[256,1024]{1,0:T(8,128)(2,1)S(1)}, u32[]{:S(2)}, u32[]{:S(2)}) collective-permute-start(bf16[256,1024]{1,0:T(8,128)(2,1)} %pad_maximum_fusion.18), channel_id=1, source_target_pairs={{0,8},{2,10},{4,12},{6,14},{8,0},{10,2},{12,4},{14,6},{16,24},{18,... | collective-permute-start | bytes 1572872 | tf_op jit(solution)/shard_map/ppermute | solution.py:105
  1051.1 26.8 %collective-permute-start.16 = (bf16[256,2048]{1,0:T(8,128)(2,1)}, bf16[256,2048]{1,0:T(8,128)(2,1)}, u32[]{:S(2)}, u32[]{:S(2)}) collective-permute-start(bf16[256,2048]{1,0:T(8,128)(2,1)} %pad_maximum_fusion.13), channel_id=1, source_target_pairs={{0,4},{2,6},{4,0},{6,2},{8,12},{10,14},{12,8},{14,10},{16,20},{18,... | collective-permute-start | bytes 3145736 | tf_op jit(solution)/shard_map/ppermute | solution.py:105
  1069.0 41.1 %collective-permute-start.46 = (bf16[768,1024]{1,0:T(8,128)(2,1)}, bf16[768,1024]{1,0:T(8,128)(2,1)}, u32[]{:S(2)}, u32[]{:S(2)}) collective-permute-start(bf16[768,1024]{1,0:T(8,128)(2,1)} %pad_maximum_fusion.7), channel_id=1, source_target_pairs={{0,4},{2,6},{4,0},{6,2},{8,12},{10,14},{12,8},{14,10},{16,20},{18,... | collective-permute-start | bytes 4718600 | tf_op jit(solution)/shard_map/ppermute | solution.py:105
  1081.6 41.3 %collective-permute-start.17 = (bf16[512,2048]{1,0:T(8,128)(2,1)}, bf16[512,2048]{1,0:T(8,128)(2,1)}, u32[]{:S(2)}, u32[]{:S(2)}) collective-permute-start(bf16[512,2048]{1,0:T(8,128)(2,1)} %pad_maximum_fusion.6), channel_id=1, source_target_pairs={{0,2},{2,0},{4,6},{6,4},{8,10},{10,8},{12,14},{14,12},{16,18},{18,... | collective-permute-start | bytes 6291464 | tf_op jit(solution)/shard_map/ppermute | solution.py:105
  1082.8 34.0 %collective-permute-start.39 = (bf16[512,1024]{1,0:T(8,128)(2,1)}, bf16[512,1024]{1,0:T(8,128)(2,1)}, u32[]{:S(2)}, u32[]{:S(2)}) collective-permute-start(bf16[512,1024]{1,0:T(8,128)(2,1)} %pad_maximum_fusion.10), channel_id=1, source_target_pairs={{0,2},{2,0},{4,6},{6,4},{8,10},{10,8},{12,14},{14,12},{16,18},{18,... | collective-permute-start | bytes 3145736 | tf_op jit(solution)/shard_map/ppermute | solution.py:105
  (191 other events, 2320.1 us)

commit v2 on v1

--- a/solution.py
+++ b/solution.py
@@ -1,6 +1,8 @@
 import jax
 import jax.numpy as jnp
 from jax import lax
+from jax.experimental import pallas as pl
+from jax.experimental.pallas import tpu as pltpu
 from jax.sharding import PartitionSpec as P
 
 H_SSM = 24
@@ -8,6 +10,8 @@
 HD = 64
 SPAN = 128
 ATT_BLOCK = 512
+N_STATE = 128
+LANES = 128
 
 
 epsilon = 1e-05
@@ -29,16 +33,6 @@
     return lax.dot_general(
         left_side, right_side, (((1,), (1,)), ((), ())), preferred_element_type=jnp.float32
     )
-
-
-def causal_conv(value_tensor, kernel):
-    tap_count = kernel.shape[0]
-    length = value_tensor.shape[1]
-    padded = jnp.pad(value_tensor, ((0, 0), (tap_count - 1, 0), (0, 0)))
-    result = padded[:, 0:length] * kernel[0]
-    for offset in range(1, tap_count):
-        result = result + padded[:, offset : offset + length] * kernel[offset]
-    return result
 
 
 def rope_tables(length, head_size):
@@ -111,7 +105,7 @@
     return bits[:1] + bits[2:] + bits[1:2] if far_first else bits
 
 
-def sum_over_dp(arrays, far_first, over_tensor=False):
+def sum_over_dp(arrays, far_first, tensor_columns=None):
     index = lax.axis_index("dp")
     bits = bits_in_order(far_first)
     places = [(index // bit) % 2 for bit in bits]
@@ -128,8 +122,11 @@
             keep, send = half_of(current, place), half_of(current, 1 - place)
         got = flip(send, bit)
         current = (keep.astype(jnp.float32) + got.astype(jnp.float32)).astype(jnp.bfloat16)
-    if over_tensor:
-        current = (current.astype(jnp.float32) + swap_tensor(current).astype(jnp.float32)).astype(jnp.bfloat16)
+    if tensor_columns is not None:
+        start, stop = tensor_columns
+        part = current[:, start:stop]
+        part = (part.astype(jnp.float32) + swap_tensor(part).astype(jnp.float32)).astype(jnp.bfloat16)
+        current = jnp.concatenate([current[:, :start], part, current[:, stop:]], axis=1)
     for bit, place in list(zip(bits, places))[:0:-1]:
         current = in_order(place, current, flip(current, bit))
     other = flip(current, bits[0])
@@ -152,66 +149,385 @@
     return value
 
 
-def ssd_spans(inner, in_vec, out_vec, step_sizes, decay_rate):
-    seq_count, length, head_count, head_size = inner.shape
-    state_size = in_vec.shape[-1]
-    block_count = length // SPAN
-
-    def to_blocks(value_tensor):
-        return jnp.swapaxes(
-            value_tensor.reshape((seq_count, block_count, SPAN) + value_tensor.shape[2:]), 0, 1
-        )
-
-    lower_mask = jnp.arange(SPAN)[:, None] >= jnp.arange(SPAN)[None, :]
-
-    def one_block(carry_state, pieces):
-        inner_block, in_block, out_block, step_block = pieces
-        cumulative = jnp.einsum(
-            "ts,bsh->bth", lower_mask.astype(jnp.float32), step_block * decay_rate, precision=top_precision
-        )
-        log_gaps = cumulative[:, :, None, :] - cumulative[:, None, :, :]
-        within = jnp.exp(jnp.where(lower_mask[None, :, :, None], log_gaps, -1e30))
-        scores = jnp.einsum("stn,sun->stu", out_block, in_block, precision=top_precision)
-        mixing = scores[..., None] * within * step_block[:, None, :, :]
-        within_block = jnp.einsum("stuh,suhp->sthp", mixing, inner_block, precision=top_precision)
-        from_state = (
-            jnp.einsum("stn,shpn->sthp", out_block, carry_state, precision=top_precision)
-            * jnp.exp(cumulative)[..., None]
-        )
-        tail_weight = jnp.exp(cumulative[:, -1:, :] - cumulative) * step_block
-        carry_state = carry_state * jnp.exp(cumulative[:, -1, :])[:, :, None, None] + jnp.einsum(
-            "suh,suhp,sun->shpn", tail_weight, inner_block, in_block, precision=top_precision
-        )
-        return (carry_state, within_block + from_state)
-
-    initial = jnp.zeros((seq_count, head_count, head_size, state_size), inner.dtype)
-    final_state, outputs = lax.scan(
-        jax.checkpoint(one_block),
-        initial,
-        (to_blocks(inner), to_blocks(in_vec), to_blocks(out_vec), to_blocks(step_sizes)),
-    )
-    return jnp.swapaxes(outputs, 0, 1).reshape(seq_count, length, head_count, head_size)
-
-
-def state_piece(pre_values, conv_kernel):
-    return jax.nn.silu(causal_conv(pre_values, conv_kernel))
-
-
-def mixer_piece(
-    inner_pre, state_act, step_pre, gating_pre, inner_conv, step_bias, decay_log, skip_scale
+def sigmoid(v):
+    return 1.0 / (1.0 + jnp.exp(-v))
+
+
+def softplus(v):
+    return jnp.maximum(v, 0.0) + jnp.log1p(jnp.exp(-jnp.abs(v)))
+
+
+def low(v):
+    return v.astype(jnp.bfloat16)
+
+
+def conv_taps(ext, taps, rows):
+    result = ext[5 : 5 + rows] * taps[0:1]
+    for j in range(1, 4):
+        result = result + ext[5 + j : 5 + j + rows] * taps[j : j + 1]
+    return result
+
+
+def exact_dot(left_side, right_side):
+    return jnp.dot(
+        left_side, right_side, preferred_element_type=jnp.float32, precision=top_precision
+    )
+
+
+def grid_of(rows, columns, axis):
+    return lax.broadcasted_iota(jnp.int32, (rows, columns), axis)
+
+
+def pair_wide(values, pair):
+    rows = values.shape[0]
+    low_half = jnp.broadcast_to(values[:, 2 * pair : 2 * pair + 1], (rows, LANES))
+    high_half = jnp.broadcast_to(values[:, 2 * pair + 1 : 2 * pair + 2], (rows, LANES))
+    return jnp.where(grid_of(rows, LANES, 1) < P_SIZE, low_half, high_half)
+
+
+def split_pair(values):
+    left = grid_of(values.shape[0], LANES, 1) < P_SIZE
+    zero = jnp.zeros_like(values)
+    return jnp.concatenate([jnp.where(left, values, zero), jnp.where(left, zero, values)], axis=0)
+
+
+def step_terms(step_ref, head_ref):
+    rows = step_ref.shape[0]
+    shifted = step_ref[...] + head_ref[0:1]
+    steps = softplus(shifted)
+    rate = head_ref[1:2]
+    lower = (grid_of(rows, rows, 0) >= grid_of(rows, rows, 1)).astype(jnp.float32)
+    cumulative = exact_dot(lower, steps * rate)
+    return shifted, steps, rate, cumulative
+
+
+def mixer_forward_kernel(
+    inner_ref, gating_ref, state_ref, step_ref, inner_taps_ref, state_taps_ref, head_ref, skip_ref,
+    gated_ref, scanned_ref, squares_ref, saved_ref,
+    inner_tail, state_tail, carry,
 ):
-    seq_count, length, channels = inner_pre.shape
-    head_count = step_pre.shape[-1]
-    state_size = state_act.shape[-1] // 2
-    inner_act = jax.nn.silu(causal_conv(inner_pre, inner_conv))
-    step_sizes = jax.nn.softplus(step_pre + step_bias)
-    decay_rate = -jnp.exp(decay_log)
-    split_act = inner_act.reshape(seq_count, length, head_count, channels // head_count)
-    scanned = ssd_spans(
-        split_act, state_act[..., :state_size], state_act[..., state_size:], step_sizes, decay_rate
-    )
-    scanned = scanned + skip_scale[:, None] * split_act
-    return scanned.reshape(seq_count, length, channels) * jax.nn.silu(gating_pre)
+    rows, channels = inner_ref.shape
+
+    @pl.when(pl.program_id(0) == 0)
+    def _():
+        inner_tail[...] = jnp.zeros_like(inner_tail)
+        state_tail[...] = jnp.zeros_like(state_tail)
+        carry[...] = jnp.zeros_like(carry)
+
+    state_pre = state_ref[...]
+    state_conv = conv_taps(
+        jnp.concatenate([state_tail[...], state_pre], axis=0), state_taps_ref[...], rows
+    )
+    state_tail[...] = state_pre[rows - 8 :]
+    state_act = state_conv * sigmoid(state_conv)
+    in_vec = low(state_act[:, :N_STATE])
+    out_vec = low(state_act[:, N_STATE:])
+    in_turned = in_vec.T
+    _, steps, _, cumulative = step_terms(step_ref, head_ref)
+    turned = cumulative.T
+    grown = jnp.exp(cumulative)
+    tail_weight = jnp.exp(cumulative[rows - 1 : rows] - cumulative) * steps
+    decay = grown[rows - 1 : rows]
+    lower_mask = grid_of(rows, rows, 0) >= grid_of(rows, rows, 1)
+    scores = back_dot(out_vec, in_vec)
+    saved_ref[0] = low(carry[...])
+    squares = jnp.zeros((rows, 1), jnp.float32)
+    for pair in range(channels // LANES):
+        lanes = slice(pair * LANES, (pair + 1) * LANES)
+        inner_pre = inner_ref[:, lanes]
+        conv = conv_taps(
+            jnp.concatenate([inner_tail[:, lanes], inner_pre], axis=0),
+            inner_taps_ref[:, lanes],
+            rows,
+        )
+        inner_tail[:, lanes] = inner_pre[rows - 8 :]
+        act = conv * sigmoid(conv)
+        mixing = []
+        for head in (2 * pair, 2 * pair + 1):
+            gaps = cumulative[:, head : head + 1] - turned[head : head + 1, :]
+            mixing.append(low(scores * jnp.exp(jnp.where(lower_mask, gaps, -1e30))))
+        mixing = jnp.concatenate(mixing, axis=1)
+        scanned = dense(mixing, split_pair(low(act * pair_wide(steps, pair))))
+        old = carry[:, lanes]
+        scanned = scanned + dense(out_vec, low(old)) * pair_wide(grown, pair)
+        scanned = scanned + act * skip_ref[:, lanes]
+        carry[:, lanes] = old * pair_wide(decay, pair) + dense(
+            in_turned, low(act * pair_wide(tail_weight, pair))
+        )
+        gating = gating_ref[:, lanes]
+        gated = scanned * (gating * sigmoid(gating))
+        gated_ref[:, lanes] = gated
+        scanned_ref[:, lanes] = low(scanned)
+        squares = squares + jnp.sum(gated * gated, axis=1, keepdims=True)
+    squares_ref[...] = squares
+
+
+def mixer_backward_kernel(
+    grad_ref, stats_ref, scanned_ref, inner_ref, inner_before_ref, gating_ref, state_ref,
+    state_before_ref, step_ref, saved_ref, inner_taps_ref, state_taps_ref, head_ref, skip_ref, gain_ref,
+    rows_ref, inner_sums_ref, state_sums_ref, head_sums_ref,
+    inner_next, state_next, carry, turned_sums,
+):
+    rows, channels = inner_ref.shape
+    place = pl.program_id(0)
+    chunk = pl.num_programs(0) - 1 - place
+
+    @pl.when(place == 0)
+    def _():
+        inner_next[...] = jnp.zeros_like(inner_next)
+        state_next[...] = jnp.zeros_like(state_next)
+        carry[...] = jnp.zeros_like(carry)
+        inner_sums_ref[...] = jnp.zeros_like(inner_sums_ref)
+        state_sums_ref[...] = jnp.zeros_like(state_sums_ref)
+        head_sums_ref[...] = jnp.zeros_like(head_sums_ref)
+        turned_sums[...] = jnp.zeros_like(turned_sums)
+
+    first = chunk == 0
+    state_ext = jnp.concatenate(
+        [jnp.where(first, 0.0, state_before_ref[...]), state_ref[...]], axis=0
+    )
+    state_conv = conv_taps(state_ext, state_taps_ref[...], rows)
+    state_sigmoid = sigmoid(state_conv)
+    state_act = state_conv * state_sigmoid
+    in_vec = low(state_act[:, :N_STATE])
+    out_vec = low(state_act[:, N_STATE:])
+    out_turned = out_vec.T
+    shifted, steps, rate, cumulative = step_terms(step_ref, head_ref)
+    turned = cumulative.T
+    steps_turned = steps.T
+    grown = jnp.exp(cumulative)
+    fade = jnp.exp(cumulative[rows - 1 : rows] - cumulative)
+    tail_weight = fade * steps
+    decay = grown[rows - 1 : rows]
+    row_at, column_at = grid_of(rows, rows, 0), grid_of(rows, rows, 1)
+    lower_mask = row_at >= column_at
+    scores = back_dot(out_vec, in_vec)
+    inverse, slope = stats_ref[:, 0:1], stats_ref[:, 1:2]
+    lane_at = grid_of(rows, LANES, 1)
+    score_grad = jnp.zeros((rows, rows), jnp.float32)
+    out_grad = jnp.zeros((rows, N_STATE), jnp.float32)
+    in_grad = jnp.zeros((rows, N_STATE), jnp.float32)
+    row_sums = jnp.zeros((rows, LANES), jnp.float32)
+    read_sums = jnp.zeros((rows, LANES), jnp.float32)
+    write_sums = jnp.zeros((rows, LANES), jnp.float32)
+    state_sums = jnp.zeros((1, LANES), jnp.float32)
+    segment_row, segment_column = grid_of(LANES, LANES, 0), grid_of(LANES, LANES, 1)
+    first_lane = grid_of(1, LANES, 1)
+    for pair in range(channels // LANES):
+        lanes = slice(pair * LANES, (pair + 1) * LANES)
+        inner_ext = jnp.concatenate(
+            [jnp.where(first, 0.0, inner_before_ref[:, lanes]), inner_ref[:, lanes]], axis=0
+        )
+        taps = inner_taps_ref[:, lanes]
+        conv = conv_taps(inner_ext, taps, rows)
+        conv_sigmoid = sigmoid(conv)
+        act = conv * conv_sigmoid
+        act_low = low(act)
+        gating = gating_ref[:, lanes]
+        gate_sigmoid = sigmoid(gating)
+        gate_act = gating * gate_sigmoid
+        scanned = scanned_ref[:, lanes].astype(jnp.float32)
+        gated = scanned * gate_act
+        grad = grad_ref[:, lanes].astype(jnp.float32)
+        gated_grad = inverse * grad * gain_ref[:, lanes] - gated * slope
+        rows_ref[:, lanes] = low(
+            gated_grad * scanned * gate_sigmoid * (1.0 + gating * (1.0 - gate_sigmoid))
+        )
+        scan_grad = gated_grad * gate_act
+        gain_sum = jnp.sum(grad * gated * inverse, axis=0, keepdims=True)
+        skip_sum = jnp.sum(scan_grad * act, axis=0, keepdims=True)
+        blocks = split_pair(low(scan_grad))
+        mixing_grad = back_dot(blocks, act_low)
+        mixing = []
+        for side in range(2):
+            head = 2 * pair + side
+            gaps = cumulative[:, head : head + 1] - turned[head : head + 1, :]
+            within = jnp.exp(jnp.where(lower_mask, gaps, -1e30))
+            part = mixing_grad[side * rows : (side + 1) * rows] * within
+            step_row = steps_turned[head : head + 1, :]
+            score_grad = score_grad + part * step_row
+            product = part * scores
+            turned_sums[head : head + 1, :] = jnp.sum(product, axis=0, keepdims=True)
+            row_sum = jnp.sum(product * step_row, axis=1, keepdims=True)
+            row_sums = jnp.where(lane_at == head, row_sum, row_sums)
+            mixing.append(low(scores * within))
+        act_grad = row_dot(jnp.concatenate(mixing, axis=0), blocks) * pair_wide(steps, pair)
+        act_grad = act_grad + skip_ref[:, lanes] * scan_grad
+        saved = saved_ref[0, :, lanes]
+        later = carry[:, lanes]
+        later_low = low(later)
+        wide_tail = pair_wide(tail_weight, pair)
+        wide_grown = pair_wide(grown, pair)
+        through = dense(in_vec, later_low)
+        act_grad = act_grad + wide_tail * through
+        raised = low(scan_grad * wide_grown)
+        to_segments = (segment_column == 2 * pair + segment_row // P_SIZE).astype(jnp.bfloat16)
+
+        def segments(values):
+            high = low(values)
+            rest = low(values - high.astype(jnp.float32))
+            return dense(high, to_segments) + dense(rest, to_segments)
+
+        read_sums = read_sums + segments(scan_grad * wide_grown * dense(out_vec, saved))
+        write_sums = write_sums + segments(act * through)
+        overlap = jnp.sum(later * saved.astype(jnp.float32), axis=0, keepdims=True)
+        left = first_lane < P_SIZE
+        left_sum = jnp.sum(jnp.where(left, overlap, 0.0), axis=1, keepdims=True)
+        right_sum = jnp.sum(jnp.where(left, 0.0, overlap), axis=1, keepdims=True)
+        state_sums = jnp.where(first_lane == 2 * pair, left_sum, state_sums)
+        state_sums = jnp.where(first_lane == 2 * pair + 1, right_sum, state_sums)
+        carry[:, lanes] = later * pair_wide(decay, pair) + dense(out_turned, raised)
+        out_grad = out_grad + back_dot(raised, saved)
+        in_grad = in_grad + back_dot(low(act * wide_tail), later_low)
+        conv_grad = act_grad * conv_sigmoid * (1.0 + conv * (1.0 - conv_sigmoid))
+        ext = jnp.concatenate([conv_grad, inner_next[:, lanes]], axis=0)
+        inner_next[:, lanes] = conv_grad[:8]
+        pre_grad = ext[3 : 3 + rows] * taps[0:1]
+        for j in range(1, 4):
+            pre_grad = pre_grad + ext[3 - j : 3 - j + rows] * taps[j : j + 1]
+        rows_ref[:, channels + pair * LANES : channels + (pair + 1) * LANES] = low(pre_grad)
+        sums = [
+            jnp.sum(conv_grad * inner_ext[5 + j : 5 + j + rows], axis=0, keepdims=True)
+            for j in range(4)
+        ]
+        zero = jnp.zeros((2, LANES), jnp.float32)
+        inner_sums_ref[:, lanes] += jnp.concatenate(sums + [gain_sum, skip_sum, zero], axis=0)
+
+    score_low = low(score_grad)
+    out_grad = out_grad + dense(score_low, in_vec)
+    in_grad = in_grad + row_dot(score_low, out_vec)
+    column_sums = turned_sums[...].T
+    upper = (column_at >= row_at).astype(jnp.float32)
+    strict = (column_at < row_at).astype(jnp.float32)
+    log_grad = (
+        exact_dot(upper, row_sums - steps * column_sums + read_sums)
+        + exact_dot(strict, tail_weight * write_sums)
+        + decay * state_sums
+    )
+    step_grad = column_sums + log_grad * rate + fade * write_sums
+    step_pre_grad = step_grad * sigmoid(shifted)
+    bias_sum = jnp.sum(step_pre_grad, axis=0, keepdims=True)
+    decay_sum = jnp.sum(log_grad * steps, axis=0, keepdims=True) * rate
+    head_sums_ref[...] += jnp.concatenate(
+        [bias_sum, decay_sum, jnp.zeros((6, LANES), jnp.float32)], axis=0
+    )
+    state_grad = jnp.concatenate([in_grad, out_grad], axis=1)
+    state_grad = state_grad * state_sigmoid * (1.0 + state_conv * (1.0 - state_sigmoid))
+    taps = state_taps_ref[...]
+    ext = jnp.concatenate([state_grad, state_next[...]], axis=0)
+    state_next[...] = state_grad[:8]
+    pre_grad = ext[3 : 3 + rows] * taps[0:1]
+    for j in range(1, 4):
+        pre_grad = pre_grad + ext[3 - j : 3 - j + rows] * taps[j : j + 1]
+    width = state_grad.shape[1]
+    rows_ref[:, 2 * channels : 2 * channels + width] = low(pre_grad)
+    rows_ref[:, 2 * channels + width :] = low(step_pre_grad)
+    sums = [
+        jnp.sum(state_grad * state_ext[5 + j : 5 + j + rows], axis=0, keepdims=True)
+        for j in range(4)
+    ]
+    state_sums_ref[...] += jnp.concatenate(sums + [jnp.zeros((4, width), jnp.float32)], axis=0)
+
+
+def whole(shape):
+    return pl.BlockSpec(shape, lambda i: (0,) * len(shape))
+
+
+def mixer_sizes(projected, tables):
+    return projected.shape[0], tables[0].shape[1], tables[1].shape[1]
+
+
+def mixer_forward(projected, tables):
+    length, channels, state_width = mixer_sizes(projected, tables)
+    count = length // SPAN
+
+    def rows_of(width, place=0):
+        return pl.BlockSpec((SPAN, width), lambda i: (i, place))
+
+    state_place = 2 * channels // state_width
+    step_place = (2 * channels + state_width) // LANES
+
+    return pl.pallas_call(
+        mixer_forward_kernel,
+        grid=(count,),
+        in_specs=[
+            rows_of(channels, 1), rows_of(channels), rows_of(state_width, state_place), rows_of(LANES, step_place),
+            whole((8, channels)), whole((8, state_width)), whole((8, LANES)), whole((1, channels)),
+        ],
+        out_specs=[
+            rows_of(channels), rows_of(channels), rows_of(1),
+            pl.BlockSpec((1, N_STATE, channels), lambda i: (i, 0, 0)),
+        ],
+        out_shape=[
+            jax.ShapeDtypeStruct((length, channels), jnp.float32),
+            jax.ShapeDtypeStruct((length, channels), jnp.bfloat16),
+            jax.ShapeDtypeStruct((length, 1), jnp.float32),
+            jax.ShapeDtypeStruct((count, N_STATE, channels), jnp.bfloat16),
+        ],
+        scratch_shapes=[
+            pltpu.VMEM((8, channels), jnp.float32),
+            pltpu.VMEM((8, state_width), jnp.float32),
+            pltpu.VMEM((N_STATE, channels), jnp.float32),
+        ],
+        compiler_params=pltpu.CompilerParams(vmem_limit_bytes=40 * 2**20),
+        cost_estimate=pl.CostEstimate(
+            flops=6 * 10**9, bytes_accessed=14 * 2**20, transcendentals=4 * 10**6
+        ),
+        name="mixer_forward",
+    )(projected, projected, projected, projected, *tables)
+
+
+def mixer_backward(grad, stats, scanned, projected, saved, tables, gain_wide):
+    length, channels, state_width = mixer_sizes(projected, tables)
+    count = length // SPAN
+    total = 2 * channels + state_width + LANES
+
+    def rows_of(width, place=0):
+        return pl.BlockSpec((SPAN, width), lambda i: (count - 1 - i, place))
+
+    def before(width, place):
+        return pl.BlockSpec(
+            (8, width), lambda i: (jnp.maximum((count - 1 - i) * (SPAN // 8) - 1, 0), place)
+        )
+
+    state_place = 2 * channels // state_width
+    step_place = (2 * channels + state_width) // LANES
+
+    return pl.pallas_call(
+        mixer_backward_kernel,
+        grid=(count,),
+        in_specs=[
+            rows_of(channels), rows_of(2), rows_of(channels), rows_of(channels, 1), before(channels, 1),
+            rows_of(channels), rows_of(state_width, state_place), before(state_width, state_place),
+            rows_of(LANES, step_place),
+            pl.BlockSpec((1, N_STATE, channels), lambda i: (count - 1 - i, 0, 0)),
+            whole((8, channels)), whole((8, state_width)), whole((8, LANES)), whole((1, channels)),
+            whole((1, channels)),
+        ],
+        out_specs=[
+            rows_of(total), whole((8, channels)), whole((8, state_width)), whole((8, LANES)),
+        ],
+        out_shape=[
+            jax.ShapeDtypeStruct((length, total), jnp.bfloat16),
+            jax.ShapeDtypeStruct((8, channels), jnp.float32),
+            jax.ShapeDtypeStruct((8, state_width), jnp.float32),
+            jax.ShapeDtypeStruct((8, LANES), jnp.float32),
+        ],
+        scratch_shapes=[
+            pltpu.VMEM((8, channels), jnp.float32),
+            pltpu.VMEM((8, state_width), jnp.float32),
+            pltpu.VMEM((N_STATE, channels), jnp.float32),
+            pltpu.VMEM((LANES, SPAN), jnp.float32),
+        ],
+        compiler_params=pltpu.CompilerParams(vmem_limit_bytes=40 * 2**20),
+        cost_estimate=pl.CostEstimate(
+            flops=20 * 10**9, bytes_accessed=20 * 2**20, transcendentals=8 * 10**6
+        ),
+        name="mixer_backward",
+    )(
+        grad, stats, scanned, projected, projected, projected, projected, projected, projected, saved,
+        *tables, gain_wide,
+    )
 
 
 def on_device(
@@ -260,30 +576,26 @@
     first_vector = first_gain.astype(jnp.float32)
     normed_share = (tokens * first_inverse * first_vector).astype(jnp.bfloat16)
     normed = gather_rows(normed_share)
-    gating_pre = dense(normed, gating_weight)
-    inner_pre = dense(normed, inner_weight)
-    state_pre = dense(normed, state_weight)
-    step_pre = dense(normed, step_weight)
-    state_act, state_back = jax.vjp(
-        state_piece, as_sequences(state_pre), state_conv.astype(jnp.float32)
-    )
-    gated, mixer_back = jax.vjp(
-        mixer_piece,
-        as_sequences(inner_pre),
-        state_act,
-        as_sequences(step_pre),
-        as_sequences(gating_pre),
-        inner_conv.astype(jnp.float32),
-        step_bias,
-        decay_log,
-        skip_scale,
-    )
-    gated_squares = both(jnp.sum(gated * gated, axis=-1))
-    mixer_inverse = lax.rsqrt(gated_squares / mixer_width + epsilon)[..., None]
+    state_width = state_weight.shape[1]
+    mixer_weights = jnp.concatenate(
+        [gating_weight, inner_weight, state_weight, jnp.pad(step_weight, ((0, 0), (0, LANES - head_local)))],
+        axis=1,
+    )
+    projected = dense(normed, mixer_weights)
+
+    def eight_rows(values):
+        return jnp.pad(values.astype(jnp.float32), ((0, 8 - values.shape[0]), (0, 0)))
+
+    head_table = jnp.pad(
+        jnp.stack([step_bias, -jnp.exp(decay_log)]), ((0, 6), (0, LANES - head_local))
+    )
+    skip_wide = jnp.repeat(skip_scale, P_SIZE)[None]
+    tables = (eight_rows(inner_conv), eight_rows(state_conv), head_table, skip_wide)
+    gated, scanned, squares, saved_states = mixer_forward(projected, tables)
+    gated_squares = both(squares)
+    mixer_inverse = lax.rsqrt(gated_squares / mixer_width + epsilon)
     mixer_vector = mixer_gain.astype(jnp.float32)
-    mixer_normed = (
-        (gated * mixer_inverse * mixer_vector).astype(jnp.bfloat16).reshape(token_count, channels)
-    )
+    mixer_normed = (gated * mixer_inverse * mixer_vector).astype(jnp.bfloat16)
     mixer_part = dense(mixer_normed, mixer_proj)
     cosine, sine_table = rope_tables(seq_len, HD)
     query_pre = dense(normed, query_weight).reshape(seq_count, seq_len, query_heads, HD)
@@ -364,29 +676,15 @@
     )
     branch_grad = gather_rows(grad_residual.astype(jnp.bfloat16))
     grad_mixer_proj = row_dot(mixer_normed, branch_grad)
-    grad_mixer_normed = back_dot(branch_grad, mixer_proj).reshape(seq_count, seq_len, channels)
-    grad_mixer_gain = jnp.sum(grad_mixer_normed * gated * mixer_inverse, axis=(0, 1))
-    mixer_scaled = grad_mixer_normed * mixer_vector
-    cross_sum = both(jnp.sum(gated * mixer_scaled, axis=-1))
-    grad_gated = (
-        mixer_inverse * mixer_scaled
-        - gated * mixer_inverse**3 * (cross_sum / mixer_width)[..., None]
-    )
-    (
-        grad_inner_pre,
-        grad_state_act,
-        grad_step_pre,
-        grad_gating_pre,
-        grad_inner_conv,
-        grad_step_bias,
-        grad_decay_log,
-        grad_skip_scale,
-    ) = mixer_back(grad_gated)
-    grad_state_pre, grad_state_conv = state_back(grad_state_act)
-    gating_rows = to_rows(grad_gating_pre)
-    inner_rows = to_rows(grad_inner_pre)
-    state_rows = to_rows(grad_state_pre)
-    step_rows = to_rows(grad_step_pre)
+    grad_mixer_normed = back_dot(branch_grad, mixer_proj)
+    cross_sum = both(jnp.sum(gated * (grad_mixer_normed * mixer_vector), axis=-1, keepdims=True))
+    stats = jnp.concatenate(
+        [mixer_inverse, mixer_inverse**3 * (cross_sum / mixer_width)], axis=1
+    )
+    mixer_rows, inner_sums, state_sums, head_sums = mixer_backward(
+        grad_mixer_normed, stats, scanned, projected, saved_states, tables, mixer_vector[None]
+    )
+    state_rows = mixer_rows[:, 2 * channels : 2 * channels + state_width]
     grad_attended = (
         back_dot(branch_grad, attention_out)
         .astype(jnp.bfloat16)
@@ -434,12 +732,7 @@
     query_rows = to_rows(grad_query_pre)
     key_grad_rows = to_rows(grad_key_pre)
     value_grad_rows = to_rows(grad_values)
-    first_back = (
-        back_dot(gating_rows, gating_weight)
-        + back_dot(inner_rows, inner_weight)
-        + back_dot(step_rows, step_weight)
-        + back_dot(state_rows, state_weight)
-    )
+    first_back = back_dot(mixer_rows, mixer_weights)
     first_back = (
         first_back
         + back_dot(query_rows, query_weight)
@@ -450,30 +743,28 @@
     grad_first_gain = jnp.sum(grad_normed * tokens * first_inverse, axis=0)
     input_grad = grad_residual + norm_back(grad_normed, tokens, first_inverse, first_vector)
     model_width = normed.shape[1]
-    step_padded = jnp.pad(step_rows, ((0, 0), (0, 128 - head_local)))
-    input_rows = jnp.concatenate(
-        [gating_rows, inner_rows, query_rows, key_grad_rows, value_grad_rows, step_padded], axis=1
-    )
+    input_rows = jnp.concatenate([mixer_rows, query_rows, key_grad_rows, value_grad_rows], axis=1)
     grad_inputs = row_dot(normed, input_rows)
-    grad_state = row_dot(normed, state_rows)
     grad_gate, grad_up, grad_down = sum_over_dp([grad_gate, grad_up, grad_down], False)
     grad_mixer_proj, attention_output_gradient = sum_over_dp(
         [grad_mixer_proj, attention_output_gradient], True
     )
-    (grad_inputs,) = sum_over_dp([grad_inputs], False)
-    (grad_state,) = sum_over_dp([grad_state], True, over_tensor=True)
-    grad_gating, grad_inner, grad_query, grad_key, grad_value, grad_step = jnp.split(
+    state_columns = (2 * channels, 2 * channels + state_width)
+    (grad_inputs,) = sum_over_dp([grad_inputs], False, state_columns)
+    step_start = 2 * channels + state_width
+    query_start = step_start + LANES
+    key_start = query_start + query_heads * HD
+    value_start = key_start + kv_heads * HD
+    grad_gating, grad_inner, grad_state, grad_step, grad_query, grad_key, grad_value = jnp.split(
         grad_inputs,
-        [
-            channels,
-            2 * channels,
-            2 * channels + query_heads * HD,
-            2 * channels + (query_heads + kv_heads) * HD,
-            2 * channels + (query_heads + 2 * kv_heads) * HD,
-        ],
+        [channels, *state_columns, query_start, key_start, value_start],
         axis=1,
     )
-    state_width = state_weight.shape[1]
+    taps = inner_conv.shape[0]
+    grad_inner_conv, grad_mixer_gain = inner_sums[:taps], inner_sums[taps]
+    grad_skip_scale = jnp.sum(inner_sums[taps + 1].reshape(head_local, P_SIZE), axis=1)
+    grad_state_conv = state_sums[:taps]
+    grad_step_bias, grad_decay_log = head_sums[0, :head_local], head_sums[1, :head_local]
     shared_small = jnp.concatenate(
         [grad_state_conv.reshape(-1), grad_first_gain, grad_second_gain]
     )
@@ -488,7 +779,6 @@
     )
     small = sum_small(jnp.concatenate([both(shared_small), own_small]))
     shared_small, own_small = small[: shared_small.shape[0]], small[shared_small.shape[0] :]
-    taps = inner_conv.shape[0]
     grad_state_conv, grad_first_gain, grad_second_gain = jnp.split(
         shared_small, [taps * state_width, taps * state_width + model_width]
     )

time: 1160 us -> 689 us (0.59)
  local copies, waits for them, and re-layouts: 354 us -> 74.4 us
  matrix products: 249 us -> 94.3 us
  Pallas kernels: 0 us -> 52.1 us
  other arithmetic: 162 us -> 111 us
  waiting for transfers between devices: 339 us -> 302 us
    dynamic_update_slice x48 -> x0, local copies, waits for them, and re-layouts: 193 us -> none  [ssd_spans(): lax.scan(jax.checkpoint(one_block), initial, (to_blocks(inner), to_blocks...]
    dot_general x136 -> x0, matrix products: 141 us -> none  [the longest x24 50.8 us: one_block(): jnp.einsum('stuh,suhp->sthp', mixing, inner_block, precision=top_precision)]
    pallas_call x0 -> x2, Pallas kernels: none -> 52.1 us  [the longest x1 31.9 us: mixer_backward(): pl.pallas_call(mixer_backward_kernel, grid=(count,), in_specs=[rows_of(ch...]
    ppermute x36 -> x28, waiting for transfers between devices: 211 us -> 165 us  [flip(): return lax.ppermute(value, 'dp', [(i, i ^ bit) for i in range(size)])]
    squeeze x40 -> x1, local copies, waits for them, and re-layouts: 34.7 us -> 0.01 us  [on_device(): head_sums[1, :head_local]]
    reduce_sum x13 -> x1, other arithmetic: 18.1 us -> 0.12 us  [on_device(): jnp.sum(inner_sums[taps + 1].reshape(head_local, P_SIZE), axis=1)]
    dynamic_slice x8 -> x0, local copies, waits for them, and re-layouts: 17.9 us -> none  [ssd_spans(): lax.scan(jax.checkpoint(one_block), initial, (to_blocks(inner), to_blocks...]
    mul x4 -> x1, local copies, waits for them, and re-layouts: 14.9 us -> 0.2 us  [on_device(): jnp.einsum('skgql,sqkgd->slkd', grad_scores, query_block, preferred_eleme...]
  transfers between devices with their start and end apart: 48 -> 40, of which waited for: 27 -> 21; matrix products, arithmetic and copies ran while one was open for 43% -> 29% of each run, Pallas kernels for 0% -> 5%
where the time goes in v2:
time: 689 us; the launch traced here: 680 us
  waiting for transfers between devices  302 us (44%)
  other arithmetic  111 us (16%)
  matrix products  94.3 us (14%)
  local copies, waits for them, and re-layouts  74.4 us (11%)
  Pallas kernels  52.1 us (8%)
  starting transfers between devices  43.7 us (6%)
    ppermute x28, waiting for transfers between devices, flip(): return lax.ppermute(value, 'dp', [(i, i ^ bit) for i in range(size)])  165 us
    ppermute x12, waiting for transfers between devices, swap_tensor(): return lax.ppermute(value, 'tensor', [(0, 1), (1, 0)])  136 us
    pallas_call x1, Pallas kernels, mixer_backward(): pl.pallas_call(mixer_backward_kernel, grid=(count,), in_specs=[rows_of(ch...  31.9 us
    ppermute x28, starting transfers between devices, flip(): return lax.ppermute(value, 'dp', [(i, i ^ bit) for i in range(size)])  29.4 us
    dot_general x9, matrix products, back_dot(): lax.dot_general(left_side, right_side, (((1,), (1,)), ((), ())), preferre...  27.2 us
    dot_general x9, matrix products, dense(): return jnp.dot(left_side, right_side, preferred_element_type=jnp.float32)  22.9 us
    unnamed x234, local copies, waits for them, and re-layouts  22.7 us
    select_n x17, other arithmetic, in_order(): first = jnp.where(place == 0, own, other)  22 us
  transfers between devices with their start and end apart: 40, of which 21 were waited for; matrix products, arithmetic and copies ran while one was open for 29% of the time, Pallas kernels for 5%

profile of v2, /device:TPU:0, one launch (start us, length us, event | category | flops | bytes accessed | tf_op | source)
XLA Modules:
  0.0 679.9 jit_solution(9751224477642109134)
XLA Ops:
  12.9 19.7 %collective-permute-done = bf16[512,1024]{1,0:T(8,128)(2,1)} collective-permute-done((bf16[512,1024]{1,0:T(8,128)(2,1)}, bf16[512,1024]{1,0:T(8,128)(2,1)}, u32[]{:S(2)}, u32[]{:S(2)}) %collective-permute-start) | collective-permute-done | bytes 1048608 | tf_op jit(solution)/shard_map/ppermute | solution.py:69
  46.1 10.5 %fusion.90.inner_ref.gating_ref.state_ref.step_ref.inner_before_ref.state_before_ref = f32[1024,1920]{1,0:T(8,128)} fusion(bf16[1024,12]{1,0:T(8,128)(2,1)} %copy.226, bf16[1024,256]{1,0:T(8,128)(2,1)} %param.28, bf16[1024,768]{1,0:T(8,128)(2,1)} %param.27, bf16[1024,768]{1,0:T(8,128)(2,1)} %param.26, bf16[512,1024]{1,0:T(8,128)(2,1)} %copy-done.65, ...), kind=kOutput, calls=%fused_computation.277 | convolution fusion | flops 4050386944 | bytes 13656064 | tf_op jit(solution)/shard_map/dot_general | solution.py:23
  56.6 20.2 %mixer_forward.1 = (f32[1024,768]{1,0:T(8,128)S(1)}, bf16[1024,768]{1,0:T(8,128)(2,1)S(1)}, f32[1024,1]{1,0:T(8,128)S(1)}, bf16[8,128,768]{2,1,0:T(8,128)(2,1)S(1)}) custom-call(f32[1024,1920]{1,0:T(8,128)} %fusion.90.inner_ref.gating_ref.state_ref.step_ref.inner_before_ref.state_before_ref, ...), custom_call_target="tpu_custom_call" | custom-call | flops 6000000000 | bytes 14680064 | tf_op jit(solution)/shard_map/mixer_forward/pallas_call | solution.py:450
  104.6 24.4 %collective-permute-done.2 = bf16[512,1024]{1,0:T(8,128)(2,1)} collective-permute-done((bf16[512,1024]{1,0:T(8,128)(2,1)}, bf16[512,1024]{1,0:T(8,128)(2,1)}, u32[]{:S(2)}, u32[]{:S(2)}) %collective-permute-start.2) | collective-permute-done | bytes 1048608 | tf_op jit(solution)/shard_map/ppermute | solution.py:69
  136.0 14.3 %copy.196 = f32[1024,256]{1,0:T(8,128)} copy(f32[1024,256]{0,1:T(8,128)S(1)} %bitcast.219) | data formatting | bytes 2097152 | tf_op jit(solution)/shard_map/mul | solution.py:51
  153.1 18.4 %collective-permute-done.3 = bf16[512,1024]{1,0:T(8,128)(2,1)} collective-permute-done((bf16[512,1024]{1,0:T(8,128)(2,1)}, bf16[512,1024]{1,0:T(8,128)(2,1)}, u32[]{:S(2)}, u32[]{:S(2)}) %collective-permute-start.3) | collective-permute-done | bytes 1048608 | tf_op jit(solution)/shard_map/ppermute | solution.py:69
  178.0 6.0 multiply_convert_fusion
  200.9 32.3 %collective-permute-done.6 = bf16[512,1024]{1,0:T(8,128)(2,1)S(1)} collective-permute-done((bf16[512,1024]{1,0:T(8,128)(2,1)S(1)}, bf16[512,1024]{1,0:T(8,128)(2,1)S(1)}, u32[]{:S(2)}, u32[]{:S(2)}) %collective-permute-start.6) | collective-permute-done | bytes 1048608 | tf_op jit(solution)/shard_map/ppermute | solution.py:69
  246.2 13.9 %collective-permute-done.7 = bf16[512,1024]{1,0:T(8,128)(2,1)S(1)} collective-permute-done((bf16[512,1024]{1,0:T(8,128)(2,1)S(1)}, bf16[512,1024]{1,0:T(8,128)(2,1)S(1)}, u32[]{:S(2)}, u32[]{:S(2)}) %collective-permute-start.7) | collective-permute-done | bytes 1048608 | tf_op jit(solution)/shard_map/ppermute | solution.py:69
  323.7 31.9 %mixer_backward.1 = (bf16[1024,1920]{1,0:T(8,128)(2,1)S(1)}, f32[8,768]{1,0:T(8,128)S(1)}, f32[8,256]{1,0:T(8,128)S(1)}, f32[8,128]{1,0:T(8,128)S(1)}) custom-call(f32[1024,768]{1,0:T(8,128)S(1)} %copy-done.11, f32[1024,2]{1,0:T(8,128)S(1)} %pad_maximum_fusion.19.stats_ref, bf16[1024,768]{1,0:T(8,128)(2,1)S(1)} %copy-done.8, ...), custom_call_target="tpu_custom_call" | custom-call | flops 20000000000 | bytes 20971520 | tf_op jit(solution)/shard_map/mixer_backward/pallas_call | solution.py:496
  355.7 6.1 fusion.88
  361.7 7.8 %concatenate.182 = bf16[1024,2304]{1,0:T(8,128)(2,1)} concatenate(bf16[1024,1920]{1,0:T(8,128)(2,1)} %copy-done.2, bf16[1024,256]{1,0:T(8,128)(2,1)S(1)} %add_convert_fusion.9, bf16[1024,64]{1,0:T(8,128)(2,1)S(1)} %fusion.73, bf16[1024,64]{1,0:T(8,128)(2,1)S(1)} %bitcast.222), dimensions={1} | concatenate | bytes 9437184 | tf_op jit(solution)/shard_map/concatenate | solution.py:746
  369.6 8.0 %fusion.93 = bf16[1024,2304]{1,0:T(8,128)(2,1)S(1)} fusion(bf16[1024,2304]{1,0:T(8,128)(2,1)} %concatenate.182, bf16[512,1024]{1,0:T(8,128)(2,1)} %copy-done.65, bf16[512,1024]{1,0:T(8,128)(2,1)S(1)} %copy-done.64), kind=kOutput, calls=%fused_computation.279 | convolution fusion | flops 4836032512 | bytes 11534336 | tf_op jit(solution)/shard_map/dot_general | solution.py:27
  388.4 23.7 %collective-permute-done.9 = bf16[512,1024]{1,0:T(8,128)(2,1)} collective-permute-done((bf16[512,1024]{1,0:T(8,128)(2,1)}, bf16[512,1024]{1,0:T(8,128)(2,1)}, u32[]{:S(2)}, u32[]{:S(2)}) %collective-permute-start.9) | collective-permute-done | bytes 1048608 | tf_op jit(solution)/shard_map/ppermute | solution.py:69
  429.0 22.4 %collective-permute-done.21 = f32[6948]{0:T(1024)S(1)} collective-permute-done((f32[6948]{0:T(1024)S(1)}, f32[6948]{0:T(1024)S(1)}, u32[]{:S(2)}, u32[]{:S(2)}) %collective-permute-start.21) | collective-permute-done | bytes 27824 | tf_op jit(solution)/shard_map/ppermute | solution.py:99
  461.5 10.9 %collective-permute-done.26 = bf16[128,1024]{1,0:T(8,128)(2,1)S(1)} collective-permute-done((bf16[128,1024]{1,0:T(8,128)(2,1)S(1)}, bf16[128,1024]{1,0:T(8,128)(2,1)S(1)}, u32[]{:S(2)}, u32[]{:S(2)}) %collective-permute-start.26) | collective-permute-done | bytes 262176 | tf_op jit(solution)/shard_map/ppermute | solution.py:99
  472.4 12.2 %collective-permute-done.33 = bf16[768,1024]{1,0:T(8,128)(2,1)S(1)} collective-permute-done((bf16[768,1024]{1,0:T(8,128)(2,1)S(1)}, bf16[768,1024]{1,0:T(8,128)(2,1)S(1)}, u32[]{:S(2)}, u32[]{:S(2)}) %collective-permute-start.33) | collective-permute-done | bytes 1572896 | tf_op jit(solution)/shard_map/ppermute | solution.py:99
  491.4 19.5 %collective-permute-done.34 = bf16[384,1024]{1,0:T(8,128)(2,1)S(1)} collective-permute-done((bf16[384,1024]{1,0:T(8,128)(2,1)S(1)}, bf16[384,1024]{1,0:T(8,128)(2,1)S(1)}, u32[]{:S(2)}, u32[]{:S(2)}) %collective-permute-start.34) | collective-permute-done | bytes 786464 | tf_op jit(solution)/shard_map/ppermute | solution.py:99
  519.2 19.7 %collective-permute-done.35 = bf16[192,1024]{1,0:T(8,128)(2,1)S(1)} collective-permute-done((bf16[192,1024]{1,0:T(8,128)(2,1)S(1)}, bf16[192,1024]{1,0:T(8,128)(2,1)S(1)}, u32[]{:S(2)}, u32[]{:S(2)}) %collective-permute-start.35) | collective-permute-done | bytes 393248 | tf_op jit(solution)/shard_map/ppermute | solution.py:99
  539.1 14.6 %collective-permute-done.15 = bf16[64,2304]{1,0:T(8,128)(2,1)S(1)} collective-permute-done((bf16[64,2304]{1,0:T(8,128)(2,1)S(1)}, bf16[64,2304]{1,0:T(8,128)(2,1)S(1)}, u32[]{:S(2)}, u32[]{:S(2)}) %collective-permute-start.15) | collective-permute-done | bytes 294944 | tf_op jit(solution)/shard_map/ppermute | solution.py:99
  562.4 16.1 %collective-permute-done.16 = bf16[128,2304]{1,0:T(8,128)(2,1)S(1)} collective-permute-done((bf16[128,2304]{1,0:T(8,128)(2,1)S(1)}, bf16[128,2304]{1,0:T(8,128)(2,1)S(1)}, u32[]{:S(2)}, u32[]{:S(2)}) %collective-permute-start.16) | collective-permute-done | bytes 589856 | tf_op jit(solution)/shard_map/ppermute | solution.py:99
  587.8 7.7 %collective-permute-done.37 = bf16[384,1024]{1,0:T(8,128)(2,1)} collective-permute-done((bf16[384,1024]{1,0:T(8,128)(2,1)S(1)}, bf16[384,1024]{1,0:T(8,128)(2,1)}, u32[]{:S(2)}, u32[]{:S(2)}) %collective-permute-start.37) | collective-permute-done | bytes 786464 | tf_op jit(solution)/shard_map/ppermute | solution.py:99
  599.9 9.9 %collective-permute-done.17 = bf16[256,2304]{1,0:T(8,128)(2,1)} collective-permute-done((bf16[256,2304]{1,0:T(8,128)(2,1)}, bf16[256,2304]{1,0:T(8,128)(2,1)}, u32[]{:S(2)}, u32[]{:S(2)}) %collective-permute-start.17) | collective-permute-done | bytes 1179680 | tf_op jit(solution)/shard_map/ppermute | solution.py:99
  618.5 24.0 %collective-permute-done.38 = bf16[768,1024]{1,0:T(8,128)(2,1)} collective-permute-done((bf16[768,1024]{1,0:T(8,128)(2,1)}, bf16[768,1024]{1,0:T(8,128)(2,1)}, u32[]{:S(2)}, u32[]{:S(2)}) %collective-permute-start.38) | collective-permute-done | bytes 1572896 | tf_op jit(solution)/shard_map/ppermute | solution.py:99
  (480 shorter events, 283.2 us)
Async XLA Ops:
  6.2 26.4 %collective-permute-start = (bf16[512,1024]{1,0:T(8,128)(2,1)}, bf16[512,1024]{1,0:T(8,128)(2,1)}, u32[]{:S(2)}, u32[]{:S(2)}) collective-permute-start(bf16[512,1024]{1,0:T(8,128)(2,1)} %fusion.29), channel_id=1, source_target_pairs={{0,1},{1,0},{2,3},{3,2},{4,5},{5,4},{6,7},{7,6},{8,9},{9,8},{10,11... | collective-permute-start | bytes 3145736 | tf_op jit(solution)/shard_map/ppermute | solution.py:69
  102.5 26.4 %collective-permute-start.2 = (bf16[512,1024]{1,0:T(8,128)(2,1)}, bf16[512,1024]{1,0:T(8,128)(2,1)}, u32[]{:S(2)}, u32[]{:S(2)}) collective-permute-start(bf16[512,1024]{1,0:T(8,128)(2,1)} %dynamic-slice_convert_fusion.11), channel_id=1, source_target_pairs={{0,1},{1,0},{2,3},{3,2},{4,5},{5,4},{6,7},{7,6},{8,9},{9,8},{10,11... | collective-permute-start | bytes 3145736 | tf_op jit(solution)/shard_map/ppermute | solution.py:69
  103.6 47.9 %collective-permute-start.5 = (bf16[512,1024]{1,0:T(8,128)(2,1)}, bf16[512,1024]{1,0:T(8,128)(2,1)}, u32[]{:S(2)}, u32[]{:S(2)}) collective-permute-start(bf16[512,1024]{1,0:T(8,128)(2,1)} %param.25), channel_id=1, source_target_pairs={{0,1},{1,0},{2,3},{3,2},{4,5},{5,4},{6,7},{7,6},{8,9},{9,8},{10,11... | collective-permute-start | bytes 3145736 | tf_op jit(solution)/shard_map/ppermute | solution.py:69
  133.9 37.6 %collective-permute-start.3 = (bf16[512,1024]{1,0:T(8,128)(2,1)}, bf16[512,1024]{1,0:T(8,128)(2,1)}, u32[]{:S(2)}, u32[]{:S(2)}) collective-permute-start(bf16[512,1024]{1,0:T(8,128)(2,1)} %multiply_convert_fusion.4), channel_id=1, source_target_pairs={{0,1},{1,0},{2,3},{3,2},{4,5},{5,4},{6,7},{7,6},{8,9},{9,8},{10,11... | collective-permute-start | bytes 3145736 | tf_op jit(solution)/shard_map/ppermute | solution.py:69
  187.8 46.1 %collective-permute-start.4 = (bf16[512,1024]{1,0:T(8,128)(2,1)S(1)}, bf16[512,1024]{1,0:T(8,128)(2,1)S(1)}, u32[]{:S(2)}, u32[]{:S(2)}) collective-permute-start(bf16[512,1024]{1,0:T(8,128)(2,1)S(1)} %dynamic-slice_convert_fusion.10), channel_id=1, source_target_pairs={{0,1},{1,0},{2,3},{3,2},{4,5},{5,4},{6,7},{7,6},{8,9},{9,8},{10,11... | collective-permute-start | bytes 3145736 | tf_op jit(solution)/shard_map/ppermute | solution.py:69
  194.1 39.0 %collective-permute-start.6 = (bf16[512,1024]{1,0:T(8,128)(2,1)S(1)}, bf16[512,1024]{1,0:T(8,128)(2,1)S(1)}, u32[]{:S(2)}, u32[]{:S(2)}) collective-permute-start(bf16[512,1024]{1,0:T(8,128)(2,1)S(1)} %dynamic-slice_convert_fusion.9), channel_id=1, source_target_pairs={{0,1},{1,0},{2,3},{3,2},{4,5},{5,4},{6,7},{7,6},{8,9},{9,8},{10,11... | collective-permute-start | bytes 3145736 | tf_op jit(solution)/shard_map/ppermute | solution.py:69
  246.2 177.3 %collective-permute-start.32 = (bf16[1536,1024]{1,0:T(8,128)(2,1)}, bf16[1536,1024]{1,0:T(8,128)(2,1)}, u32[]{:S(2)}, u32[]{:S(2)}) collective-permute-start(bf16[1536,1024]{1,0:T(8,128)(2,1)} %pad_maximum_fusion.1), channel_id=1, source_target_pairs={{0,2},{2,0},{4,6},{6,4},{8,10},{10,8},{12,14},{14,12},{16,18},{18,... | collective-permute-start | bytes 9437192 | tf_op jit(solution)/shard_map/ppermute | solution.py:99
  301.4 85.3 %collective-permute-start.24 = (bf16[512,1024]{1,0:T(8,128)(2,1)}, bf16[512,1024]{1,0:T(8,128)(2,1)}, u32[]{:S(2)}, u32[]{:S(2)}) collective-permute-start(bf16[512,1024]{1,0:T(8,128)(2,1)} %pad_maximum_fusion.14), channel_id=1, source_target_pairs={{0,2},{2,0},{4,6},{6,4},{8,10},{10,8},{12,14},{14,12},{16,18},{18,... | collective-permute-start | bytes 3145736 | tf_op jit(solution)/shard_map/ppermute | solution.py:99
  381.1 37.6 %collective-permute-start.10 = (bf16[512,2304]{1,0:T(8,128)(2,1)}, bf16[512,2304]{1,0:T(8,128)(2,1)}, u32[]{:S(2)}, u32[]{:S(2)}) collective-permute-start(bf16[512,2304]{1,0:T(8,128)(2,1)} %dynamic-slice_convert_fusion), channel_id=1, source_target_pairs={{0,2},{2,0},{4,6},{6,4},{8,10},{10,8},{12,14},{14,12},{16,18},{18,... | collective-permute-start | bytes 7077896 | tf_op jit(solution)/shard_map/ppermute | solution.py:99
  415.3 42.5 %collective-permute-start.25 = (bf16[256,1024]{1,0:T(8,128)(2,1)S(1)}, bf16[256,1024]{1,0:T(8,128)(2,1)}, u32[]{:S(2)}, u32[]{:S(2)}) collective-permute-start(bf16[256,1024]{1,0:T(8,128)(2,1)S(1)} %constant_dynamic-slice_fusion.5), channel_id=1, source_target_pairs={{0,8},{2,10},{4,12},{6,14},{8,0},{10,2},{12,4},{14,6},{16,24},{18,... | collective-permute-start | bytes 1572872 | tf_op jit(solution)/shard_map/ppermute | solution.py:99
  421.9 37.6 %collective-permute-start.11 = (bf16[256,2304]{1,0:T(8,128)(2,1)S(1)}, bf16[256,2304]{1,0:T(8,128)(2,1)S(1)}, u32[]{:S(2)}, u32[]{:S(2)}) collective-permute-start(bf16[256,2304]{1,0:T(8,128)(2,1)S(1)} %constant_dynamic-slice_fusion.8), channel_id=1, source_target_pairs={{0,4},{2,6},{4,0},{6,2},{8,12},{10,14},{12,8},{14,10},{16,20},{18,... | collective-permute-start | bytes 3538952 | tf_op jit(solution)/shard_map/ppermute | solution.py:99
  428.2 56.4 %collective-permute-start.33 = (bf16[768,1024]{1,0:T(8,128)(2,1)S(1)}, bf16[768,1024]{1,0:T(8,128)(2,1)S(1)}, u32[]{:S(2)}, u32[]{:S(2)}) collective-permute-start(bf16[768,1024]{1,0:T(8,128)(2,1)S(1)} %constant_dynamic-slice_fusion.2), channel_id=1, source_target_pairs={{0,4},{2,6},{4,0},{6,2},{8,12},{10,14},{12,8},{14,10},{16,20},{18,... | collective-permute-start | bytes 4718600 | tf_op jit(solution)/shard_map/ppermute | solution.py:99
  455.3 130.1 %collective-permute-start.23 = (f32[6948]{0:T(1024)S(1)}, f32[6948]{0:T(1024)S(1)}, u32[]{:S(2)}, u32[]{:S(2)}) collective-permute-start(f32[6948]{0:T(1024)S(1)} %add.374), channel_id=1, source_target_pairs={{0,16},{2,18},{4,20},{6,22},{8,24},{10,26},{12,28},{14,30},{16,0},... | collective-permute-start | bytes 83384 | tf_op jit(solution)/shard_map/ppermute | solution.py:99
  459.9 27.2 %collective-permute-start.12 = (bf16[128,2304]{1,0:T(8,128)(2,1)S(1)}, bf16[128,2304]{1,0:T(8,128)(2,1)S(1)}, u32[]{:S(2)}, u32[]{:S(2)}) collective-permute-start(bf16[128,2304]{1,0:T(8,128)(2,1)S(1)} %constant_dynamic-slice_fusion.7), channel_id=1, source_target_pairs={{0,8},{2,10},{4,12},{6,14},{8,0},{10,2},{12,4},{14,6},{16,24},{18,... | collective-permute-start | bytes 1769480 | tf_op jit(solution)/shard_map/ppermute | solution.py:99
  489.9 27.7 %collective-permute-start.27 = (bf16[64,1024]{1,0:T(8,128)(2,1)S(1)}, bf16[64,1024]{1,0:T(8,128)(2,1)S(1)}, u32[]{:S(2)}, u32[]{:S(2)}) collective-permute-start(bf16[64,1024]{1,0:T(8,128)(2,1)S(1)} %constant_dynamic-slice_fusion.3), channel_id=1, source_target_pairs={{0,4},{2,6},{4,0},{6,2},{8,12},{10,14},{12,8},{14,10},{16,20},{18,... | collective-permute-start | bytes 393224 | tf_op jit(solution)/shard_map/ppermute | solution.py:99
  511.7 27.1 %collective-permute-start.35 = (bf16[192,1024]{1,0:T(8,128)(2,1)S(1)}, bf16[192,1024]{1,0:T(8,128)(2,1)S(1)}, u32[]{:S(2)}, u32[]{:S(2)}) collective-permute-start(bf16[192,1024]{1,0:T(8,128)(2,1)S(1)} %constant_dynamic-slice_fusion), channel_id=1, source_target_pairs={{0,16},{2,18},{4,20},{6,22},{8,24},{10,26},{12,28},{14,30},{16,0},... | collective-permute-start | bytes 1179656 | tf_op jit(solution)/shard_map/ppermute | solution.py:99
  515.4 38.3 %collective-permute-start.15 = (bf16[64,2304]{1,0:T(8,128)(2,1)S(1)}, bf16[64,2304]{1,0:T(8,128)(2,1)S(1)}, u32[]{:S(2)}, u32[]{:S(2)}) collective-permute-start(bf16[64,2304]{1,0:T(8,128)(2,1)S(1)} %pad_maximum_fusion.24), channel_id=1, source_target_pairs={{0,16},{2,18},{4,20},{6,22},{8,24},{10,26},{12,28},{14,30},{16,0},... | collective-permute-start | bytes 884744 | tf_op jit(solution)/shard_map/ppermute | solution.py:99
  517.6 36.3 %collective-permute-start.28 = (bf16[64,1024]{1,0:T(8,128)(2,1)S(1)}, bf16[64,1024]{1,0:T(8,128)(2,1)S(1)}, u32[]{:S(2)}, u32[]{:S(2)}) collective-permute-start(bf16[64,1024]{1,0:T(8,128)(2,1)S(1)} %add_convert_fusion.13), channel_id=1, source_target_pairs={{0,4},{2,6},{4,0},{6,2},{8,12},{10,14},{12,8},{14,10},{16,20},{18,... | collective-permute-start | bytes 393224 | tf_op jit(solution)/shard_map/ppermute | solution.py:99
  554.7 31.9 %collective-permute-start.29 = (bf16[128,1024]{1,0:T(8,128)(2,1)}, bf16[128,1024]{1,0:T(8,128)(2,1)}, u32[]{:S(2)}, u32[]{:S(2)}) collective-permute-start(bf16[128,1024]{1,0:T(8,128)(2,1)} %pad_maximum_fusion.25), channel_id=1, source_target_pairs={{0,16},{2,18},{4,20},{6,22},{8,24},{10,26},{12,28},{14,30},{16,0},... | collective-permute-start | bytes 786440 | tf_op jit(solution)/shard_map/ppermute | solution.py:99
  562.3 33.2 %collective-permute-start.37 = (bf16[384,1024]{1,0:T(8,128)(2,1)S(1)}, bf16[384,1024]{1,0:T(8,128)(2,1)}, u32[]{:S(2)}, u32[]{:S(2)}) collective-permute-start(bf16[384,1024]{1,0:T(8,128)(2,1)S(1)} %pad_maximum_fusion.15), channel_id=1, source_target_pairs={{0,8},{2,10},{4,12},{6,14},{8,0},{10,2},{12,4},{14,6},{16,24},{18,... | collective-permute-start | bytes 2359304 | tf_op jit(solution)/shard_map/ppermute | solution.py:99
  580.7 29.2 %collective-permute-start.17 = (bf16[256,2304]{1,0:T(8,128)(2,1)}, bf16[256,2304]{1,0:T(8,128)(2,1)}, u32[]{:S(2)}, u32[]{:S(2)}) collective-permute-start(bf16[256,2304]{1,0:T(8,128)(2,1)} %pad_maximum_fusion.11), channel_id=1, source_target_pairs={{0,4},{2,6},{4,0},{6,2},{8,12},{10,14},{12,8},{14,10},{16,20},{18,... | collective-permute-start | bytes 3538952 | tf_op jit(solution)/shard_map/ppermute | solution.py:99
  598.4 44.1 %collective-permute-start.38 = (bf16[768,1024]{1,0:T(8,128)(2,1)}, bf16[768,1024]{1,0:T(8,128)(2,1)}, u32[]{:S(2)}, u32[]{:S(2)}) collective-permute-start(bf16[768,1024]{1,0:T(8,128)(2,1)} %pad_maximum_fusion.7), channel_id=1, source_target_pairs={{0,4},{2,6},{4,0},{6,2},{8,12},{10,14},{12,8},{14,10},{16,20},{18,... | collective-permute-start | bytes 4718600 | tf_op jit(solution)/shard_map/ppermute | solution.py:99
  613.3 39.8 %collective-permute-start.18 = (bf16[512,2304]{1,0:T(8,128)(2,1)}, bf16[512,2304]{1,0:T(8,128)(2,1)}, u32[]{:S(2)}, u32[]{:S(2)}) collective-permute-start(bf16[512,2304]{1,0:T(8,128)(2,1)} %pad_maximum_fusion.2), channel_id=1, source_target_pairs={{0,2},{2,0},{4,6},{6,4},{8,10},{10,8},{12,14},{14,12},{16,18},{18,... | collective-permute-start | bytes 7077896 | tf_op jit(solution)/shard_map/ppermute | solution.py:99
  614.7 32.6 %collective-permute-start.31 = (bf16[512,1024]{1,0:T(8,128)(2,1)}, bf16[512,1024]{1,0:T(8,128)(2,1)}, u32[]{:S(2)}, u32[]{:S(2)}) collective-permute-start(bf16[512,1024]{1,0:T(8,128)(2,1)} %pad_maximum_fusion.10), channel_id=1, source_target_pairs={{0,2},{2,0},{4,6},{6,4},{8,10},{10,8},{12,14},{14,12},{16,18},{18,... | collective-permute-start | bytes 3145736 | tf_op jit(solution)/shard_map/ppermute | solution.py:99
  (130 other events, 1469.0 us)

commit v3 on v2

--- a/solution.py
+++ b/solution.py
@@ -9,7 +9,9 @@
 P_SIZE = 64
 HD = 64
 SPAN = 128
-ATT_BLOCK = 512
+QUERY_BLOCK = 256
+PIECES = 2
+SEG_MOST = 512
 N_STATE = 128
 LANES = 128
 
@@ -35,27 +37,16 @@
     )
 
 
-def rope_tables(length, head_size):
+def rope_tables(length):
     positions = jnp.arange(length, dtype=jnp.float32)
-    frequency = rope_base ** (-jnp.arange(0, head_size, 2, dtype=jnp.float32) / head_size)
+    frequency = rope_base ** (-jnp.arange(0, HD, 2, dtype=jnp.float32) / HD)
     angles = positions[:, None] * frequency[None, :]
-    angles = jnp.concatenate([angles, angles], axis=-1)
-    return (jnp.cos(angles)[:, None, :], jnp.sin(angles)[:, None, :])
-
-
-def rotate(value_tensor, cosine, sine_table):
-    half_size = value_tensor.shape[-1] // 2
-    turned = jnp.concatenate(
-        [-value_tensor[..., half_size:], value_tensor[..., :half_size]], axis=-1
-    )
-    return value_tensor * cosine + turned * sine_table
-
-
-def unrotate(grad_values, cosine, sine_table):
-    half_size = grad_values.shape[-1] // 2
-    product = grad_values * sine_table
-    turned = jnp.concatenate([product[..., half_size:], -product[..., :half_size]], axis=-1)
-    return grad_values * cosine + turned
+    copies = [1] * (2 * LANES // HD)
+    cosine, sine = jnp.cos(angles), jnp.sin(angles)
+    return (
+        jnp.concatenate([cosine for _ in copies], axis=1),
+        jnp.concatenate([sine for _ in copies], axis=1),
+    )
 
 
 def norm_back(grad_values, value_tensor, inverse, gain_vector):
@@ -88,10 +79,12 @@
     return lax.dynamic_slice_in_dim(value, place * half, half, 0)
 
 
-def scatter_rows(partial):
-    place = lax.axis_index("tensor")
-    got = swap_tensor(half_of(partial, 1 - place).astype(jnp.bfloat16))
-    return half_of(partial, place).astype(jnp.float32) + got.astype(jnp.float32)
+def rows_at(value, start, count):
+    return lax.dynamic_slice_in_dim(value, start, count, 0)
+
+
+def swapped_sum(own, other):
+    return own + swap_tensor(low(other)).astype(jnp.float32)
 
 
 def flip(value, bit):
@@ -105,39 +98,76 @@
     return bits[:1] + bits[2:] + bits[1:2] if far_first else bits
 
 
-def sum_over_dp(arrays, far_first, tensor_columns=None):
+def dp_stages(whole, split=None, tensor_columns=None):
     index = lax.axis_index("dp")
-    bits = bits_in_order(far_first)
-    places = [(index // bit) % 2 for bit in bits]
-
-    def joined(parts):
-        return parts[0] if len(parts) == 1 else jnp.concatenate(parts, axis=0)
-
-    current = None
-    for bit, place in zip(bits, places):
-        if current is None:
-            keep = joined([half_of(a, place).astype(jnp.bfloat16) for a in arrays])
-            send = joined([half_of(a, 1 - place).astype(jnp.bfloat16) for a in arrays])
-        else:
-            keep, send = half_of(current, place), half_of(current, 1 - place)
-        got = flip(send, bit)
-        current = (keep.astype(jnp.float32) + got.astype(jnp.float32)).astype(jnp.bfloat16)
+    near, far = bits_in_order(False), bits_in_order(True)
+    orders = [far] if split is None else [near, far]
+
+    def place_of(bit):
+        return (index // bit) % 2
+
+    def exchange(value, bit):
+        place = place_of(bit)
+        return half_of(value, place), flip(half_of(value, 1 - place), bit)
+
+    def total(keep, got):
+        return low(keep.astype(jnp.float32) + got.astype(jnp.float32))
+
+    keep, got = exchange(whole, near[0])
+    (got,) = yield [got]
+    share = total(keep, got)
+    parts = [share] if split is None else [share[:, :split], share[:, split:]]
+    for step in range(1, len(near)):
+        pairs = [exchange(part, order[step]) for part, order in zip(parts, orders)]
+        arrived = yield [got for _, got in pairs]
+        parts = [total(keep, got) for (keep, _), got in zip(pairs, arrived)]
     if tensor_columns is not None:
         start, stop = tensor_columns
-        part = current[:, start:stop]
-        part = (part.astype(jnp.float32) + swap_tensor(part).astype(jnp.float32)).astype(jnp.bfloat16)
-        current = jnp.concatenate([current[:, :start], part, current[:, stop:]], axis=1)
-    for bit, place in list(zip(bits, places))[:0:-1]:
-        current = in_order(place, current, flip(current, bit))
-    other = flip(current, bits[0])
-    results, start = [], 0
-    for a in arrays:
-        rows = a.shape[0] // 2
-        results.append(
-            in_order(places[0], current[start : start + rows], other[start : start + rows]).astype(jnp.float32)
-        )
-        start += rows
-    return results
+        part = parts[-1][:, start:stop]
+        (got,) = yield [swap_tensor(part)]
+        parts[-1] = jnp.concatenate(
+            [parts[-1][:, :start], total(part, got), parts[-1][:, stop:]], axis=1
+        )
+    for step in range(len(near) - 1, 0, -1):
+        got = [flip(part, order[step]) for part, order in zip(parts, orders)]
+        got = yield got
+        parts = [
+            in_order(place_of(order[step]), part, other)
+            for part, order, other in zip(parts, orders, got)
+        ]
+    share = parts[0] if split is None else jnp.concatenate(parts, axis=1)
+    (got,) = yield [flip(share, near[0])]
+    return in_order(place_of(near[0]), share, got)
+
+
+class DpSum:
+    def __init__(self, whole, split=None, tensor_columns=None):
+        self.stages = dp_stages(low(whole), split, tensor_columns)
+        self.arrived = next(self.stages)
+        self.result = None
+
+    def advance(self, *others):
+        if self.result is not None:
+            return []
+        arrived = self.arrived
+        flat = [one for several in others for one in several]
+        if flat:
+            arrived = list(lax.optimization_barrier((*arrived, *flat))[: len(arrived)])
+        try:
+            self.arrived = self.stages.send(arrived)
+        except StopIteration as end:
+            self.result = end.value
+        return arrived
+
+    def finish(self):
+        while self.result is None:
+            self.advance()
+        return self.result
+
+
+def after(value, *arrived):
+    flat = [one for several in arrived for one in several]
+    return lax.optimization_barrier((value, *flat))[0] if flat else value
 
 
 def sum_small(value):
@@ -429,6 +459,158 @@
     state_sums_ref[...] += jnp.concatenate(sums + [jnp.zeros((4, width), jnp.float32)], axis=0)
 
 
+def turn(values):
+    first = grid_of(values.shape[0], LANES, 1) % HD < HD // 2
+    ahead = pltpu.roll(values, LANES - HD // 2, 1)
+    behind = pltpu.roll(values, HD // 2, 1)
+    return first, ahead, behind
+
+
+def rotated(values, cosine, sine):
+    first, ahead, behind = turn(values)
+    return values * cosine + jnp.where(first, -ahead, behind) * sine
+
+
+def rotated_back(values, cosine, sine):
+    first, ahead, behind = turn(values * sine)
+    return values * cosine + jnp.where(first, ahead, -behind)
+
+
+def doubled(pair):
+    left = grid_of(pair.shape[0], LANES, 1) < HD
+    turned = pltpu.roll(pair, HD, 1)
+    return jnp.where(left, pair, turned), jnp.where(left, turned, pair)
+
+
+def attention_blocks(length):
+    for start in range(0, length, QUERY_BLOCK):
+        yield start, max(0, start - SEG_MOST), start + QUERY_BLOCK
+
+
+def allowed_keys(start, low_key, high_key, segment_column_ref, segment_row_ref):
+    shape = (QUERY_BLOCK, high_key - low_key)
+    query_at = start + lax.broadcasted_iota(jnp.int32, shape, 0)
+    key_at = low_key + lax.broadcasted_iota(jnp.int32, shape, 1)
+    same = segment_column_ref[start : start + QUERY_BLOCK] == segment_row_ref[:, low_key:high_key]
+    return (key_at <= query_at) & same
+
+
+def attention_forward_kernel(
+    projected_ref, segment_column_ref, segment_row_ref, cosine_ref, sine_ref, attended_ref, totals_ref,
+    keys_ref, values_ref,
+):
+    length, width = projected_ref.shape
+    query_width = width - LANES
+    key_part, value_part = doubled(projected_ref[:, query_width:])
+    keys_ref[...] = low(rotated(key_part, cosine_ref[...], sine_ref[...]))
+    values_ref[...] = low(value_part)
+    left = grid_of(QUERY_BLOCK, LANES, 1) < HD
+    for start, low_key, high_key in attention_blocks(length):
+        rows = slice(start, start + QUERY_BLOCK)
+        allowed = allowed_keys(start, low_key, high_key, segment_column_ref, segment_row_ref)
+        keys, values = keys_ref[low_key:high_key], values_ref[low_key:high_key]
+        for pair in range(query_width // LANES):
+            lanes = slice(pair * LANES, (pair + 1) * LANES)
+            queries = low(rotated(projected_ref[rows, lanes], cosine_ref[rows], sine_ref[rows]))
+            both_heads = split_pair(queries)
+            outputs = []
+            for side in range(2):
+                one = both_heads[side * QUERY_BLOCK : (side + 1) * QUERY_BLOCK]
+                scores = jnp.where(allowed, back_dot(one, keys) * HD**-0.5, -1e30)
+                row_max = jnp.max(scores, axis=1, keepdims=True)
+                weights = jnp.exp(scores - row_max)
+                row_total = jnp.sum(weights, axis=1, keepdims=True)
+                outputs.append(dense(low(weights * (1.0 / row_total)), values))
+                head = 2 * pair + side
+                totals_ref[rows, head : head + 1] = row_max + jnp.log(row_total)
+            attended_ref[rows, lanes] = low(jnp.where(left, outputs[0], outputs[1]))
+
+
+def attention_backward_kernel(
+    projected_ref, grad_ref, totals_ref, segment_column_ref, segment_row_ref, cosine_ref, sine_ref,
+    rows_ref, keys_ref, values_ref, keys_grad_ref, values_grad_ref,
+):
+    length, width = projected_ref.shape
+    query_width = width - LANES
+    key_part, value_part = doubled(projected_ref[:, query_width:])
+    keys_ref[...] = low(rotated(key_part, cosine_ref[...], sine_ref[...]))
+    values_ref[...] = low(value_part)
+    keys_grad_ref[...] = jnp.zeros_like(keys_grad_ref)
+    values_grad_ref[...] = jnp.zeros_like(values_grad_ref)
+    left = grid_of(QUERY_BLOCK, LANES, 1) < HD
+    for start, low_key, high_key in attention_blocks(length):
+        rows = slice(start, start + QUERY_BLOCK)
+        allowed = allowed_keys(start, low_key, high_key, segment_column_ref, segment_row_ref)
+        keys, values = keys_ref[low_key:high_key], values_ref[low_key:high_key]
+        for pair in range(query_width // LANES):
+            lanes = slice(pair * LANES, (pair + 1) * LANES)
+            queries = low(rotated(projected_ref[rows, lanes], cosine_ref[rows], sine_ref[rows]))
+            both_heads = split_pair(queries)
+            both_grads = split_pair(grad_ref[rows, lanes])
+            outputs = []
+            for side in range(2):
+                half = slice(side * QUERY_BLOCK, (side + 1) * QUERY_BLOCK)
+                one, grad = both_heads[half], both_grads[half]
+                head = 2 * pair + side
+                scores = jnp.where(allowed, back_dot(one, keys) * HD**-0.5, -1e30)
+                probs = jnp.exp(scores - totals_ref[rows, head : head + 1])
+                probs_grad = back_dot(grad, values)
+                delta = jnp.sum(probs * probs_grad, axis=1, keepdims=True)
+                scores_grad = low(probs * (probs_grad - delta))
+                outputs.append(dense(scores_grad, keys) * HD**-0.5)
+                keys_grad_ref[low_key:high_key] += row_dot(scores_grad, one) * HD**-0.5
+                values_grad_ref[low_key:high_key] += row_dot(low(probs), grad)
+            query_grad = jnp.where(left, outputs[0], outputs[1])
+            rows_ref[rows, lanes] = low(rotated_back(query_grad, cosine_ref[rows], sine_ref[rows]))
+    keys_grad = keys_grad_ref[...]
+    keys_grad = keys_grad + pltpu.roll(keys_grad, HD, 1)
+    keys_grad = rotated_back(keys_grad, cosine_ref[...], sine_ref[...])
+    values_grad = values_grad_ref[...]
+    values_grad = values_grad + pltpu.roll(values_grad, HD, 1)
+    left = grid_of(length, LANES, 1) < HD
+    rows_ref[:, query_width:] = low(jnp.where(left, keys_grad, values_grad))
+
+
+def attention_forward(projected, segment_column, segment_row, cosine, sine):
+    length, width = projected.shape
+    query_width = width - LANES
+    return pl.pallas_call(
+        attention_forward_kernel,
+        out_shape=[
+            jax.ShapeDtypeStruct((length, query_width), jnp.bfloat16),
+            jax.ShapeDtypeStruct((length, query_width // HD), jnp.float32),
+        ],
+        scratch_shapes=[
+            pltpu.VMEM((length, LANES), jnp.bfloat16),
+            pltpu.VMEM((length, LANES), jnp.bfloat16),
+        ],
+        compiler_params=pltpu.CompilerParams(vmem_limit_bytes=40 * 2**20),
+        cost_estimate=pl.CostEstimate(
+            flops=5 * 10**9, bytes_accessed=5 * 2**20, transcendentals=3 * 10**6
+        ),
+        name="attention_forward",
+    )(projected, segment_column, segment_row, cosine, sine)
+
+
+def attention_backward(projected, grad, totals, segment_column, segment_row, cosine, sine):
+    length, width = projected.shape
+    return pl.pallas_call(
+        attention_backward_kernel,
+        out_shape=jax.ShapeDtypeStruct((length, width), jnp.bfloat16),
+        scratch_shapes=[
+            pltpu.VMEM((length, LANES), jnp.bfloat16),
+            pltpu.VMEM((length, LANES), jnp.bfloat16),
+            pltpu.VMEM((length, LANES), jnp.float32),
+            pltpu.VMEM((length, LANES), jnp.float32),
+        ],
+        compiler_params=pltpu.CompilerParams(vmem_limit_bytes=40 * 2**20),
+        cost_estimate=pl.CostEstimate(
+            flops=10**10, bytes_accessed=6 * 2**20, transcendentals=3 * 10**6
+        ),
+        name="attention_backward",
+    )(projected, grad, totals, segment_column, segment_row, cosine, sine)
+
+
 def whole(shape):
     return pl.BlockSpec(shape, lambda i: (0,) * len(shape))
 
@@ -556,26 +738,22 @@
     down_projection_weight,
 ):
     seq_count, seq_len = segment_ids.shape
-    token_count = seq_count * seq_len
     channels = inner_weight.shape[1]
     head_local = step_weight.shape[1]
     query_heads = query_weight.shape[1] // HD
     kv_heads = key_weight.shape[1] // HD
-    group_width = query_heads // kv_heads
-    scale_factor = HD ** (-0.5)
     mixer_width = H_SSM * P_SIZE
-
-    def as_sequences(value_tensor):
-        return value_tensor.reshape(seq_count, seq_len, value_tensor.shape[-1])
-
-    def to_rows(value_tensor):
-        return value_tensor.reshape(token_count, -1).astype(jnp.bfloat16)
 
     tokens = block_input.astype(jnp.float32)
     first_inverse = lax.rsqrt(jnp.mean(tokens * tokens, axis=-1, keepdims=True) + epsilon)
     first_vector = first_gain.astype(jnp.float32)
     normed_share = (tokens * first_inverse * first_vector).astype(jnp.bfloat16)
     normed = gather_rows(normed_share)
+    model_width = normed.shape[1]
+    place = lax.axis_index("tensor")
+    share_rows = tokens.shape[0]
+    piece_rows = share_rows // PIECES
+    other_grad = swap_tensor(after(out_grad, [normed]))
     state_width = state_weight.shape[1]
     mixer_weights = jnp.concatenate(
         [gating_weight, inner_weight, state_weight, jnp.pad(step_weight, ((0, 0), (0, LANES - head_local)))],
@@ -596,168 +774,148 @@
     mixer_inverse = lax.rsqrt(gated_squares / mixer_width + epsilon)
     mixer_vector = mixer_gain.astype(jnp.float32)
     mixer_normed = (gated * mixer_inverse * mixer_vector).astype(jnp.bfloat16)
-    mixer_part = dense(mixer_normed, mixer_proj)
-    cosine, sine_table = rope_tables(seq_len, HD)
-    query_pre = dense(normed, query_weight).reshape(seq_count, seq_len, query_heads, HD)
-    key_pre = dense(normed, key_weight).reshape(seq_count, seq_len, kv_heads, HD)
-    value_pre = dense(normed, value_weight)
-    queries = (
-        rotate(query_pre, cosine, sine_table)
-        .astype(jnp.bfloat16)
-        .reshape(seq_count, seq_len, kv_heads, group_width, HD)
-    )
-    key_rows = rotate(key_pre, cosine, sine_table).astype(jnp.bfloat16)
-    value_rows = value_pre.astype(jnp.bfloat16).reshape(seq_count, seq_len, kv_heads, HD)
-    positions = jnp.arange(seq_len)
-
-    def block_scores(block_start):
-        query_block = queries[:, block_start : block_start + ATT_BLOCK]
-        seg_block = segment_ids[:, block_start : block_start + ATT_BLOCK]
-        row_index = block_start + jnp.arange(ATT_BLOCK)
-        allowed = (positions[None, :] <= row_index[:, None])[None] & (
-            seg_block[:, :, None] == segment_ids[:, None, :]
-        )
-        scores = (
-            jnp.einsum(
-                "sqkgd,slkd->skgql", query_block, key_rows, preferred_element_type=jnp.float32
-            )
-            * scale_factor
-        )
-        return (query_block, jnp.where(allowed[:, None, None], scores, -1e30))
-
-    block_starts = list(range(0, seq_len, ATT_BLOCK))
-    attended_blocks = []
-    log_totals = []
-    for block_start in block_starts:
-        query_block, scores = block_scores(block_start)
-        row_max = jnp.max(scores, axis=-1, keepdims=True)
-        exponents = jnp.exp(scores - row_max)
-        row_total = jnp.sum(exponents, axis=-1, keepdims=True)
-        attn_probs = (exponents / row_total).astype(jnp.bfloat16)
-        log_totals.append(row_max + jnp.log(row_total))
-        attended_blocks.append(
-            jnp.einsum(
-                "skgql,slkd->sqkgd", attn_probs, value_rows, preferred_element_type=jnp.float32
-            )
-        )
-    attended = (
-        jnp.concatenate(attended_blocks, axis=1)
-        .astype(jnp.bfloat16)
-        .reshape(token_count, query_heads * HD)
-    )
-    attn_part = dense(attended, attention_out)
-    branch_share = scatter_rows(mixer_part + attn_part)
-    residual = tokens + branch_share
-    second_inverse = lax.rsqrt(jnp.mean(residual * residual, axis=-1, keepdims=True) + epsilon)
+    cosine, sine = rope_tables(seq_len)
+    segments = (segment_ids.reshape(seq_len, 1), segment_ids.reshape(1, seq_len))
+    attention_weights = jnp.concatenate([query_weight, key_weight, value_weight], axis=1)
+    attention_inputs = dense(normed, attention_weights)
+    attended, log_totals = attention_forward(attention_inputs, *segments, cosine, sine)
     second_vector = second_gain.astype(jnp.float32)
-    normed_two_share = (residual * second_inverse * second_vector).astype(jnp.bfloat16)
-    normed_two = gather_rows(normed_two_share)
-    full_grad = gather_rows(out_grad)
-    gate_pre = dense(normed_two, gate_weight)
-    up_pre = dense(normed_two, up_weight)
-    gate_sigmoid = jax.nn.sigmoid(gate_pre)
-    gate_act = gate_pre * gate_sigmoid
-    hidden = (gate_act * up_pre).astype(jnp.bfloat16)
-    ffn_share = scatter_rows(dense(hidden, down_projection_weight))
-    block_output = (residual + ffn_share).astype(jnp.bfloat16)
-    grad_down = row_dot(hidden, full_grad)
-    grad_hidden = back_dot(full_grad, down_projection_weight)
-    grad_gate_pre = (
-        grad_hidden * up_pre * gate_sigmoid * (1.0 + gate_pre * (1.0 - gate_sigmoid))
-    ).astype(jnp.bfloat16)
-    grad_up_pre = (grad_hidden * gate_act).astype(jnp.bfloat16)
-    grad_gate = row_dot(normed_two, grad_gate_pre)
-    grad_up = row_dot(normed_two, grad_up_pre)
-    second_back = back_dot(grad_gate_pre, gate_weight) + back_dot(grad_up_pre, up_weight)
-    grad_normed_two = scatter_rows(second_back)
-    grad_second_gain = jnp.sum(grad_normed_two * residual * second_inverse, axis=0)
-    grad_residual = out_grad.astype(jnp.float32) + norm_back(
-        grad_normed_two, residual, second_inverse, second_vector
-    )
-    branch_grad = gather_rows(grad_residual.astype(jnp.bfloat16))
-    grad_mixer_proj = row_dot(mixer_normed, branch_grad)
+
+    def branch_rows(start):
+        return dense(rows_at(mixer_normed, start, piece_rows), mixer_proj) + dense(
+            rows_at(attended, start, piece_rows), attention_out
+        )
+
+    def piece_of(value, piece):
+        return value[piece * piece_rows : (piece + 1) * piece_rows]
+
+    residuals, second_inverses, kept, outputs, second_grads = [], [], [], [], []
+    branch_own, branch_other, first_residual_grads = [], [], []
+    for piece in range(PIECES):
+        offset = piece * piece_rows
+        other_part = branch_rows((1 - place) * share_rows + offset)
+        residual = piece_of(tokens, piece) + swapped_sum(
+            branch_rows(place * share_rows + offset), other_part
+        )
+        inverse = lax.rsqrt(jnp.mean(residual * residual, axis=-1, keepdims=True) + epsilon)
+        residuals.append(residual)
+        second_inverses.append(inverse)
+    normed_pieces = []
+    for residual, inverse in zip(residuals, second_inverses):
+        normed_own = low(residual * inverse * second_vector)
+        normed_pieces.append(jnp.concatenate([normed_own, swap_tensor(normed_own)], axis=0))
+    gradient_pieces = []
+    for piece in range(PIECES):
+        normed_two = normed_pieces[piece]
+        full_grad = jnp.concatenate([piece_of(out_grad, piece), piece_of(other_grad, piece)], axis=0)
+        gate_pre = dense(normed_two, gate_weight)
+        up_pre = dense(normed_two, up_weight)
+        gate_sigmoid = jax.nn.sigmoid(gate_pre)
+        gate_act = gate_pre * gate_sigmoid
+        hidden = low(gate_act * up_pre)
+        grad_hidden = back_dot(full_grad, down_projection_weight)
+        grad_gate_pre = low(
+            grad_hidden * up_pre * gate_sigmoid * (1.0 + gate_pre * (1.0 - gate_sigmoid))
+        )
+        grad_up_pre = low(grad_hidden * gate_act)
+        kept.append((hidden, full_grad, jnp.concatenate([grad_gate_pre, grad_up_pre], axis=1)))
+
+        def second_back(rows):
+            return back_dot(grad_gate_pre[rows], gate_weight) + back_dot(grad_up_pre[rows], up_weight)
+
+        own, other = slice(0, piece_rows), slice(piece_rows, 2 * piece_rows)
+        second_grads.append(swapped_sum(second_back(own), second_back(other)))
+        outputs.append((dense(hidden[own], down_projection_weight), dense(hidden[other], down_projection_weight)))
+    hidden_rows, full_rows, gate_up_rows = [jnp.concatenate(parts, axis=0) for parts in zip(*kept)]
+    normed_rows = jnp.concatenate(normed_pieces, axis=0)
+    ffn_grads = jnp.concatenate(
+        [low(row_dot(hidden_rows, full_rows)), low(row_dot(normed_rows, gate_up_rows))], axis=1
+    )
+    second_grads[-1] = after(second_grads[-1], [ffn_grads])
+    ffn_share = lax.psum_scatter(ffn_grads, "dp", scatter_dimension=0, tiled=True)
+    ffn_sums = lax.all_gather(ffn_share, "dp", axis=0, tiled=True)
+    for piece in range(PIECES):
+        residual, inverse = residuals[piece], second_inverses[piece]
+        grad_residual = piece_of(out_grad, piece).astype(jnp.float32) + norm_back(
+            second_grads[piece], residual, inverse, second_vector
+        )
+        first_residual_grads.append(grad_residual)
+        branch_own.append(low(grad_residual))
+        branch_other.append(swap_tensor(branch_own[-1]))
+    residual = jnp.concatenate(residuals, axis=0)
+    grad_normed_two = jnp.concatenate(second_grads, axis=0)
+    grad_second_gain = jnp.sum(
+        grad_normed_two * residual * jnp.concatenate(second_inverses, axis=0), axis=0
+    )
+    grad_residual = jnp.concatenate(first_residual_grads, axis=0)
+    branch_grad = in_order(
+        place, jnp.concatenate(branch_own, axis=0), jnp.concatenate(branch_other, axis=0)
+    )
+    block_output = jnp.concatenate(
+        [
+            low(residuals[piece] + swapped_sum(own, after(other, [branch_grad])))
+            for piece, (own, other) in enumerate(outputs)
+        ],
+        axis=0,
+    )
     grad_mixer_normed = back_dot(branch_grad, mixer_proj)
-    cross_sum = both(jnp.sum(gated * (grad_mixer_normed * mixer_vector), axis=-1, keepdims=True))
+    cross_part = jnp.sum(gated * (grad_mixer_normed * mixer_vector), axis=-1, keepdims=True)
+    cross_sum = both(cross_part)
+    grad_attended = low(back_dot(branch_grad, attention_out))
+    branch_sum = DpSum(
+        jnp.concatenate(
+            [low(row_dot(mixer_normed, branch_grad)), low(row_dot(attended, branch_grad))], axis=0
+        )
+    )
+    attention_rows = attention_backward(
+        attention_inputs, after(grad_attended, [cross_part]), log_totals, *segments, cosine, sine
+    )
     stats = jnp.concatenate(
         [mixer_inverse, mixer_inverse**3 * (cross_sum / mixer_width)], axis=1
     )
+    stats = after(stats, branch_sum.advance(), [attention_rows])
     mixer_rows, inner_sums, state_sums, head_sums = mixer_backward(
         grad_mixer_normed, stats, scanned, projected, saved_states, tables, mixer_vector[None]
     )
-    state_rows = mixer_rows[:, 2 * channels : 2 * channels + state_width]
-    grad_attended = (
-        back_dot(branch_grad, attention_out)
-        .astype(jnp.bfloat16)
-        .reshape(seq_count, seq_len, kv_heads, group_width, HD)
-    )
-    attention_output_gradient = row_dot(attended, branch_grad)
-    key_gradients = jnp.zeros((seq_count, seq_len, kv_heads, HD), jnp.float32)
-    grad_values = jnp.zeros((seq_count, seq_len, kv_heads, HD), jnp.float32)
-    query_grads = []
-    for block_index in range(len(block_starts)):
-        block_start = block_starts[block_index]
-        query_block, scores = block_scores(block_start)
-        attn_probs = jnp.exp(scores - log_totals[block_index])
-        grad_block = grad_attended[:, block_start : block_start + ATT_BLOCK]
-        grad_probs = jnp.einsum(
-            "sqkgd,slkd->skgql", grad_block, value_rows, preferred_element_type=jnp.float32
-        )
-        row_delta = jnp.sum(attn_probs * grad_probs, axis=-1, keepdims=True)
-        grad_scores = (attn_probs * (grad_probs - row_delta)).astype(jnp.bfloat16)
-        query_grads.append(
-            jnp.einsum(
-                "skgql,slkd->sqkgd", grad_scores, key_rows, preferred_element_type=jnp.float32
-            )
-            * scale_factor
-        )
-        key_gradients = (
-            key_gradients
-            + jnp.einsum(
-                "skgql,sqkgd->slkd", grad_scores, query_block, preferred_element_type=jnp.float32
-            )
-            * scale_factor
-        )
-        grad_values = grad_values + jnp.einsum(
-            "skgql,sqkgd->slkd",
-            attn_probs.astype(jnp.bfloat16),
-            grad_block,
-            preferred_element_type=jnp.float32,
-        )
-    grad_query_pre = unrotate(
-        jnp.concatenate(query_grads, axis=1).reshape(seq_count, seq_len, query_heads, HD),
-        cosine,
-        sine_table,
-    )
-    grad_key_pre = unrotate(key_gradients, cosine, sine_table)
-    query_rows = to_rows(grad_query_pre)
-    key_grad_rows = to_rows(grad_key_pre)
-    value_grad_rows = to_rows(grad_values)
-    first_back = back_dot(mixer_rows, mixer_weights)
-    first_back = (
-        first_back
-        + back_dot(query_rows, query_weight)
-        + back_dot(key_grad_rows, key_weight)
-        + back_dot(value_grad_rows, value_weight)
-    )
-    grad_normed = scatter_rows(first_back)
+    normed_again = after(normed, [mixer_rows])
+
+    def first_back(start):
+        return back_dot(rows_at(mixer_rows, start, share_rows), mixer_weights) + back_dot(
+            rows_at(attention_rows, start, share_rows), attention_weights
+        )
+
+    grad_inputs = jnp.concatenate(
+        [low(row_dot(normed_again, mixer_rows)), low(row_dot(normed_again, attention_rows))], axis=1
+    )
+    split = grad_inputs.shape[1] // (2 * LANES) * LANES
+    input_sum = DpSum(
+        grad_inputs, split, (2 * channels - split, 2 * channels + state_width - split)
+    )
+    mixer_rows = after(mixer_rows, [grad_inputs])
+    other_part = first_back((1 - place) * share_rows)
+    grad_normed = swapped_sum(first_back(place * share_rows), other_part)
     grad_first_gain = jnp.sum(grad_normed * tokens * first_inverse, axis=0)
     input_grad = grad_residual + norm_back(grad_normed, tokens, first_inverse, first_vector)
-    model_width = normed.shape[1]
-    input_rows = jnp.concatenate([mixer_rows, query_rows, key_grad_rows, value_grad_rows], axis=1)
-    grad_inputs = row_dot(normed, input_rows)
-    grad_gate, grad_up, grad_down = sum_over_dp([grad_gate, grad_up, grad_down], False)
-    grad_mixer_proj, attention_output_gradient = sum_over_dp(
-        [grad_mixer_proj, attention_output_gradient], True
-    )
-    state_columns = (2 * channels, 2 * channels + state_width)
-    (grad_inputs,) = sum_over_dp([grad_inputs], False, state_columns)
+    ffn_width = gate_weight.shape[1]
+    input_sum.advance(branch_sum.advance())
+    input_sum.advance(branch_sum.advance())
+    input_sum.advance(branch_sum.advance(), [ffn_sums])
+    grad_down, grad_gate, grad_up = jnp.split(
+        ffn_sums.astype(jnp.float32), [model_width, model_width + ffn_width], axis=1
+    )
+    input_sum.advance(branch_sum.advance())
+    input_sum.advance(branch_sum.advance())
+    input_sum.advance(branch_sum.advance(), [grad_down, grad_gate, grad_up])
+    input_sum.advance(branch_sum.advance())
+    branch_sums = branch_sum.finish().astype(jnp.float32)
+    grad_mixer_proj, attention_output_gradient = branch_sums[:channels], branch_sums[channels:]
+    input_sum.advance([grad_mixer_proj, attention_output_gradient])
     step_start = 2 * channels + state_width
     query_start = step_start + LANES
     key_start = query_start + query_heads * HD
-    value_start = key_start + kv_heads * HD
     grad_gating, grad_inner, grad_state, grad_step, grad_query, grad_key, grad_value = jnp.split(
-        grad_inputs,
-        [channels, *state_columns, query_start, key_start, value_start],
+        input_sum.finish().astype(jnp.float32),
+        [channels, 2 * channels, step_start, query_start, key_start, key_start + kv_heads * HD],
         axis=1,
     )
     taps = inner_conv.shape[0]

time: 689 us -> 512 us (0.74)
  waiting for transfers between devices: 302 us -> 194 us
  other arithmetic: 111 us -> 58.9 us
  local copies, waits for them, and re-layouts: 74.4 us -> 47.6 us
  Pallas kernels: 52.1 us -> 71.3 us
  matrix products: 94.3 us -> 77.3 us
  between operations: 2.61 us -> 16.3 us
    ppermute x28 -> x26, waiting for transfers between devices: 165 us -> 105 us  [flip(): return lax.ppermute(value, 'dp', [(i, i ^ bit) for i in range(size)])]
    ppermute x12 -> x17, waiting for transfers between devices: 136 us -> 82.6 us  [swap_tensor(): return lax.ppermute(value, 'tensor', [(0, 1), (1, 0)])]
    dot_general x12 -> x0, matrix products: 24.5 us -> none  [the longest x2 6.71 us: block_scores(): jnp.einsum('sqkgd,slkd->skgql', query_block, key_rows, preferred_element_...]
    pallas_call x0 -> x2, Pallas kernels: none -> 19.5 us  [the longest x1 11.6 us: attention_backward(): pl.pallas_call(attention_backward_kernel, out_shape=jax.ShapeDtypeStruct(...]
    mul x3 -> x0, local copies, waits for them, and re-layouts: 15.6 us -> none  [the longest x2 15.4 us: rotate(): return value_tensor * cosine + turned * sine_table]
    convert_element_type x23 -> x18, other arithmetic: 31.4 us -> 16.2 us  [the longest x14 7.41 us: low(): return v.astype(jnp.bfloat16)]
    ppermute x28 -> x26, starting transfers between devices: 29.4 us -> 15.8 us  [flip(): return lax.ppermute(value, 'dp', [(i, i ^ bit) for i in range(size)])]
    reduce_sum x5 -> x1, other arithmetic: 11.8 us -> 0.3 us  [on_device(): jnp.sum(grad_normed_two * residual * jnp.concatenate(second_inverses, axi...]
  transfers between devices with their start and end apart: 40 -> 45, of which waited for: 21 -> 27; matrix products, arithmetic and copies ran while one was open for 29% -> 22% of each run, Pallas kernels for 5% -> 14%
where the time goes in v3:
time: 512 us; the launch traced here: 504 us
  waiting for transfers between devices  194 us (38%)
  matrix products  77.3 us (15%)
  Pallas kernels  71.3 us (14%)
  other arithmetic  58.9 us (12%)
  local copies, waits for them, and re-layouts  47.6 us (9%)
  starting transfers between devices  38.1 us (7%)
  between operations  16.3 us (3%)
    ppermute x26, waiting for transfers between devices, flip(): return lax.ppermute(value, 'dp', [(i, i ^ bit) for i in range(size)])  105 us
    ppermute x17, waiting for transfers between devices, swap_tensor(): return lax.ppermute(value, 'tensor', [(0, 1), (1, 0)])  82.6 us
    pallas_call x1, Pallas kernels, mixer_backward(): pl.pallas_call(mixer_backward_kernel, grid=(count,), in_specs=[rows_of(ch...  31.6 us
    dot_general x18, matrix products, dense(): return jnp.dot(left_side, right_side, preferred_element_type=jnp.float32)  29.4 us
    dot_general x16, matrix products, back_dot(): lax.dot_general(left_side, right_side, (((1,), (1,)), ((), ())), preferre...  27.9 us
    ppermute x17, starting transfers between devices, swap_tensor(): return lax.ppermute(value, 'tensor', [(0, 1), (1, 0)])  21.8 us
    pallas_call x1, Pallas kernels, mixer_forward(): pl.pallas_call(mixer_forward_kernel, grid=(count,), in_specs=[rows_of(cha...  20.2 us
    dot_general x6, matrix products, row_dot(): lax.dot_general(left_side, right_side, (((0,), (0,)), ((), ())), preferre...  20.1 us
  transfers between devices with their start and end apart: 45, of which 27 were waited for; matrix products, arithmetic and copies ran while one was open for 22% of the time, Pallas kernels for 14%

profile of v3, /device:TPU:0, one launch (start us, length us, event | category | flops | bytes accessed | tf_op | source)
XLA Modules:
  0.0 504.0 jit_solution(2650366316034525293)
XLA Ops:
  27.2 12.1 %collective-permute-done = bf16[512,1024]{1,0:T(8,128)(2,1)} collective-permute-done((bf16[512,1024]{1,0:T(8,128)(2,1)}, bf16[512,1024]{1,0:T(8,128)(2,1)}, u32[]{:S(2)}, u32[]{:S(2)}) %collective-permute-start) | collective-permute-done | bytes 1048608 | tf_op jit(solution)/shard_map/ppermute | solution.py:60
  44.4 7.7 %fusion.143.inner_ref.gating_ref.state_ref.step_ref.inner_before_ref.state_before_ref = f32[1024,1920]{1,0:T(8,128)} fusion(bf16[512,1024]{1,0:T(8,128)(2,1)S(1)} %get-tuple-element.210, bf16[512,1024]{1,0:T(8,128)(2,1)S(1)} %get-tuple-element.209, bf16[1024,12]{1,0:T(8,128)(2,1)S(1)} %copy-done.80, bf16[1024,256]{1,0:T(8,128)(2,1)S(1)} %copy-done.98, ...), kind=kOutput, calls=%fused_computation.284 | convolution fusion | flops 4050386944 | bytes 13656064 | tf_op jit(solution)/shard_map/dot_general | solution.py:25
  52.1 20.2 %mixer_forward.1 = (f32[1024,768]{1,0:T(8,128)S(1)}, bf16[1024,768]{1,0:T(8,128)(2,1)S(1)}, f32[1024,1]{1,0:T(8,128)S(1)}, bf16[8,128,768]{2,1,0:T(8,128)(2,1)S(1)}) custom-call(f32[1024,1920]{1,0:T(8,128)} %fusion.143.inner_ref.gating_ref.state_ref.step_ref.inner_before_ref.state_before_ref, ...), custom_call_target="tpu_custom_call" | custom-call | flops 6000000000 | bytes 14680064 | tf_op jit(solution)/shard_map/mixer_forward/pallas_call | solution.py:632
  75.1 7.9 %attention_forward.1 = (bf16[1024,256]{1,0:T(8,128)(2,1)S(1)}, f32[1024,4]{1,0:T(8,128)S(1)}) custom-call(f32[1024,384]{1,0:T(8,128)S(1)} %fusion.142.projected_ref, s32[1024,1]{1,0:T(8,128)S(1)} %copy.90.segment_column_ref, s32[1,1024]{1,0:T(1,128)S(1)} %copy-done.8, f32[1024,128]{1,0:T(8,128)S(1)} %get-tuple-element.261.cosine_ref, ...), custom_call_target="tpu_custom_call" | custom-call | flops 5000000000 | bytes 5242880 | tf_op jit(solution)/shard_map/attention_forward/pallas_call | solution.py:577
  95.7 10.7 %collective-permute-done.6 = bf16[256,1024]{1,0:T(8,128)(2,1)S(1)} collective-permute-done((bf16[256,1024]{1,0:T(8,128)(2,1)S(1)}, bf16[256,1024]{1,0:T(8,128)(2,1)S(1)}, u32[]{:S(2)}, u32[]{:S(2)}) %collective-permute-start.6) | collective-permute-done | bytes 524320 | tf_op jit(solution)/shard_map/ppermute | solution.py:60
  107.0 7.6 %collective-permute-done.2 = bf16[256,1024]{1,0:T(8,128)(2,1)S(1)} collective-permute-done((bf16[256,1024]{1,0:T(8,128)(2,1)S(1)}, bf16[256,1024]{1,0:T(8,128)(2,1)S(1)}, u32[]{:S(2)}, u32[]{:S(2)}) %collective-permute-start.2) | collective-permute-done | bytes 524320 | tf_op jit(solution)/shard_map/ppermute | solution.py:60
  120.9 17.2 %collective-permute-done.7 = bf16[256,1024]{1,0:T(8,128)(2,1)S(1)} collective-permute-done((bf16[256,1024]{1,0:T(8,128)(2,1)S(1)}, bf16[256,1024]{1,0:T(8,128)(2,1)S(1)}, u32[]{:S(2)}, u32[]{:S(2)}) %collective-permute-start.7) | collective-permute-done | bytes 524320 | tf_op jit(solution)/shard_map/ppermute | solution.py:60
  157.2 7.5 %fusion.10 = bf16[1024,2048]{1,0:T(8,128)(2,1)S(1)} fusion(bf16[512,1024]{1,0:T(8,128)(2,1)} %get-tuple-element.200, bf16[512,1024]{1,0:T(8,128)(2,1)} %get-tuple-element.201, bf16[512,1024]{1,0:T(8,128)(2,1)} %get-tuple-element.199, bf16[512,1024]{1,0:T(8,128)(2,1)} %get-tuple-element.198, bf16[256,1024]{1,0:T(8,128)(2,1)} %copy-done.101, ...), kind=kOutput, calls=%fused_computation.19 | convolution fusion | flops 4322230272 | bytes 10485760 | tf_op jit(solution)/shard_map/dot_general | solution.py:29
  183.5 6.0 %collective-permute-done.8 = bf16[256,1024]{1,0:T(8,128)(2,1)S(1)} collective-permute-done((bf16[256,1024]{1,0:T(8,128)(2,1)S(1)}, bf16[256,1024]{1,0:T(8,128)(2,1)S(1)}, u32[]{:S(2)}, u32[]{:S(2)}) %collective-permute-start.8) | collective-permute-done | bytes 524320 | tf_op jit(solution)/shard_map/ppermute | solution.py:60
  190.3 5.5 %collective-permute-done.5 = bf16[256,1024]{1,0:T(8,128)(2,1)S(1)} collective-permute-done((bf16[256,1024]{1,0:T(8,128)(2,1)S(1)}, bf16[256,1024]{1,0:T(8,128)(2,1)S(1)}, u32[]{:S(2)}, u32[]{:S(2)}) %collective-permute-start.5) | collective-permute-done | bytes 524320 | tf_op jit(solution)/shard_map/ppermute | solution.py:60
  204.0 16.5 %collective-permute-done.9 = bf16[256,1024]{1,0:T(8,128)(2,1)S(1)} collective-permute-done((bf16[256,1024]{1,0:T(8,128)(2,1)S(1)}, bf16[256,1024]{1,0:T(8,128)(2,1)S(1)}, u32[]{:S(2)}, u32[]{:S(2)}) %collective-permute-start.9) | collective-permute-done | bytes 524320 | tf_op jit(solution)/shard_map/ppermute | solution.py:60
  236.7 11.6 %attention_backward.1 = bf16[1024,384]{1,0:T(8,128)(2,1)S(1)} custom-call(f32[1024,384]{1,0:T(8,128)S(1)} %copy-done.15, bf16[1024,256]{1,0:T(8,128)(2,1)S(1)} %convolution_convert_fusion.3.grad_ref, f32[1024,4]{1,0:T(8,128)S(1)} %copy-done.17, s32[1024,1]{1,0:T(8,128)S(1)} %copy.90.segment_column_ref, s32[1,1024]{1,0:T(1,128)S(1)} %copy-done.8, ...), custom_call_target="tpu_custom_call" | custom-call | flops 10000000000 | bytes 6291456 | tf_op jit(solution)/shard_map/attention_backward/pallas_call | solution.py:597
  248.3 6.4 %reduce-scatter.2.cloned.1.call-done = bf16[64,3072]{1,0:T(8,128)(2,1)} async-done(((bf16[1024,3072]{1,0:T(8,128)(2,1)}), bf16[64,3072]{1,0:T(8,128)(2,1)}) %reduce-scatter.2.cloned.1.call-update) | async-done | bytes 393232 | tf_op jit(solution)/shard_map/reduce_scatter | solution.py:835
  262.0 31.6 %mixer_backward.1 = (bf16[1024,1920]{1,0:T(8,128)(2,1)S(1)}, f32[8,768]{1,0:T(8,128)S(1)}, f32[8,256]{1,0:T(8,128)S(1)}, f32[8,128]{1,0:T(8,128)S(1)}) custom-call(f32[1024,768]{1,0:T(8,128)S(1)} %copy-done.13, f32[1024,2]{1,0:T(8,128)S(1)} %copy.98.stats_ref, bf16[1024,768]{1,0:T(8,128)(2,1)S(1)} %copy-done.10, ...), custom_call_target="tpu_custom_call" | custom-call | flops 20000000000 | bytes 20971520 | tf_op jit(solution)/shard_map/mixer_backward/pallas_call | solution.py:678
  303.8 20.9 %collective-permute-done.17 = bf16[256,1024]{1,0:T(8,128)(2,1)S(1)} collective-permute-done((bf16[256,1024]{1,0:T(8,128)(2,1)S(1)}, bf16[256,1024]{1,0:T(8,128)(2,1)S(1)}, u32[]{:S(2)}, u32[]{:S(2)}) %collective-permute-start.17) | collective-permute-done | bytes 524320 | tf_op jit(solution)/shard_map/ppermute | solution.py:92
  327.9 11.5 %collective-permute-done.20 = bf16[128,1024]{1,0:T(8,128)(2,1)S(1)} collective-permute-done((bf16[128,1024]{1,0:T(8,128)(2,1)S(1)}, bf16[128,1024]{1,0:T(8,128)(2,1)S(1)}, u32[]{:S(2)}, u32[]{:S(2)}) %collective-permute-start.20) | collective-permute-done | bytes 262176 | tf_op jit(solution)/shard_map/ppermute | solution.py:92
  352.3 10.6 %collective-permute-done.18 = bf16[256,1152]{1,0:T(8,128)(2,1)S(1)} collective-permute-done((bf16[256,1152]{1,0:T(8,128)(2,1)S(1)}, bf16[256,1152]{1,0:T(8,128)(2,1)S(1)}, u32[]{:S(2)}, u32[]{:S(2)}) %collective-permute-start.18) | collective-permute-done | bytes 589856 | tf_op jit(solution)/shard_map/ppermute | solution.py:92
  362.9 5.3 %collective-permute-done.19 = bf16[256,1152]{1,0:T(8,128)(2,1)S(1)} collective-permute-done((bf16[256,1152]{1,0:T(8,128)(2,1)S(1)}, bf16[256,1152]{1,0:T(8,128)(2,1)S(1)}, u32[]{:S(2)}, u32[]{:S(2)}) %collective-permute-start.19) | collective-permute-done | bytes 589856 | tf_op jit(solution)/shard_map/ppermute | solution.py:92
  372.8 9.2 %collective-permute-done.22 = bf16[128,1152]{1,0:T(8,128)(2,1)S(1)} collective-permute-done((bf16[128,1152]{1,0:T(8,128)(2,1)S(1)}, bf16[128,1152]{1,0:T(8,128)(2,1)S(1)}, u32[]{:S(2)}, u32[]{:S(2)}) %collective-permute-start.22) | collective-permute-done | bytes 294944 | tf_op jit(solution)/shard_map/ppermute | solution.py:92
  386.9 10.8 %collective-permute-done.31 = bf16[256,1024]{1,0:T(8,128)(2,1)} collective-permute-done((bf16[256,1024]{1,0:T(8,128)(2,1)}, bf16[256,1024]{1,0:T(8,128)(2,1)}, u32[]{:S(2)}, u32[]{:S(2)}) %collective-permute-start.31) | collective-permute-done | bytes 524320 | tf_op jit(solution)/shard_map/ppermute | solution.py:92
  413.6 11.2 %collective-permute-done.32 = bf16[128,1152]{1,0:T(8,128)(2,1)S(1)} collective-permute-done((bf16[128,1152]{1,0:T(8,128)(2,1)S(1)}, bf16[128,1152]{1,0:T(8,128)(2,1)S(1)}, u32[]{:S(2)}, u32[]{:S(2)}) %collective-permute-start.32) | collective-permute-done | bytes 294944 | tf_op jit(solution)/shard_map/ppermute | solution.py:92
  431.9 9.8 %collective-permute-done.35 = bf16[256,1152]{1,0:T(8,128)(2,1)S(1)} collective-permute-done((bf16[256,1152]{1,0:T(8,128)(2,1)S(1)}, bf16[256,1152]{1,0:T(8,128)(2,1)S(1)}, u32[]{:S(2)}, u32[]{:S(2)}) %collective-permute-start.35) | collective-permute-done | bytes 589856 | tf_op jit(solution)/shard_map/ppermute | solution.py:92
  470.9 11.3 %broadcast_select_fusion.1 = (bf16[512,2304]{1,0:T(8,128)(2,1)S(1)}, bf16[512,2304]{1,0:T(8,128)(2,1)S(1)}) fusion(bf16[512,2304]{1,0:T(8,128)(2,1)} %collective-permute-done.37, pred[]{:T(512)S(6)} %eq.60, bf16[256,1152]{1,0:T(8,128)(2,1)S(1)} %copy-done.48, bf16[256,1152]{1,0:T(8,128)(2,1)S(1)} %copy-done.46, bf16[256,1152]{1,0:T(8,128)(2,1)S(1)} %copy-done.44, ...), kind=kLoop, calls=%fused_computation.34 | loop fusion | flops 11796480 | bytes 9437185 | tf_op jit(solution)/shard_map/jit(_where)/select_n | solution.py:68
  490.9 6.1 %fusion.150 = (f32[1024,768]{1,0:T(8,128)}, f32[1024,768]{1,0:T(8,128)}) fusion(f32[1024,2304]{1,0:T(8,128)} %maximum_convert_fusion), kind=kLoop, calls=%fused_computation.288 | loop fusion | bytes 12582912 | tf_op jit(solution)/shard_map/split | solution.py:916
  (449 shorter events, 212.3 us)
Async XLA Ops:
  7.2 247.5 %reduce-scatter.2.cloned.1.call-start = ((), (), s32[]{:S(2)}) async-start(), calls=%async_computation.1 | async-start | bytes 6684672 | tf_op jit(solution)/shard_map/reduce_scatter | solution.py:835
  12.8 26.5 %collective-permute-start = (bf16[512,1024]{1,0:T(8,128)(2,1)}, bf16[512,1024]{1,0:T(8,128)(2,1)}, u32[]{:S(2)}, u32[]{:S(2)}) collective-permute-start(bf16[512,1024]{1,0:T(8,128)(2,1)} %fusion.17), channel_id=1, source_target_pairs={{0,1},{1,0},{2,3},{3,2},{4,5},{5,4},{6,7},{7,6},{8,9},{9,8},{10,11... | collective-permute-start | bytes 3145736 | tf_op jit(solution)/shard_map/ppermute | solution.py:60
  42.6 75.4 %collective-permute-start.4 = (bf16[512,1024]{1,0:T(8,128)(2,1)}, bf16[512,1024]{1,0:T(8,128)(2,1)}, u32[]{:S(2)}, u32[]{:S(2)}) collective-permute-start(bf16[512,1024]{1,0:T(8,128)(2,1)} %param.25), channel_id=1, source_target_pairs={{0,1},{1,0},{2,3},{3,2},{4,5},{5,4},{6,7},{7,6},{8,9},{9,8},{10,11... | collective-permute-start | bytes 3145736 | tf_op jit(solution)/shard_map/ppermute | solution.py:60
  93.9 20.7 %collective-permute-start.2 = (bf16[256,1024]{1,0:T(8,128)(2,1)S(1)}, bf16[256,1024]{1,0:T(8,128)(2,1)S(1)}, u32[]{:S(2)}, u32[]{:S(2)}) collective-permute-start(bf16[256,1024]{1,0:T(8,128)(2,1)S(1)} %fusion.57), channel_id=1, source_target_pairs={{0,1},{1,0},{2,3},{3,2},{4,5},{5,4},{6,7},{7,6},{8,9},{9,8},{10,11... | collective-permute-start | bytes 1572872 | tf_op jit(solution)/shard_map/ppermute | solution.py:60
  116.0 27.9 %collective-permute-start.3 = (bf16[256,1024]{1,0:T(8,128)(2,1)S(1)}, bf16[256,1024]{1,0:T(8,128)(2,1)S(1)}, u32[]{:S(2)}, u32[]{:S(2)}) collective-permute-start(bf16[256,1024]{1,0:T(8,128)(2,1)S(1)} %get-tuple-element.243), channel_id=1, source_target_pairs={{0,1},{1,0},{2,3},{3,2},{4,5},{5,4},{6,7},{7,6},{8,9},{9,8},{10,11... | collective-permute-start | bytes 1572872 | tf_op jit(solution)/shard_map/ppermute | solution.py:60
  117.6 20.5 %collective-permute-start.7 = (bf16[256,1024]{1,0:T(8,128)(2,1)S(1)}, bf16[256,1024]{1,0:T(8,128)(2,1)S(1)}, u32[]{:S(2)}, u32[]{:S(2)}) collective-permute-start(bf16[256,1024]{1,0:T(8,128)(2,1)S(1)} %get-tuple-element.244), channel_id=1, source_target_pairs={{0,1},{1,0},{2,3},{3,2},{4,5},{5,4},{6,7},{7,6},{8,9},{9,8},{10,11... | collective-permute-start | bytes 1572872 | tf_op jit(solution)/shard_map/ppermute | solution.py:60
  167.9 217.8 %all-gather.2.cloned.1.call-start = ((), (), s32[]{:S(2)}) async-start(), calls=%async_computation.2 | async-start | bytes 6684672 | tf_op jit(solution)/shard_map/all_gather | solution.py:836
  177.9 17.9 %collective-permute-start.5 = (bf16[256,1024]{1,0:T(8,128)(2,1)S(1)}, bf16[256,1024]{1,0:T(8,128)(2,1)S(1)}, u32[]{:S(2)}, u32[]{:S(2)}) collective-permute-start(bf16[256,1024]{1,0:T(8,128)(2,1)S(1)} %fusion.55), channel_id=1, source_target_pairs={{0,1},{1,0},{2,3},{3,2},{4,5},{5,4},{6,7},{7,6},{8,9},{9,8},{10,11... | collective-permute-start | bytes 1572872 | tf_op jit(solution)/shard_map/ppermute | solution.py:60
  200.1 20.4 %collective-permute-start.10 = (bf16[256,1024]{1,0:T(8,128)(2,1)S(1)}, bf16[256,1024]{1,0:T(8,128)(2,1)S(1)}, u32[]{:S(2)}, u32[]{:S(2)}) collective-permute-start(bf16[256,1024]{1,0:T(8,128)(2,1)S(1)} %get-tuple-element.182), channel_id=1, source_target_pairs={{0,1},{1,0},{2,3},{3,2},{4,5},{5,4},{6,7},{7,6},{8,9},{9,8},{10,11... | collective-permute-start | bytes 1572872 | tf_op jit(solution)/shard_map/ppermute | solution.py:60
  201.8 18.6 %collective-permute-start.9 = (bf16[256,1024]{1,0:T(8,128)(2,1)S(1)}, bf16[256,1024]{1,0:T(8,128)(2,1)S(1)}, u32[]{:S(2)}, u32[]{:S(2)}) collective-permute-start(bf16[256,1024]{1,0:T(8,128)(2,1)S(1)} %get-tuple-element.215), channel_id=1, source_target_pairs={{0,1},{1,0},{2,3},{3,2},{4,5},{5,4},{6,7},{7,6},{8,9},{9,8},{10,11... | collective-permute-start | bytes 1572872 | tf_op jit(solution)/shard_map/ppermute | solution.py:60
  226.6 28.2 %collective-permute-start.13 = (f32[1024,1]{0,1:T(1,128)S(1)}, f32[1024,1]{0,1:T(1,128)S(1)}, u32[]{:S(2)}, u32[]{:S(2)}) collective-permute-start(f32[1024,1]{0,1:T(1,128)S(1)} %bitcast.55), channel_id=1, source_target_pairs={{0,1},{1,0},{2,3},{3,2},{4,5},{5,4},{6,7},{7,6},{8,9},{9,8},{10,11... | collective-permute-start | bytes 12296 | tf_op jit(solution)/shard_map/ppermute | solution.py:60
  229.0 25.8 %collective-permute-start.11 = (bf16[256,1024]{1,0:T(8,128)(2,1)}, bf16[256,1024]{1,0:T(8,128)(2,1)S(1)}, u32[]{:S(2)}, u32[]{:S(2)}) collective-permute-start(bf16[256,1024]{1,0:T(8,128)(2,1)} %fusion.95), channel_id=1, source_target_pairs={{0,1},{1,0},{2,3},{3,2},{4,5},{5,4},{6,7},{7,6},{8,9},{9,8},{10,11... | collective-permute-start | bytes 1572872 | tf_op jit(solution)/shard_map/ppermute | solution.py:60
  229.4 223.0 %collective-permute-start.12 = (bf16[256,1024]{1,0:T(8,128)(2,1)}, bf16[256,1024]{1,0:T(8,128)(2,1)}, u32[]{:S(2)}, u32[]{:S(2)}) collective-permute-start(bf16[256,1024]{1,0:T(8,128)(2,1)} %fusion.73), channel_id=1, source_target_pairs={{0,1},{1,0},{2,3},{3,2},{4,5},{5,4},{6,7},{7,6},{8,9},{9,8},{10,11... | collective-permute-start | bytes 1572872 | tf_op jit(solution)/shard_map/ppermute | solution.py:60
  235.9 22.6 %collective-permute-start.14 = (bf16[512,1024]{1,0:T(8,128)(2,1)}, bf16[512,1024]{1,0:T(8,128)(2,1)}, u32[]{:S(2)}, u32[]{:S(2)}) collective-permute-start(bf16[512,1024]{1,0:T(8,128)(2,1)} %fusion.60), channel_id=1, source_target_pairs={{0,2},{2,0},{4,6},{6,4},{8,10},{10,8},{12,14},{14,12},{16,18},{18,... | collective-permute-start | bytes 3145736 | tf_op jit(solution)/shard_map/ppermute | solution.py:92
  296.2 28.5 %collective-permute-start.17 = (bf16[256,1024]{1,0:T(8,128)(2,1)S(1)}, bf16[256,1024]{1,0:T(8,128)(2,1)S(1)}, u32[]{:S(2)}, u32[]{:S(2)}) collective-permute-start(bf16[256,1024]{1,0:T(8,128)(2,1)S(1)} %constant_dynamic-slice_fusion.8), channel_id=1, source_target_pairs={{0,8},{2,10},{4,12},{6,14},{8,0},{10,2},{12,4},{14,6},{16,24},{18,... | collective-permute-start | bytes 1572872 | tf_op jit(solution)/shard_map/ppermute | solution.py:92
  303.8 42.9 %collective-permute-start.16 = (bf16[512,2304]{1,0:T(8,128)(2,1)S(1)}, bf16[512,2304]{1,0:T(8,128)(2,1)S(1)}, u32[]{:S(2)}, u32[]{:S(2)}) collective-permute-start(bf16[512,2304]{1,0:T(8,128)(2,1)S(1)} %fusion.14), channel_id=1, source_target_pairs={{0,2},{2,0},{4,6},{6,4},{8,10},{10,8},{12,14},{14,12},{16,18},{18,... | collective-permute-start | bytes 7077896 | tf_op jit(solution)/shard_map/ppermute | solution.py:92
  347.5 15.4 %collective-permute-start.18 = (bf16[256,1152]{1,0:T(8,128)(2,1)S(1)}, bf16[256,1152]{1,0:T(8,128)(2,1)S(1)}, u32[]{:S(2)}, u32[]{:S(2)}) collective-permute-start(bf16[256,1152]{1,0:T(8,128)(2,1)S(1)} %constant_dynamic-slice_fusion.7), channel_id=1, source_target_pairs={{0,4},{2,6},{4,0},{6,2},{8,12},{10,14},{12,8},{14,10},{16,20},{18,... | collective-permute-start | bytes 1769480 | tf_op jit(solution)/shard_map/ppermute | solution.py:92
  348.2 20.1 %collective-permute-start.19 = (bf16[256,1152]{1,0:T(8,128)(2,1)S(1)}, bf16[256,1152]{1,0:T(8,128)(2,1)S(1)}, u32[]{:S(2)}, u32[]{:S(2)}) collective-permute-start(bf16[256,1152]{1,0:T(8,128)(2,1)S(1)} %constant_dynamic-slice_fusion.6), channel_id=1, source_target_pairs={{0,8},{2,10},{4,12},{6,14},{8,0},{10,2},{12,4},{14,6},{16,24},{18,... | collective-permute-start | bytes 1769480 | tf_op jit(solution)/shard_map/ppermute | solution.py:92
  351.6 20.2 %collective-permute-start.29 = (bf16[128,1024]{1,0:T(8,128)(2,1)S(1)}, bf16[128,1024]{1,0:T(8,128)(2,1)S(1)}, u32[]{:S(2)}, u32[]{:S(2)}) collective-permute-start(bf16[128,1024]{1,0:T(8,128)(2,1)S(1)} %pad_maximum_fusion.21), channel_id=1, source_target_pairs={{0,16},{2,18},{4,20},{6,22},{8,24},{10,26},{12,28},{14,30},{16,0},... | collective-permute-start | bytes 786440 | tf_op jit(solution)/shard_map/ppermute | solution.py:92
  369.6 16.2 %collective-permute-start.21 = (bf16[128,1152]{1,0:T(8,128)(2,1)S(1)}, bf16[128,1152]{1,0:T(8,128)(2,1)S(1)}, u32[]{:S(2)}, u32[]{:S(2)}) collective-permute-start(bf16[128,1152]{1,0:T(8,128)(2,1)S(1)} %constant_dynamic-slice_fusion.4), channel_id=1, source_target_pairs={{0,8},{2,10},{4,12},{6,14},{8,0},{10,2},{12,4},{14,6},{16,24},{18,... | collective-permute-start | bytes 884744 | tf_op jit(solution)/shard_map/ppermute | solution.py:92
  372.7 25.0 %collective-permute-start.31 = (bf16[256,1024]{1,0:T(8,128)(2,1)}, bf16[256,1024]{1,0:T(8,128)(2,1)}, u32[]{:S(2)}, u32[]{:S(2)}) collective-permute-start(bf16[256,1024]{1,0:T(8,128)(2,1)} %pad_maximum_fusion.18), channel_id=1, source_target_pairs={{0,8},{2,10},{4,12},{6,14},{8,0},{10,2},{12,4},{14,6},{16,24},{18,... | collective-permute-start | bytes 1572872 | tf_op jit(solution)/shard_map/ppermute | solution.py:92
  410.7 16.3 %collective-permute-start.33 = (bf16[128,1152]{1,0:T(8,128)(2,1)S(1)}, bf16[128,1152]{1,0:T(8,128)(2,1)S(1)}, u32[]{:S(2)}, u32[]{:S(2)}) collective-permute-start(bf16[128,1152]{1,0:T(8,128)(2,1)S(1)} %pad_maximum_fusion.20), channel_id=1, source_target_pairs={{0,16},{2,18},{4,20},{6,22},{8,24},{10,26},{12,28},{14,30},{16,0},... | collective-permute-start | bytes 884744 | tf_op jit(solution)/shard_map/ppermute | solution.py:92
  413.0 31.6 %collective-permute-start.15 = (bf16[512,1024]{1,0:T(8,128)(2,1)S(1)}, bf16[512,1024]{1,0:T(8,128)(2,1)S(1)}, u32[]{:S(2)}, u32[]{:S(2)}) collective-permute-start(bf16[512,1024]{1,0:T(8,128)(2,1)S(1)} %copy-done.60), channel_id=1, source_target_pairs={{0,1},{1,0},{2,3},{3,2},{4,5},{5,4},{6,7},{7,6},{8,9},{9,8},{10,11... | collective-permute-start | bytes 3145736 | tf_op jit(solution)/shard_map/ppermute | solution.py:60
  444.6 26.3 %collective-permute-start.37 = (bf16[512,2304]{1,0:T(8,128)(2,1)}, bf16[512,2304]{1,0:T(8,128)(2,1)}, u32[]{:S(2)}, u32[]{:S(2)}) collective-permute-start(bf16[512,2304]{1,0:T(8,128)(2,1)} %maximum_maximum_fusion), channel_id=1, source_target_pairs={{0,2},{2,0},{4,6},{6,4},{8,10},{10,8},{12,14},{14,12},{16,18},{18,... | collective-permute-start | bytes 7077896 | tf_op jit(solution)/shard_map/ppermute | solution.py:92
  (125 other events, 1207.5 us)
Sparse Core Ops, SparseCore 0:
  168.1 86.6 reduce-scatter.1
  257.3 65.3 all-gather.1

commit v4 on v3

--- a/solution.py
+++ b/solution.py
@@ -1,3 +1,5 @@
+import functools
+
 import jax
 import jax.numpy as jnp
 from jax import lax
@@ -137,7 +139,34 @@
         ]
     share = parts[0] if split is None else jnp.concatenate(parts, axis=1)
     (got,) = yield [flip(share, near[0])]
+    if split is not None:
+        return share, got, place_of(near[0])
     return in_order(place_of(near[0]), share, got)
+
+
+def unpack_kernel(starts, place_ref, own_ref, other_ref, *output_refs):
+    half = pl.program_id(0) // (pl.num_programs(0) // 2)
+    values = jnp.where(half == place_ref[0], own_ref[...], other_ref[...]).astype(jnp.float32)
+    for start, output_ref in zip(starts, output_refs):
+        output_ref[...] = values[:, start : start + output_ref.shape[1]]
+
+
+def unpack(own, other, place, columns):
+    half_rows, width = own.shape
+    steps = half_rows // SPAN
+    rows = pl.BlockSpec((SPAN, width), lambda i: (i % steps, 0))
+    return pl.pallas_call(
+        functools.partial(unpack_kernel, [start for start, _ in columns]),
+        grid=(2 * steps,),
+        in_specs=[pl.BlockSpec(memory_space=pltpu.SMEM), rows, rows],
+        out_specs=[pl.BlockSpec((SPAN, size), lambda i: (i, 0)) for _, size in columns],
+        out_shape=[jax.ShapeDtypeStruct((2 * half_rows, size), jnp.float32) for _, size in columns],
+        compiler_params=pltpu.CompilerParams(vmem_limit_bytes=40 * 2**20),
+        cost_estimate=pl.CostEstimate(
+            flops=0, bytes_accessed=16 * half_rows * width, transcendentals=0
+        ),
+        name="unpack",
+    )(place.reshape(1).astype(jnp.int32), own, other)
 
 
 class DpSum:
@@ -170,15 +199,6 @@
     return lax.optimization_barrier((value, *flat))[0] if flat else value
 
 
-def sum_small(value):
-    size = lax.axis_size("dp")
-    bit = 1
-    while bit < size:
-        value = value + flip(value, bit)
-        bit *= 2
-    return value
-
-
 def sigmoid(v):
     return 1.0 / (1.0 + jnp.exp(-v))
 
@@ -234,7 +254,7 @@
 def mixer_forward_kernel(
     inner_ref, gating_ref, state_ref, step_ref, inner_taps_ref, state_taps_ref, head_ref, skip_ref,
     gated_ref, scanned_ref, squares_ref, saved_ref,
-    inner_tail, state_tail, carry,
+    inner_tail, state_tail, carry, written,
 ):
     rows, channels = inner_ref.shape
 
@@ -260,7 +280,9 @@
     decay = grown[rows - 1 : rows]
     lower_mask = grid_of(rows, rows, 0) >= grid_of(rows, rows, 1)
     scores = back_dot(out_vec, in_vec)
-    saved_ref[0] = low(carry[...])
+    saved = low(carry[...])
+    saved_ref[0] = saved
+    from_state = dense(out_vec, saved)
     squares = jnp.zeros((rows, 1), jnp.float32)
     for pair in range(channels // LANES):
         lanes = slice(pair * LANES, (pair + 1) * LANES)
@@ -278,18 +300,19 @@
             mixing.append(low(scores * jnp.exp(jnp.where(lower_mask, gaps, -1e30))))
         mixing = jnp.concatenate(mixing, axis=1)
         scanned = dense(mixing, split_pair(low(act * pair_wide(steps, pair))))
-        old = carry[:, lanes]
-        scanned = scanned + dense(out_vec, low(old)) * pair_wide(grown, pair)
+        scanned = scanned + from_state[:, lanes] * pair_wide(grown, pair)
         scanned = scanned + act * skip_ref[:, lanes]
-        carry[:, lanes] = old * pair_wide(decay, pair) + dense(
-            in_turned, low(act * pair_wide(tail_weight, pair))
-        )
+        written[:, lanes] = low(act * pair_wide(tail_weight, pair))
         gating = gating_ref[:, lanes]
         gated = scanned * (gating * sigmoid(gating))
         gated_ref[:, lanes] = gated
         scanned_ref[:, lanes] = low(scanned)
         squares = squares + jnp.sum(gated * gated, axis=1, keepdims=True)
     squares_ref[...] = squares
+    update = dense(in_turned, written[...])
+    for pair in range(channels // LANES):
+        lanes = slice(pair * LANES, (pair + 1) * LANES)
+        carry[:, lanes] = carry[:, lanes] * pair_wide(decay, pair) + update[:, lanes]
 
 
 def mixer_backward_kernel(
@@ -650,6 +673,7 @@
             pltpu.VMEM((8, channels), jnp.float32),
             pltpu.VMEM((8, state_width), jnp.float32),
             pltpu.VMEM((N_STATE, channels), jnp.float32),
+            pltpu.VMEM((SPAN, channels), jnp.bfloat16),
         ],
         compiler_params=pltpu.CompilerParams(vmem_limit_bytes=40 * 2**20),
         cost_estimate=pl.CostEstimate(
@@ -824,14 +848,16 @@
             return back_dot(grad_gate_pre[rows], gate_weight) + back_dot(grad_up_pre[rows], up_weight)
 
         own, other = slice(0, piece_rows), slice(piece_rows, 2 * piece_rows)
-        second_grads.append(swapped_sum(second_back(own), second_back(other)))
+        second_other = second_back(other)
+        second_own = second_back(own)
+        second_grads.append(swapped_sum(second_own, second_other))
         outputs.append((dense(hidden[own], down_projection_weight), dense(hidden[other], down_projection_weight)))
+    kept = [tuple(after(one, [second_own, second_other]) for one in pieces) for pieces in kept]
     hidden_rows, full_rows, gate_up_rows = [jnp.concatenate(parts, axis=0) for parts in zip(*kept)]
     normed_rows = jnp.concatenate(normed_pieces, axis=0)
     ffn_grads = jnp.concatenate(
         [low(row_dot(hidden_rows, full_rows)), low(row_dot(normed_rows, gate_up_rows))], axis=1
     )
-    second_grads[-1] = after(second_grads[-1], [ffn_grads])
     ffn_share = lax.psum_scatter(ffn_grads, "dp", scatter_dimension=0, tiled=True)
     ffn_sums = lax.all_gather(ffn_share, "dp", axis=0, tiled=True)
     for piece in range(PIECES):
@@ -906,18 +932,6 @@
     input_sum.advance(branch_sum.advance())
     input_sum.advance(branch_sum.advance())
     input_sum.advance(branch_sum.advance(), [grad_down, grad_gate, grad_up])
-    input_sum.advance(branch_sum.advance())
-    branch_sums = branch_sum.finish().astype(jnp.float32)
-    grad_mixer_proj, attention_output_gradient = branch_sums[:channels], branch_sums[channels:]
-    input_sum.advance([grad_mixer_proj, attention_output_gradient])
-    step_start = 2 * channels + state_width
-    query_start = step_start + LANES
-    key_start = query_start + query_heads * HD
-    grad_gating, grad_inner, grad_state, grad_step, grad_query, grad_key, grad_value = jnp.split(
-        input_sum.finish().astype(jnp.float32),
-        [channels, 2 * channels, step_start, query_start, key_start, key_start + kv_heads * HD],
-        axis=1,
-    )
     taps = inner_conv.shape[0]
     grad_inner_conv, grad_mixer_gain = inner_sums[:taps], inner_sums[taps]
     grad_skip_scale = jnp.sum(inner_sums[taps + 1].reshape(head_local, P_SIZE), axis=1)
@@ -935,7 +949,35 @@
             grad_skip_scale,
         ]
     )
-    small = sum_small(jnp.concatenate([both(shared_small), own_small]))
+    small = jnp.concatenate([both(shared_small), own_small])
+    small_bits = bits_in_order(False)
+    for bit in small_bits:
+        got = flip(small, bit)
+        if bit == small_bits[-2]:
+            input_sum.advance(branch_sum.advance(), [got])
+        small = small + got
+    branch_sums = branch_sum.finish().astype(jnp.float32)
+    grad_mixer_proj, attention_output_gradient = branch_sums[:channels], branch_sums[channels:]
+    input_sum.advance([grad_mixer_proj, attention_output_gradient, small, input_grad, block_output])
+    own_share, other_share, share_place = input_sum.finish()
+    step_start = 2 * channels + state_width
+    query_start = step_start + LANES
+    key_start = query_start + query_heads * HD
+    value_start = key_start + kv_heads * HD
+    grad_gating, grad_inner, grad_state, grad_step, grad_query, grad_key, grad_value = unpack(
+        own_share,
+        other_share,
+        share_place,
+        [
+            (0, channels),
+            (channels, channels),
+            (2 * channels, state_width),
+            (step_start, head_local),
+            (query_start, query_heads * HD),
+            (key_start, kv_heads * HD),
+            (value_start, kv_heads * HD),
+        ],
+    )
     shared_small, own_small = small[: shared_small.shape[0]], small[shared_small.shape[0] :]
     grad_state_conv, grad_first_gain, grad_second_gain = jnp.split(
         shared_small, [taps * state_width, taps * state_width + model_width]
@@ -951,7 +993,7 @@
         grad_gating,
         grad_inner,
         grad_state,
-        grad_step[:, :head_local],
+        grad_step,
         grad_step_bias,
         grad_decay_log,
         grad_skip_scale,

time: 512 us -> 493 us (0.963)
  waiting for transfers between devices: 194 us -> 171 us
  Pallas kernels: 71.3 us -> 78.4 us
  matrix products: 77.3 us -> 70.5 us
  other arithmetic: 58.9 us -> 52.5 us
  starting transfers between devices: 38.1 us -> 44.2 us
    ppermute x26, waiting for transfers between devices: 105 us -> 81.3 us  [flip(): return lax.ppermute(value, 'dp', [(i, i ^ bit) for i in range(size)])]
    select_n x13 -> x12, other arithmetic: 16.4 us -> 5.01 us  [in_order(): first = jnp.where(place == 0, own, other)]
    convert_element_type x14, other arithmetic: 7.41 us -> 15.1 us  [low(): return v.astype(jnp.bfloat16)]
    pallas_call x0 -> x1, Pallas kernels: none -> 7.7 us  [unpack(): pl.pallas_call(functools.partial(unpack_kernel, [start for start, _ in co...]
    unnamed x217 -> x201, local copies, waits for them, and re-layouts: 19.8 us -> 26.9 us
    dot_general x18, matrix products: 29.4 us -> 22.8 us  [dense(): return jnp.dot(left_side, right_side, preferred_element_type=jnp.float32)]
    ppermute x26, starting transfers between devices: 15.8 us -> 22.2 us  [flip(): return lax.ppermute(value, 'dp', [(i, i ^ bit) for i in range(size)])]
    split x1 -> x0, local copies, waits for them, and re-layouts: 6.1 us -> none  [on_device(): jnp.split(input_sum.finish().astype(jnp.float32), [channels, 2 * channels...]
  transfers between devices with their start and end apart: 45 -> 45, of which waited for: 27 -> 24; matrix products, arithmetic and copies ran while one was open for 22% -> 25% of each run, Pallas kernels for 14% -> 15%
where the time goes in v4:
time: 493 us; the launch traced here: 484 us
  waiting for transfers between devices  171 us (35%)
  Pallas kernels  78.4 us (16%)
  matrix products  70.5 us (14%)
  other arithmetic  52.5 us (11%)
  local copies, waits for them, and re-layouts  52.2 us (11%)
  starting transfers between devices  44.2 us (9%)
  between operations  16.2 us (3%)
    ppermute x17, waiting for transfers between devices, swap_tensor(): return lax.ppermute(value, 'tensor', [(0, 1), (1, 0)])  81.7 us
    ppermute x26, waiting for transfers between devices, flip(): return lax.ppermute(value, 'dp', [(i, i ^ bit) for i in range(size)])  81.3 us
    pallas_call x1, Pallas kernels, mixer_backward(): pl.pallas_call(mixer_backward_kernel, grid=(count,), in_specs=[rows_of(ch...  31.8 us
    dot_general x16, matrix products, back_dot(): lax.dot_general(left_side, right_side, (((1,), (1,)), ((), ())), preferre...  30.4 us
    unnamed x201, local copies, waits for them, and re-layouts  26.9 us
    dot_general x18, matrix products, dense(): return jnp.dot(left_side, right_side, preferred_element_type=jnp.float32)  22.8 us
    ppermute x26, starting transfers between devices, flip(): return lax.ppermute(value, 'dp', [(i, i ^ bit) for i in range(size)])  22.2 us
    ppermute x17, starting transfers between devices, swap_tensor(): return lax.ppermute(value, 'tensor', [(0, 1), (1, 0)])  21.9 us
  transfers between devices with their start and end apart: 45, of which 24 were waited for; matrix products, arithmetic and copies ran while one was open for 25% of the time, Pallas kernels for 15%

profile of v4, /device:TPU:0, one launch (start us, length us, event | category | flops | bytes accessed | tf_op | source)
XLA Modules:
  0.0 484.5 jit_solution(10108188831769082929)
XLA Ops:
  27.1 12.2 %collective-permute-done = bf16[512,1024]{1,0:T(8,128)(2,1)} collective-permute-done((bf16[512,1024]{1,0:T(8,128)(2,1)}, bf16[512,1024]{1,0:T(8,128)(2,1)}, u32[]{:S(2)}, u32[]{:S(2)}) %collective-permute-start) | collective-permute-done | bytes 1048608 | tf_op jit(solution)/shard_map/ppermute | solution.py:62
  44.4 7.7 %fusion.124.inner_ref.gating_ref.state_ref.step_ref.inner_before_ref.state_before_ref = f32[1024,1920]{1,0:T(8,128)} fusion(bf16[512,1024]{1,0:T(8,128)(2,1)S(1)} %get-tuple-element.227, bf16[512,1024]{1,0:T(8,128)(2,1)S(1)} %get-tuple-element.226, bf16[1024,12]{1,0:T(8,128)(2,1)S(1)} %copy-done.71, bf16[1024,256]{1,0:T(8,128)(2,1)S(1)} %copy-done.89, ...), kind=kOutput, calls=%fused_computation.263 | convolution fusion | flops 4050386944 | bytes 13656064 | tf_op jit(solution)/shard_map/dot_general | solution.py:27
  52.1 19.2 %mixer_forward.1 = (f32[1024,768]{1,0:T(8,128)S(1)}, bf16[1024,768]{1,0:T(8,128)(2,1)S(1)}, f32[1024,1]{1,0:T(8,128)S(1)}, bf16[8,128,768]{2,1,0:T(8,128)(2,1)S(1)}) custom-call(f32[1024,1920]{1,0:T(8,128)} %fusion.124.inner_ref.gating_ref.state_ref.step_ref.inner_before_ref.state_before_ref, ...), custom_call_target="tpu_custom_call" | custom-call | flops 6000000000 | bytes 14680064 | tf_op jit(solution)/shard_map/mixer_forward/pallas_call | solution.py:655
  74.0 7.9 %attention_forward.1 = (bf16[1024,256]{1,0:T(8,128)(2,1)S(1)}, f32[1024,4]{1,0:T(8,128)S(1)}) custom-call(f32[1024,384]{1,0:T(8,128)S(1)} %fusion.123.projected_ref, s32[1024,1]{1,0:T(8,128)S(1)} %copy.90.segment_column_ref, s32[1,1024]{1,0:T(1,128)S(1)} %copy-done.11, f32[1024,128]{1,0:T(8,128)S(1)} %get-tuple-element.278.cosine_ref, ...), custom_call_target="tpu_custom_call" | custom-call | flops 5000000000 | bytes 5242880 | tf_op jit(solution)/shard_map/attention_forward/pallas_call | solution.py:600
  94.8 10.7 %collective-permute-done.6 = bf16[256,1024]{1,0:T(8,128)(2,1)S(1)} collective-permute-done((bf16[256,1024]{1,0:T(8,128)(2,1)S(1)}, bf16[256,1024]{1,0:T(8,128)(2,1)S(1)}, u32[]{:S(2)}, u32[]{:S(2)}) %collective-permute-start.6) | collective-permute-done | bytes 524320 | tf_op jit(solution)/shard_map/ppermute | solution.py:62
  106.0 7.6 %collective-permute-done.2 = bf16[256,1024]{1,0:T(8,128)(2,1)S(1)} collective-permute-done((bf16[256,1024]{1,0:T(8,128)(2,1)S(1)}, bf16[256,1024]{1,0:T(8,128)(2,1)S(1)}, u32[]{:S(2)}, u32[]{:S(2)}) %collective-permute-start.2) | collective-permute-done | bytes 524320 | tf_op jit(solution)/shard_map/ppermute | solution.py:62
  121.1 15.4 %collective-permute-done.7 = bf16[256,1024]{1,0:T(8,128)(2,1)S(1)} collective-permute-done((bf16[256,1024]{1,0:T(8,128)(2,1)S(1)}, bf16[256,1024]{1,0:T(8,128)(2,1)S(1)}, u32[]{:S(2)}, u32[]{:S(2)}) %collective-permute-start.7) | collective-permute-done | bytes 524320 | tf_op jit(solution)/shard_map/ppermute | solution.py:62
  182.5 6.8 %collective-permute-done.8 = bf16[256,1024]{1,0:T(8,128)(2,1)S(1)} collective-permute-done((bf16[256,1024]{1,0:T(8,128)(2,1)}, bf16[256,1024]{1,0:T(8,128)(2,1)S(1)}, u32[]{:S(2)}, u32[]{:S(2)}) %collective-permute-start.8) | collective-permute-done | bytes 524320 | tf_op jit(solution)/shard_map/ppermute | solution.py:62
  189.2 6.3 %collective-permute-done.5 = bf16[256,1024]{1,0:T(8,128)(2,1)S(1)} collective-permute-done((bf16[256,1024]{1,0:T(8,128)(2,1)S(1)}, bf16[256,1024]{1,0:T(8,128)(2,1)S(1)}, u32[]{:S(2)}, u32[]{:S(2)}) %collective-permute-start.5) | collective-permute-done | bytes 524320 | tf_op jit(solution)/shard_map/ppermute | solution.py:62
  203.1 17.4 %collective-permute-done.9 = bf16[256,1024]{1,0:T(8,128)(2,1)S(1)} collective-permute-done((bf16[256,1024]{1,0:T(8,128)(2,1)S(1)}, bf16[256,1024]{1,0:T(8,128)(2,1)S(1)}, u32[]{:S(2)}, u32[]{:S(2)}) %collective-permute-start.9) | collective-permute-done | bytes 524320 | tf_op jit(solution)/shard_map/ppermute | solution.py:62
  236.0 11.8 %attention_backward.1 = bf16[1024,384]{1,0:T(8,128)(2,1)S(1)} custom-call(f32[1024,384]{1,0:T(8,128)S(1)} %copy-done.18, bf16[1024,256]{1,0:T(8,128)(2,1)S(1)} %convolution_convert_fusion.3.grad_ref, f32[1024,4]{1,0:T(8,128)S(1)} %copy-done.20, s32[1024,1]{1,0:T(8,128)S(1)} %copy.90.segment_column_ref, s32[1,1024]{1,0:T(1,128)S(1)} %copy-done.11, ...), custom_call_target="tpu_custom_call" | custom-call | flops 10000000000 | bytes 6291456 | tf_op jit(solution)/shard_map/attention_backward/pallas_call | solution.py:620
  250.7 7.5 %reduce-scatter.2.cloned.1.call-done = bf16[64,3072]{1,0:T(8,128)(2,1)} async-done(((bf16[1024,3072]{1,0:T(8,128)(2,1)}), bf16[64,3072]{1,0:T(8,128)(2,1)}) %reduce-scatter.2.cloned.1.call-update) | async-done | bytes 393232 | tf_op jit(solution)/shard_map/reduce_scatter | solution.py:861
  261.5 31.8 %mixer_backward.1 = (bf16[1024,1920]{1,0:T(8,128)(2,1)S(1)}, f32[8,768]{1,0:T(8,128)S(1)}, f32[8,256]{1,0:T(8,128)S(1)}, f32[8,128]{1,0:T(8,128)S(1)}) custom-call(f32[1024,768]{1,0:T(8,128)S(1)} %copy-done.16, f32[1024,2]{1,0:T(8,128)S(1)} %copy.97.stats_ref, bf16[1024,768]{1,0:T(8,128)(2,1)S(1)} %copy-done.13, ...), custom_call_target="tpu_custom_call" | custom-call | flops 20000000000 | bytes 20971520 | tf_op jit(solution)/shard_map/mixer_backward/pallas_call | solution.py:702
  298.3 4.8 convolution_convert_fusion
  316.9 11.1 %collective-permute-done.17 = bf16[256,1024]{1,0:T(8,128)(2,1)S(1)} collective-permute-done((bf16[256,1024]{1,0:T(8,128)(2,1)S(1)}, bf16[256,1024]{1,0:T(8,128)(2,1)S(1)}, u32[]{:S(2)}, u32[]{:S(2)}) %collective-permute-start.17) | collective-permute-done | bytes 524320 | tf_op jit(solution)/shard_map/ppermute | solution.py:94
  329.7 14.0 %collective-permute-done.20 = bf16[128,1024]{1,0:T(8,128)(2,1)} collective-permute-done((bf16[128,1024]{1,0:T(8,128)(2,1)}, bf16[128,1024]{1,0:T(8,128)(2,1)}, u32[]{:S(2)}, u32[]{:S(2)}) %collective-permute-start.20) | collective-permute-done | bytes 262176 | tf_op jit(solution)/shard_map/ppermute | solution.py:94
  369.7 9.1 %collective-permute-done.37 = f32[6948]{0:T(1024)S(1)} collective-permute-done((f32[6948]{0:T(1024)S(1)}, f32[6948]{0:T(1024)S(1)}, u32[]{:S(2)}, u32[]{:S(2)}) %collective-permute-start.37) | collective-permute-done | bytes 27824 | tf_op jit(solution)/shard_map/ppermute | solution.py:94
  378.9 5.8 %collective-permute-done.38 = f32[6948]{0:T(1024)S(1)} collective-permute-done((f32[6948]{0:T(1024)S(1)}, f32[6948]{0:T(1024)S(1)}, u32[]{:S(2)}, u32[]{:S(2)}) %collective-permute-start.38) | collective-permute-done | bytes 27824 | tf_op jit(solution)/shard_map/ppermute | solution.py:94
  394.2 6.5 %collective-permute-done.22 = bf16[128,1152]{1,0:T(8,128)(2,1)} collective-permute-done((bf16[128,1152]{1,0:T(8,128)(2,1)S(1)}, bf16[128,1152]{1,0:T(8,128)(2,1)}, u32[]{:S(2)}, u32[]{:S(2)}) %collective-permute-start.22) | collective-permute-done | bytes 294944 | tf_op jit(solution)/shard_map/ppermute | solution.py:94
  409.3 7.6 %collective-permute-done.31 = bf16[256,1024]{1,0:T(8,128)(2,1)S(1)} collective-permute-done((bf16[256,1024]{1,0:T(8,128)(2,1)}, bf16[256,1024]{1,0:T(8,128)(2,1)S(1)}, u32[]{:S(2)}, u32[]{:S(2)}) %collective-permute-start.31) | collective-permute-done | bytes 524320 | tf_op jit(solution)/shard_map/ppermute | solution.py:94
  422.9 5.1 %fusion.131 = (f32[1024,1024]{1,0:T(8,128)}, f32[1024,1024]{1,0:T(8,128)}, f32[1024,1024]{1,0:T(8,128)}) fusion(bf16[1024,3072]{1,0:T(8,128)(2,1)S(1)} %copy-done.30), kind=kLoop, calls=%fused_computation.267 | loop fusion | bytes 25165824 | tf_op jit(solution)/shard_map/split | solution.py:929
  433.5 8.1 %collective-permute-done.32 = bf16[128,1152]{1,0:T(8,128)(2,1)S(1)} collective-permute-done((bf16[128,1152]{1,0:T(8,128)(2,1)S(1)}, bf16[128,1152]{1,0:T(8,128)(2,1)S(1)}, u32[]{:S(2)}, u32[]{:S(2)}) %collective-permute-start.32) | collective-permute-done | bytes 294944 | tf_op jit(solution)/shard_map/ppermute | solution.py:94
  450.0 6.5 %collective-permute-done.39 = bf16[256,1152]{1,0:T(8,128)(2,1)S(1)} collective-permute-done((bf16[256,1152]{1,0:T(8,128)(2,1)S(1)}, bf16[256,1152]{1,0:T(8,128)(2,1)S(1)}, u32[]{:S(2)}, u32[]{:S(2)}) %collective-permute-start.39) | collective-permute-done | bytes 589856 | tf_op jit(solution)/shard_map/ppermute | solution.py:94
  465.3 7.7 %unpack.1 = (f32[1024,768]{1,0:T(8,128)}, f32[1024,768]{1,0:T(8,128)}, f32[1024,256]{1,0:T(8,128)}, f32[1024,12]{1,0:T(8,128)S(1)}, f32[1024,256]{1,0:T(8,128)},...) custom-call(s32[1]{0:T(128)} %bitcast.4.place_ref, bf16[512,2304]{1,0:T(8,128)(2,1)S(1)} %copy-done.3, ...), custom_call_target="tpu_custom_call" | custom-call | bytes 18874368 | tf_op jit(solution)/shard_map/unpack/pallas_call | solution.py:158
  (431 shorter events, 219.7 us)
Async XLA Ops:
  7.2 250.9 %reduce-scatter.2.cloned.1.call-start = ((), (), s32[]{:S(2)}) async-start(), calls=%async_computation.1 | async-start | bytes 6684672 | tf_op jit(solution)/shard_map/reduce_scatter | solution.py:861
  12.8 26.5 %collective-permute-start = (bf16[512,1024]{1,0:T(8,128)(2,1)}, bf16[512,1024]{1,0:T(8,128)(2,1)}, u32[]{:S(2)}, u32[]{:S(2)}) collective-permute-start(bf16[512,1024]{1,0:T(8,128)(2,1)} %fusion.13), channel_id=1, source_target_pairs={{0,1},{1,0},{2,3},{3,2},{4,5},{5,4},{6,7},{7,6},{8,9},{9,8},{10,11... | collective-permute-start | bytes 3145736 | tf_op jit(solution)/shard_map/ppermute | solution.py:62
  42.6 73.9 %collective-permute-start.4 = (bf16[512,1024]{1,0:T(8,128)(2,1)}, bf16[512,1024]{1,0:T(8,128)(2,1)}, u32[]{:S(2)}, u32[]{:S(2)}) collective-permute-start(bf16[512,1024]{1,0:T(8,128)(2,1)} %param.25), channel_id=1, source_target_pairs={{0,1},{1,0},{2,3},{3,2},{4,5},{5,4},{6,7},{7,6},{8,9},{9,8},{10,11... | collective-permute-start | bytes 3145736 | tf_op jit(solution)/shard_map/ppermute | solution.py:62
  92.9 20.7 %collective-permute-start.2 = (bf16[256,1024]{1,0:T(8,128)(2,1)S(1)}, bf16[256,1024]{1,0:T(8,128)(2,1)S(1)}, u32[]{:S(2)}, u32[]{:S(2)}) collective-permute-start(bf16[256,1024]{1,0:T(8,128)(2,1)S(1)} %fusion.48), channel_id=1, source_target_pairs={{0,1},{1,0},{2,3},{3,2},{4,5},{5,4},{6,7},{7,6},{8,9},{9,8},{10,11... | collective-permute-start | bytes 1572872 | tf_op jit(solution)/shard_map/ppermute | solution.py:62
  114.4 33.0 %collective-permute-start.3 = (bf16[256,1024]{1,0:T(8,128)(2,1)S(1)}, bf16[256,1024]{1,0:T(8,128)(2,1)S(1)}, u32[]{:S(2)}, u32[]{:S(2)}) collective-permute-start(bf16[256,1024]{1,0:T(8,128)(2,1)S(1)} %get-tuple-element.260), channel_id=1, source_target_pairs={{0,1},{1,0},{2,3},{3,2},{4,5},{5,4},{6,7},{7,6},{8,9},{9,8},{10,11... | collective-permute-start | bytes 1572872 | tf_op jit(solution)/shard_map/ppermute | solution.py:62
  116.0 20.5 %collective-permute-start.7 = (bf16[256,1024]{1,0:T(8,128)(2,1)S(1)}, bf16[256,1024]{1,0:T(8,128)(2,1)S(1)}, u32[]{:S(2)}, u32[]{:S(2)}) collective-permute-start(bf16[256,1024]{1,0:T(8,128)(2,1)S(1)} %get-tuple-element.261), channel_id=1, source_target_pairs={{0,1},{1,0},{2,3},{3,2},{4,5},{5,4},{6,7},{7,6},{8,9},{9,8},{10,11... | collective-permute-start | bytes 1572872 | tf_op jit(solution)/shard_map/ppermute | solution.py:62
  171.3 233.8 %all-gather.2.cloned.1.call-start = ((), (), s32[]{:S(2)}) async-start(), calls=%async_computation.2 | async-start | bytes 6684672 | tf_op jit(solution)/shard_map/all_gather | solution.py:862
  179.2 16.3 %collective-permute-start.5 = (bf16[256,1024]{1,0:T(8,128)(2,1)S(1)}, bf16[256,1024]{1,0:T(8,128)(2,1)S(1)}, u32[]{:S(2)}, u32[]{:S(2)}) collective-permute-start(bf16[256,1024]{1,0:T(8,128)(2,1)S(1)} %fusion.47), channel_id=1, source_target_pairs={{0,1},{1,0},{2,3},{3,2},{4,5},{5,4},{6,7},{7,6},{8,9},{9,8},{10,11... | collective-permute-start | bytes 1572872 | tf_op jit(solution)/shard_map/ppermute | solution.py:62
  200.0 20.5 %collective-permute-start.10 = (bf16[256,1024]{1,0:T(8,128)(2,1)S(1)}, bf16[256,1024]{1,0:T(8,128)(2,1)S(1)}, u32[]{:S(2)}, u32[]{:S(2)}) collective-permute-start(bf16[256,1024]{1,0:T(8,128)(2,1)S(1)} %get-tuple-element.206), channel_id=1, source_target_pairs={{0,1},{1,0},{2,3},{3,2},{4,5},{5,4},{6,7},{7,6},{8,9},{9,8},{10,11... | collective-permute-start | bytes 1572872 | tf_op jit(solution)/shard_map/ppermute | solution.py:62
  201.8 18.7 %collective-permute-start.9 = (bf16[256,1024]{1,0:T(8,128)(2,1)S(1)}, bf16[256,1024]{1,0:T(8,128)(2,1)S(1)}, u32[]{:S(2)}, u32[]{:S(2)}) collective-permute-start(bf16[256,1024]{1,0:T(8,128)(2,1)S(1)} %get-tuple-element.232), channel_id=1, source_target_pairs={{0,1},{1,0},{2,3},{3,2},{4,5},{5,4},{6,7},{7,6},{8,9},{9,8},{10,11... | collective-permute-start | bytes 1572872 | tf_op jit(solution)/shard_map/ppermute | solution.py:62
  226.4 21.5 %collective-permute-start.13 = (f32[1024,1]{0,1:T(1,128)S(1)}, f32[1024,1]{0,1:T(1,128)S(1)}, u32[]{:S(2)}, u32[]{:S(2)}) collective-permute-start(f32[1024,1]{0,1:T(1,128)S(1)} %bitcast.56), channel_id=1, source_target_pairs={{0,1},{1,0},{2,3},{3,2},{4,5},{5,4},{6,7},{7,6},{8,9},{9,8},{10,11... | collective-permute-start | bytes 12296 | tf_op jit(solution)/shard_map/ppermute | solution.py:62
  228.9 19.0 %collective-permute-start.11 = (bf16[256,1024]{1,0:T(8,128)(2,1)S(1)}, bf16[256,1024]{1,0:T(8,128)(2,1)S(1)}, u32[]{:S(2)}, u32[]{:S(2)}) collective-permute-start(bf16[256,1024]{1,0:T(8,128)(2,1)S(1)} %fusion.76), channel_id=1, source_target_pairs={{0,1},{1,0},{2,3},{3,2},{4,5},{5,4},{6,7},{7,6},{8,9},{9,8},{10,11... | collective-permute-start | bytes 1572872 | tf_op jit(solution)/shard_map/ppermute | solution.py:62
  229.2 19.4 %collective-permute-start.12 = (bf16[256,1024]{1,0:T(8,128)(2,1)S(1)}, bf16[256,1024]{1,0:T(8,128)(2,1)S(1)}, u32[]{:S(2)}, u32[]{:S(2)}) collective-permute-start(bf16[256,1024]{1,0:T(8,128)(2,1)S(1)} %fusion.56), channel_id=1, source_target_pairs={{0,1},{1,0},{2,3},{3,2},{4,5},{5,4},{6,7},{7,6},{8,9},{9,8},{10,11... | collective-permute-start | bytes 1572872 | tf_op jit(solution)/shard_map/ppermute | solution.py:62
  234.7 15.8 %collective-permute-start.14 = (bf16[512,1024]{1,0:T(8,128)(2,1)S(1)}, bf16[512,1024]{1,0:T(8,128)(2,1)}, u32[]{:S(2)}, u32[]{:S(2)}) collective-permute-start(bf16[512,1024]{1,0:T(8,128)(2,1)S(1)} %fusion.51), channel_id=1, source_target_pairs={{0,2},{2,0},{4,6},{6,4},{8,10},{10,8},{12,14},{14,12},{16,18},{18,... | collective-permute-start | bytes 3145736 | tf_op jit(solution)/shard_map/ppermute | solution.py:94
  295.9 32.2 %collective-permute-start.17 = (bf16[256,1024]{1,0:T(8,128)(2,1)S(1)}, bf16[256,1024]{1,0:T(8,128)(2,1)S(1)}, u32[]{:S(2)}, u32[]{:S(2)}) collective-permute-start(bf16[256,1024]{1,0:T(8,128)(2,1)S(1)} %constant_dynamic-slice_fusion.8), channel_id=1, source_target_pairs={{0,8},{2,10},{4,12},{6,14},{8,0},{10,2},{12,4},{14,6},{16,24},{18,... | collective-permute-start | bytes 1572872 | tf_op jit(solution)/shard_map/ppermute | solution.py:94
  306.4 52.3 %collective-permute-start.16 = (bf16[512,2304]{1,0:T(8,128)(2,1)}, bf16[512,2304]{1,0:T(8,128)(2,1)}, u32[]{:S(2)}, u32[]{:S(2)}) collective-permute-start(bf16[512,2304]{1,0:T(8,128)(2,1)} %fusion.10), channel_id=1, source_target_pairs={{0,2},{2,0},{4,6},{6,4},{8,10},{10,8},{12,14},{14,12},{16,18},{18,... | collective-permute-start | bytes 7077896 | tf_op jit(solution)/shard_map/ppermute | solution.py:94
  315.4 37.0 %collective-permute-start.15 = (bf16[512,1024]{1,0:T(8,128)(2,1)}, bf16[512,1024]{1,0:T(8,128)(2,1)}, u32[]{:S(2)}, u32[]{:S(2)}) collective-permute-start(bf16[512,1024]{1,0:T(8,128)(2,1)} %add_convert_fusion.2), channel_id=1, source_target_pairs={{0,1},{1,0},{2,3},{3,2},{4,5},{5,4},{6,7},{7,6},{8,9},{9,8},{10,11... | collective-permute-start | bytes 3145736 | tf_op jit(solution)/shard_map/ppermute | solution.py:62
  364.2 20.9 %collective-permute-start.18 = (bf16[256,1152]{1,0:T(8,128)(2,1)}, bf16[256,1152]{1,0:T(8,128)(2,1)}, u32[]{:S(2)}, u32[]{:S(2)}) collective-permute-start(bf16[256,1152]{1,0:T(8,128)(2,1)} %constant_dynamic-slice_fusion.7), channel_id=1, source_target_pairs={{0,4},{2,6},{4,0},{6,2},{8,12},{10,14},{12,8},{14,10},{16,20},{18,... | collective-permute-start | bytes 1769480 | tf_op jit(solution)/shard_map/ppermute | solution.py:94
  365.0 20.0 %collective-permute-start.19 = (bf16[256,1152]{1,0:T(8,128)(2,1)S(1)}, bf16[256,1152]{1,0:T(8,128)(2,1)}, u32[]{:S(2)}, u32[]{:S(2)}) collective-permute-start(bf16[256,1152]{1,0:T(8,128)(2,1)S(1)} %constant_dynamic-slice_fusion.6), channel_id=1, source_target_pairs={{0,8},{2,10},{4,12},{6,14},{8,0},{10,2},{12,4},{14,6},{16,24},{18,... | collective-permute-start | bytes 1769480 | tf_op jit(solution)/shard_map/ppermute | solution.py:94
  367.5 24.0 %collective-permute-start.29 = (bf16[128,1024]{1,0:T(8,128)(2,1)S(1)}, bf16[128,1024]{1,0:T(8,128)(2,1)S(1)}, u32[]{:S(2)}, u32[]{:S(2)}) collective-permute-start(bf16[128,1024]{1,0:T(8,128)(2,1)S(1)} %pad_maximum_fusion.25), channel_id=1, source_target_pairs={{0,16},{2,18},{4,20},{6,22},{8,24},{10,26},{12,28},{14,30},{16,0},... | collective-permute-start | bytes 786440 | tf_op jit(solution)/shard_map/ppermute | solution.py:94
  384.7 48.0 %collective-permute-start.41 = (f32[6948]{0:T(1024)S(1)}, f32[6948]{0:T(1024)}, u32[]{:S(2)}, u32[]{:S(2)}) collective-permute-start(f32[6948]{0:T(1024)S(1)} %add.393), channel_id=1, source_target_pairs={{0,16},{2,18},{4,20},{6,22},{8,24},{10,26},{12,28},{14,30},{16,0},... | collective-permute-start | bytes 83384 | tf_op jit(solution)/shard_map/ppermute | solution.py:94
  392.5 24.4 %collective-permute-start.31 = (bf16[256,1024]{1,0:T(8,128)(2,1)}, bf16[256,1024]{1,0:T(8,128)(2,1)S(1)}, u32[]{:S(2)}, u32[]{:S(2)}) collective-permute-start(bf16[256,1024]{1,0:T(8,128)(2,1)} %pad_maximum_fusion.22), channel_id=1, source_target_pairs={{0,8},{2,10},{4,12},{6,14},{8,0},{10,2},{12,4},{14,6},{16,24},{18,... | collective-permute-start | bytes 1572872 | tf_op jit(solution)/shard_map/ppermute | solution.py:94
  417.2 16.3 %collective-permute-start.34 = (bf16[512,1024]{1,0:T(8,128)(2,1)S(1)}, bf16[512,1024]{1,0:T(8,128)(2,1)S(1)}, u32[]{:S(2)}, u32[]{:S(2)}) collective-permute-start(bf16[512,1024]{1,0:T(8,128)(2,1)S(1)} %pad_maximum_fusion.12), channel_id=1, source_target_pairs={{0,2},{2,0},{4,6},{6,4},{8,10},{10,8},{12,14},{14,12},{16,18},{18,... | collective-permute-start | bytes 3145736 | tf_op jit(solution)/shard_map/ppermute | solution.py:94
  428.3 15.3 %collective-permute-start.33 = (bf16[128,1152]{1,0:T(8,128)(2,1)S(1)}, bf16[128,1152]{1,0:T(8,128)(2,1)S(1)}, u32[]{:S(2)}, u32[]{:S(2)}) collective-permute-start(bf16[128,1152]{1,0:T(8,128)(2,1)S(1)} %pad_maximum_fusion.24), channel_id=1, source_target_pairs={{0,16},{2,18},{4,20},{6,22},{8,24},{10,26},{12,28},{14,30},{16,0},... | collective-permute-start | bytes 884744 | tf_op jit(solution)/shard_map/ppermute | solution.py:94
  (117 other events, 1180.0 us)
Sparse Core Ops, SparseCore 0:
  171.5 86.6 reduce-scatter.1
  260.7 67.3 all-gather.1

commit v5 on v4

--- a/solution.py
+++ b/solution.py
@@ -153,13 +153,14 @@
 
 def unpack(own, other, place, columns):
     half_rows, width = own.shape
-    steps = half_rows // SPAN
-    rows = pl.BlockSpec((SPAN, width), lambda i: (i % steps, 0))
+    block = 2 * SPAN
+    steps = half_rows // block
+    rows = pl.BlockSpec((block, width), lambda i: (i % steps, 0))
     return pl.pallas_call(
         functools.partial(unpack_kernel, [start for start, _ in columns]),
         grid=(2 * steps,),
         in_specs=[pl.BlockSpec(memory_space=pltpu.SMEM), rows, rows],
-        out_specs=[pl.BlockSpec((SPAN, size), lambda i: (i, 0)) for _, size in columns],
+        out_specs=[pl.BlockSpec((block, size), lambda i: (i, 0)) for _, size in columns],
         out_shape=[jax.ShapeDtypeStruct((2 * half_rows, size), jnp.float32) for _, size in columns],
         compiler_params=pltpu.CompilerParams(vmem_limit_bytes=40 * 2**20),
         cost_estimate=pl.CostEstimate(

time: 493 us -> 492 us (level)
  no operation moved by 1% of the time
where the time goes in v5:
time: 492 us; the launch traced here: 483 us
  waiting for transfers between devices  171 us (35%)
  Pallas kernels  76.9 us (16%)
  matrix products  70.5 us (14%)
  other arithmetic  52.5 us (11%)
  local copies, waits for them, and re-layouts  52.2 us (11%)
  starting transfers between devices  44.2 us (9%)
  between operations  16.2 us (3%)
    ppermute x17, waiting for transfers between devices, swap_tensor(): return lax.ppermute(value, 'tensor', [(0, 1), (1, 0)])  81.7 us
    ppermute x26, waiting for transfers between devices, flip(): return lax.ppermute(value, 'dp', [(i, i ^ bit) for i in range(size)])  81.3 us
    pallas_call x1, Pallas kernels, mixer_backward(): pl.pallas_call(mixer_backward_kernel, grid=(count,), in_specs=[rows_of(ch...  31.8 us
    dot_general x16, matrix products, back_dot(): lax.dot_general(left_side, right_side, (((1,), (1,)), ((), ())), preferre...  30.4 us
    unnamed x201, local copies, waits for them, and re-layouts  26.9 us
    dot_general x18, matrix products, dense(): return jnp.dot(left_side, right_side, preferred_element_type=jnp.float32)  22.8 us
    ppermute x26, starting transfers between devices, flip(): return lax.ppermute(value, 'dp', [(i, i ^ bit) for i in range(size)])  22.2 us
    ppermute x17, starting transfers between devices, swap_tensor(): return lax.ppermute(value, 'tensor', [(0, 1), (1, 0)])  21.9 us
  transfers between devices with their start and end apart: 45, of which 24 were waited for; matrix products, arithmetic and copies ran while one was open for 25% of the time, Pallas kernels for 15%

profile of v5, /device:TPU:0, one launch (start us, length us, event | category | flops | bytes accessed | tf_op | source)
XLA Modules:
  0.0 483.0 jit_solution(16207561666947797510)
XLA Ops:
  27.1 12.2 %collective-permute-done = bf16[512,1024]{1,0:T(8,128)(2,1)} collective-permute-done((bf16[512,1024]{1,0:T(8,128)(2,1)}, bf16[512,1024]{1,0:T(8,128)(2,1)}, u32[]{:S(2)}, u32[]{:S(2)}) %collective-permute-start) | collective-permute-done | bytes 1048608 | tf_op jit(solution)/shard_map/ppermute | solution.py:62
  44.4 7.7 %fusion.124.inner_ref.gating_ref.state_ref.step_ref.inner_before_ref.state_before_ref = f32[1024,1920]{1,0:T(8,128)} fusion(bf16[512,1024]{1,0:T(8,128)(2,1)S(1)} %get-tuple-element.227, bf16[512,1024]{1,0:T(8,128)(2,1)S(1)} %get-tuple-element.226, bf16[1024,12]{1,0:T(8,128)(2,1)S(1)} %copy-done.71, bf16[1024,256]{1,0:T(8,128)(2,1)S(1)} %copy-done.89, ...), kind=kOutput, calls=%fused_computation.263 | convolution fusion | flops 4050386944 | bytes 13656064 | tf_op jit(solution)/shard_map/dot_general | solution.py:27
  52.1 19.2 %mixer_forward.1 = (f32[1024,768]{1,0:T(8,128)S(1)}, bf16[1024,768]{1,0:T(8,128)(2,1)S(1)}, f32[1024,1]{1,0:T(8,128)S(1)}, bf16[8,128,768]{2,1,0:T(8,128)(2,1)S(1)}) custom-call(f32[1024,1920]{1,0:T(8,128)} %fusion.124.inner_ref.gating_ref.state_ref.step_ref.inner_before_ref.state_before_ref, ...), custom_call_target="tpu_custom_call" | custom-call | flops 6000000000 | bytes 14680064 | tf_op jit(solution)/shard_map/mixer_forward/pallas_call | solution.py:656
  74.0 7.9 %attention_forward.1 = (bf16[1024,256]{1,0:T(8,128)(2,1)S(1)}, f32[1024,4]{1,0:T(8,128)S(1)}) custom-call(f32[1024,384]{1,0:T(8,128)S(1)} %fusion.123.projected_ref, s32[1024,1]{1,0:T(8,128)S(1)} %copy.90.segment_column_ref, s32[1,1024]{1,0:T(1,128)S(1)} %copy-done.11, f32[1024,128]{1,0:T(8,128)S(1)} %get-tuple-element.278.cosine_ref, ...), custom_call_target="tpu_custom_call" | custom-call | flops 5000000000 | bytes 5242880 | tf_op jit(solution)/shard_map/attention_forward/pallas_call | solution.py:601
  94.8 10.7 %collective-permute-done.6 = bf16[256,1024]{1,0:T(8,128)(2,1)S(1)} collective-permute-done((bf16[256,1024]{1,0:T(8,128)(2,1)S(1)}, bf16[256,1024]{1,0:T(8,128)(2,1)S(1)}, u32[]{:S(2)}, u32[]{:S(2)}) %collective-permute-start.6) | collective-permute-done | bytes 524320 | tf_op jit(solution)/shard_map/ppermute | solution.py:62
  106.0 7.6 %collective-permute-done.2 = bf16[256,1024]{1,0:T(8,128)(2,1)S(1)} collective-permute-done((bf16[256,1024]{1,0:T(8,128)(2,1)S(1)}, bf16[256,1024]{1,0:T(8,128)(2,1)S(1)}, u32[]{:S(2)}, u32[]{:S(2)}) %collective-permute-start.2) | collective-permute-done | bytes 524320 | tf_op jit(solution)/shard_map/ppermute | solution.py:62
  121.1 15.4 %collective-permute-done.7 = bf16[256,1024]{1,0:T(8,128)(2,1)S(1)} collective-permute-done((bf16[256,1024]{1,0:T(8,128)(2,1)S(1)}, bf16[256,1024]{1,0:T(8,128)(2,1)S(1)}, u32[]{:S(2)}, u32[]{:S(2)}) %collective-permute-start.7) | collective-permute-done | bytes 524320 | tf_op jit(solution)/shard_map/ppermute | solution.py:62
  182.5 6.8 %collective-permute-done.8 = bf16[256,1024]{1,0:T(8,128)(2,1)S(1)} collective-permute-done((bf16[256,1024]{1,0:T(8,128)(2,1)}, bf16[256,1024]{1,0:T(8,128)(2,1)S(1)}, u32[]{:S(2)}, u32[]{:S(2)}) %collective-permute-start.8) | collective-permute-done | bytes 524320 | tf_op jit(solution)/shard_map/ppermute | solution.py:62
  189.2 6.3 %collective-permute-done.5 = bf16[256,1024]{1,0:T(8,128)(2,1)S(1)} collective-permute-done((bf16[256,1024]{1,0:T(8,128)(2,1)S(1)}, bf16[256,1024]{1,0:T(8,128)(2,1)S(1)}, u32[]{:S(2)}, u32[]{:S(2)}) %collective-permute-start.5) | collective-permute-done | bytes 524320 | tf_op jit(solution)/shard_map/ppermute | solution.py:62
  203.1 17.4 %collective-permute-done.9 = bf16[256,1024]{1,0:T(8,128)(2,1)S(1)} collective-permute-done((bf16[256,1024]{1,0:T(8,128)(2,1)S(1)}, bf16[256,1024]{1,0:T(8,128)(2,1)S(1)}, u32[]{:S(2)}, u32[]{:S(2)}) %collective-permute-start.9) | collective-permute-done | bytes 524320 | tf_op jit(solution)/shard_map/ppermute | solution.py:62
  236.0 11.8 %attention_backward.1 = bf16[1024,384]{1,0:T(8,128)(2,1)S(1)} custom-call(f32[1024,384]{1,0:T(8,128)S(1)} %copy-done.18, bf16[1024,256]{1,0:T(8,128)(2,1)S(1)} %convolution_convert_fusion.3.grad_ref, f32[1024,4]{1,0:T(8,128)S(1)} %copy-done.20, s32[1024,1]{1,0:T(8,128)S(1)} %copy.90.segment_column_ref, s32[1,1024]{1,0:T(1,128)S(1)} %copy-done.11, ...), custom_call_target="tpu_custom_call" | custom-call | flops 10000000000 | bytes 6291456 | tf_op jit(solution)/shard_map/attention_backward/pallas_call | solution.py:621
  250.7 7.5 %reduce-scatter.2.cloned.1.call-done = bf16[64,3072]{1,0:T(8,128)(2,1)} async-done(((bf16[1024,3072]{1,0:T(8,128)(2,1)}), bf16[64,3072]{1,0:T(8,128)(2,1)}) %reduce-scatter.2.cloned.1.call-update) | async-done | bytes 393232 | tf_op jit(solution)/shard_map/reduce_scatter | solution.py:862
  261.5 31.8 %mixer_backward.1 = (bf16[1024,1920]{1,0:T(8,128)(2,1)S(1)}, f32[8,768]{1,0:T(8,128)S(1)}, f32[8,256]{1,0:T(8,128)S(1)}, f32[8,128]{1,0:T(8,128)S(1)}) custom-call(f32[1024,768]{1,0:T(8,128)S(1)} %copy-done.16, f32[1024,2]{1,0:T(8,128)S(1)} %copy.97.stats_ref, bf16[1024,768]{1,0:T(8,128)(2,1)S(1)} %copy-done.13, ...), custom_call_target="tpu_custom_call" | custom-call | flops 20000000000 | bytes 20971520 | tf_op jit(solution)/shard_map/mixer_backward/pallas_call | solution.py:703
  298.3 4.8 %convolution_convert_fusion = bf16[1024,1920]{1,0:T(8,128)(2,1)S(1)} fusion(bf16[1024,1024]{1,0:T(8,128)(2,1)S(1)} %copy-done.53, bf16[1024,1920]{1,0:T(8,128)(2,1)S(1)} %get-tuple-element.79), kind=kOutput, calls=%fused_computation.15 | convolution fusion | flops 4028497920 | bytes 9961472 | tf_op jit(solution)/shard_map/dot_general | solution.py:31
  316.9 11.1 %collective-permute-done.17 = bf16[256,1024]{1,0:T(8,128)(2,1)S(1)} collective-permute-done((bf16[256,1024]{1,0:T(8,128)(2,1)S(1)}, bf16[256,1024]{1,0:T(8,128)(2,1)S(1)}, u32[]{:S(2)}, u32[]{:S(2)}) %collective-permute-start.17) | collective-permute-done | bytes 524320 | tf_op jit(solution)/shard_map/ppermute | solution.py:94
  329.7 14.0 %collective-permute-done.20 = bf16[128,1024]{1,0:T(8,128)(2,1)} collective-permute-done((bf16[128,1024]{1,0:T(8,128)(2,1)}, bf16[128,1024]{1,0:T(8,128)(2,1)}, u32[]{:S(2)}, u32[]{:S(2)}) %collective-permute-start.20) | collective-permute-done | bytes 262176 | tf_op jit(solution)/shard_map/ppermute | solution.py:94
  369.7 9.1 %collective-permute-done.37 = f32[6948]{0:T(1024)S(1)} collective-permute-done((f32[6948]{0:T(1024)S(1)}, f32[6948]{0:T(1024)S(1)}, u32[]{:S(2)}, u32[]{:S(2)}) %collective-permute-start.37) | collective-permute-done | bytes 27824 | tf_op jit(solution)/shard_map/ppermute | solution.py:94
  378.9 5.8 %collective-permute-done.38 = f32[6948]{0:T(1024)S(1)} collective-permute-done((f32[6948]{0:T(1024)S(1)}, f32[6948]{0:T(1024)S(1)}, u32[]{:S(2)}, u32[]{:S(2)}) %collective-permute-start.38) | collective-permute-done | bytes 27824 | tf_op jit(solution)/shard_map/ppermute | solution.py:94
  394.2 6.5 %collective-permute-done.22 = bf16[128,1152]{1,0:T(8,128)(2,1)} collective-permute-done((bf16[128,1152]{1,0:T(8,128)(2,1)S(1)}, bf16[128,1152]{1,0:T(8,128)(2,1)}, u32[]{:S(2)}, u32[]{:S(2)}) %collective-permute-start.22) | collective-permute-done | bytes 294944 | tf_op jit(solution)/shard_map/ppermute | solution.py:94
  409.3 7.6 %collective-permute-done.31 = bf16[256,1024]{1,0:T(8,128)(2,1)S(1)} collective-permute-done((bf16[256,1024]{1,0:T(8,128)(2,1)}, bf16[256,1024]{1,0:T(8,128)(2,1)S(1)}, u32[]{:S(2)}, u32[]{:S(2)}) %collective-permute-start.31) | collective-permute-done | bytes 524320 | tf_op jit(solution)/shard_map/ppermute | solution.py:94
  422.9 5.1 %fusion.131 = (f32[1024,1024]{1,0:T(8,128)}, f32[1024,1024]{1,0:T(8,128)}, f32[1024,1024]{1,0:T(8,128)}) fusion(bf16[1024,3072]{1,0:T(8,128)(2,1)S(1)} %copy-done.30), kind=kLoop, calls=%fused_computation.267 | loop fusion | bytes 25165824 | tf_op jit(solution)/shard_map/split | solution.py:930
  433.5 8.1 %collective-permute-done.32 = bf16[128,1152]{1,0:T(8,128)(2,1)S(1)} collective-permute-done((bf16[128,1152]{1,0:T(8,128)(2,1)S(1)}, bf16[128,1152]{1,0:T(8,128)(2,1)S(1)}, u32[]{:S(2)}, u32[]{:S(2)}) %collective-permute-start.32) | collective-permute-done | bytes 294944 | tf_op jit(solution)/shard_map/ppermute | solution.py:94
  450.0 6.5 %collective-permute-done.39 = bf16[256,1152]{1,0:T(8,128)(2,1)S(1)} collective-permute-done((bf16[256,1152]{1,0:T(8,128)(2,1)S(1)}, bf16[256,1152]{1,0:T(8,128)(2,1)S(1)}, u32[]{:S(2)}, u32[]{:S(2)}) %collective-permute-start.39) | collective-permute-done | bytes 589856 | tf_op jit(solution)/shard_map/ppermute | solution.py:94
  465.3 6.2 %unpack.1 = (f32[1024,768]{1,0:T(8,128)}, f32[1024,768]{1,0:T(8,128)}, f32[1024,256]{1,0:T(8,128)}, f32[1024,12]{1,0:T(8,128)S(1)}, f32[1024,256]{1,0:T(8,128)},...) custom-call(s32[1]{0:T(128)} %bitcast.4.place_ref, bf16[512,2304]{1,0:T(8,128)(2,1)S(1)} %copy-done.3, ...), custom_call_target="tpu_custom_call" | custom-call | bytes 18874368 | tf_op jit(solution)/shard_map/unpack/pallas_call | solution.py:159
  (431 shorter events, 219.7 us)
Async XLA Ops:
  7.2 250.9 %reduce-scatter.2.cloned.1.call-start = ((), (), s32[]{:S(2)}) async-start(), calls=%async_computation.1 | async-start | bytes 6684672 | tf_op jit(solution)/shard_map/reduce_scatter | solution.py:862
  12.8 26.5 %collective-permute-start = (bf16[512,1024]{1,0:T(8,128)(2,1)}, bf16[512,1024]{1,0:T(8,128)(2,1)}, u32[]{:S(2)}, u32[]{:S(2)}) collective-permute-start(bf16[512,1024]{1,0:T(8,128)(2,1)} %fusion.13), channel_id=1, source_target_pairs={{0,1},{1,0},{2,3},{3,2},{4,5},{5,4},{6,7},{7,6},{8,9},{9,8},{10,11... | collective-permute-start | bytes 3145736 | tf_op jit(solution)/shard_map/ppermute | solution.py:62
  42.6 73.9 %collective-permute-start.4 = (bf16[512,1024]{1,0:T(8,128)(2,1)}, bf16[512,1024]{1,0:T(8,128)(2,1)}, u32[]{:S(2)}, u32[]{:S(2)}) collective-permute-start(bf16[512,1024]{1,0:T(8,128)(2,1)} %param.25), channel_id=1, source_target_pairs={{0,1},{1,0},{2,3},{3,2},{4,5},{5,4},{6,7},{7,6},{8,9},{9,8},{10,11... | collective-permute-start | bytes 3145736 | tf_op jit(solution)/shard_map/ppermute | solution.py:62
  92.9 20.7 %collective-permute-start.2 = (bf16[256,1024]{1,0:T(8,128)(2,1)S(1)}, bf16[256,1024]{1,0:T(8,128)(2,1)S(1)}, u32[]{:S(2)}, u32[]{:S(2)}) collective-permute-start(bf16[256,1024]{1,0:T(8,128)(2,1)S(1)} %fusion.48), channel_id=1, source_target_pairs={{0,1},{1,0},{2,3},{3,2},{4,5},{5,4},{6,7},{7,6},{8,9},{9,8},{10,11... | collective-permute-start | bytes 1572872 | tf_op jit(solution)/shard_map/ppermute | solution.py:62
  114.4 33.0 %collective-permute-start.3 = (bf16[256,1024]{1,0:T(8,128)(2,1)S(1)}, bf16[256,1024]{1,0:T(8,128)(2,1)S(1)}, u32[]{:S(2)}, u32[]{:S(2)}) collective-permute-start(bf16[256,1024]{1,0:T(8,128)(2,1)S(1)} %get-tuple-element.260), channel_id=1, source_target_pairs={{0,1},{1,0},{2,3},{3,2},{4,5},{5,4},{6,7},{7,6},{8,9},{9,8},{10,11... | collective-permute-start | bytes 1572872 | tf_op jit(solution)/shard_map/ppermute | solution.py:62
  116.0 20.5 %collective-permute-start.7 = (bf16[256,1024]{1,0:T(8,128)(2,1)S(1)}, bf16[256,1024]{1,0:T(8,128)(2,1)S(1)}, u32[]{:S(2)}, u32[]{:S(2)}) collective-permute-start(bf16[256,1024]{1,0:T(8,128)(2,1)S(1)} %get-tuple-element.261), channel_id=1, source_target_pairs={{0,1},{1,0},{2,3},{3,2},{4,5},{5,4},{6,7},{7,6},{8,9},{9,8},{10,11... | collective-permute-start | bytes 1572872 | tf_op jit(solution)/shard_map/ppermute | solution.py:62
  171.3 233.8 %all-gather.2.cloned.1.call-start = ((), (), s32[]{:S(2)}) async-start(), calls=%async_computation.2 | async-start | bytes 6684672 | tf_op jit(solution)/shard_map/all_gather | solution.py:863
  179.2 16.3 %collective-permute-start.5 = (bf16[256,1024]{1,0:T(8,128)(2,1)S(1)}, bf16[256,1024]{1,0:T(8,128)(2,1)S(1)}, u32[]{:S(2)}, u32[]{:S(2)}) collective-permute-start(bf16[256,1024]{1,0:T(8,128)(2,1)S(1)} %fusion.47), channel_id=1, source_target_pairs={{0,1},{1,0},{2,3},{3,2},{4,5},{5,4},{6,7},{7,6},{8,9},{9,8},{10,11... | collective-permute-start | bytes 1572872 | tf_op jit(solution)/shard_map/ppermute | solution.py:62
  200.0 20.5 %collective-permute-start.10 = (bf16[256,1024]{1,0:T(8,128)(2,1)S(1)}, bf16[256,1024]{1,0:T(8,128)(2,1)S(1)}, u32[]{:S(2)}, u32[]{:S(2)}) collective-permute-start(bf16[256,1024]{1,0:T(8,128)(2,1)S(1)} %get-tuple-element.206), channel_id=1, source_target_pairs={{0,1},{1,0},{2,3},{3,2},{4,5},{5,4},{6,7},{7,6},{8,9},{9,8},{10,11... | collective-permute-start | bytes 1572872 | tf_op jit(solution)/shard_map/ppermute | solution.py:62
  201.8 18.7 %collective-permute-start.9 = (bf16[256,1024]{1,0:T(8,128)(2,1)S(1)}, bf16[256,1024]{1,0:T(8,128)(2,1)S(1)}, u32[]{:S(2)}, u32[]{:S(2)}) collective-permute-start(bf16[256,1024]{1,0:T(8,128)(2,1)S(1)} %get-tuple-element.232), channel_id=1, source_target_pairs={{0,1},{1,0},{2,3},{3,2},{4,5},{5,4},{6,7},{7,6},{8,9},{9,8},{10,11... | collective-permute-start | bytes 1572872 | tf_op jit(solution)/shard_map/ppermute | solution.py:62
  226.4 21.5 %collective-permute-start.13 = (f32[1024,1]{0,1:T(1,128)S(1)}, f32[1024,1]{0,1:T(1,128)S(1)}, u32[]{:S(2)}, u32[]{:S(2)}) collective-permute-start(f32[1024,1]{0,1:T(1,128)S(1)} %bitcast.56), channel_id=1, source_target_pairs={{0,1},{1,0},{2,3},{3,2},{4,5},{5,4},{6,7},{7,6},{8,9},{9,8},{10,11... | collective-permute-start | bytes 12296 | tf_op jit(solution)/shard_map/ppermute | solution.py:62
  228.9 19.0 %collective-permute-start.11 = (bf16[256,1024]{1,0:T(8,128)(2,1)S(1)}, bf16[256,1024]{1,0:T(8,128)(2,1)S(1)}, u32[]{:S(2)}, u32[]{:S(2)}) collective-permute-start(bf16[256,1024]{1,0:T(8,128)(2,1)S(1)} %fusion.76), channel_id=1, source_target_pairs={{0,1},{1,0},{2,3},{3,2},{4,5},{5,4},{6,7},{7,6},{8,9},{9,8},{10,11... | collective-permute-start | bytes 1572872 | tf_op jit(solution)/shard_map/ppermute | solution.py:62
  229.2 19.4 %collective-permute-start.12 = (bf16[256,1024]{1,0:T(8,128)(2,1)S(1)}, bf16[256,1024]{1,0:T(8,128)(2,1)S(1)}, u32[]{:S(2)}, u32[]{:S(2)}) collective-permute-start(bf16[256,1024]{1,0:T(8,128)(2,1)S(1)} %fusion.56), channel_id=1, source_target_pairs={{0,1},{1,0},{2,3},{3,2},{4,5},{5,4},{6,7},{7,6},{8,9},{9,8},{10,11... | collective-permute-start | bytes 1572872 | tf_op jit(solution)/shard_map/ppermute | solution.py:62
  234.7 15.8 %collective-permute-start.14 = (bf16[512,1024]{1,0:T(8,128)(2,1)S(1)}, bf16[512,1024]{1,0:T(8,128)(2,1)}, u32[]{:S(2)}, u32[]{:S(2)}) collective-permute-start(bf16[512,1024]{1,0:T(8,128)(2,1)S(1)} %fusion.51), channel_id=1, source_target_pairs={{0,2},{2,0},{4,6},{6,4},{8,10},{10,8},{12,14},{14,12},{16,18},{18,... | collective-permute-start | bytes 3145736 | tf_op jit(solution)/shard_map/ppermute | solution.py:94
  295.9 32.2 %collective-permute-start.17 = (bf16[256,1024]{1,0:T(8,128)(2,1)S(1)}, bf16[256,1024]{1,0:T(8,128)(2,1)S(1)}, u32[]{:S(2)}, u32[]{:S(2)}) collective-permute-start(bf16[256,1024]{1,0:T(8,128)(2,1)S(1)} %constant_dynamic-slice_fusion.8), channel_id=1, source_target_pairs={{0,8},{2,10},{4,12},{6,14},{8,0},{10,2},{12,4},{14,6},{16,24},{18,... | collective-permute-start | bytes 1572872 | tf_op jit(solution)/shard_map/ppermute | solution.py:94
  306.4 52.3 %collective-permute-start.16 = (bf16[512,2304]{1,0:T(8,128)(2,1)}, bf16[512,2304]{1,0:T(8,128)(2,1)}, u32[]{:S(2)}, u32[]{:S(2)}) collective-permute-start(bf16[512,2304]{1,0:T(8,128)(2,1)} %fusion.10), channel_id=1, source_target_pairs={{0,2},{2,0},{4,6},{6,4},{8,10},{10,8},{12,14},{14,12},{16,18},{18,... | collective-permute-start | bytes 7077896 | tf_op jit(solution)/shard_map/ppermute | solution.py:94
  315.4 37.0 %collective-permute-start.15 = (bf16[512,1024]{1,0:T(8,128)(2,1)}, bf16[512,1024]{1,0:T(8,128)(2,1)}, u32[]{:S(2)}, u32[]{:S(2)}) collective-permute-start(bf16[512,1024]{1,0:T(8,128)(2,1)} %add_convert_fusion.2), channel_id=1, source_target_pairs={{0,1},{1,0},{2,3},{3,2},{4,5},{5,4},{6,7},{7,6},{8,9},{9,8},{10,11... | collective-permute-start | bytes 3145736 | tf_op jit(solution)/shard_map/ppermute | solution.py:62
  364.2 20.9 %collective-permute-start.18 = (bf16[256,1152]{1,0:T(8,128)(2,1)}, bf16[256,1152]{1,0:T(8,128)(2,1)}, u32[]{:S(2)}, u32[]{:S(2)}) collective-permute-start(bf16[256,1152]{1,0:T(8,128)(2,1)} %constant_dynamic-slice_fusion.7), channel_id=1, source_target_pairs={{0,4},{2,6},{4,0},{6,2},{8,12},{10,14},{12,8},{14,10},{16,20},{18,... | collective-permute-start | bytes 1769480 | tf_op jit(solution)/shard_map/ppermute | solution.py:94
  365.0 20.0 %collective-permute-start.19 = (bf16[256,1152]{1,0:T(8,128)(2,1)S(1)}, bf16[256,1152]{1,0:T(8,128)(2,1)}, u32[]{:S(2)}, u32[]{:S(2)}) collective-permute-start(bf16[256,1152]{1,0:T(8,128)(2,1)S(1)} %constant_dynamic-slice_fusion.6), channel_id=1, source_target_pairs={{0,8},{2,10},{4,12},{6,14},{8,0},{10,2},{12,4},{14,6},{16,24},{18,... | collective-permute-start | bytes 1769480 | tf_op jit(solution)/shard_map/ppermute | solution.py:94
  367.5 24.0 %collective-permute-start.29 = (bf16[128,1024]{1,0:T(8,128)(2,1)S(1)}, bf16[128,1024]{1,0:T(8,128)(2,1)S(1)}, u32[]{:S(2)}, u32[]{:S(2)}) collective-permute-start(bf16[128,1024]{1,0:T(8,128)(2,1)S(1)} %pad_maximum_fusion.25), channel_id=1, source_target_pairs={{0,16},{2,18},{4,20},{6,22},{8,24},{10,26},{12,28},{14,30},{16,0},... | collective-permute-start | bytes 786440 | tf_op jit(solution)/shard_map/ppermute | solution.py:94
  384.7 48.0 %collective-permute-start.41 = (f32[6948]{0:T(1024)S(1)}, f32[6948]{0:T(1024)}, u32[]{:S(2)}, u32[]{:S(2)}) collective-permute-start(f32[6948]{0:T(1024)S(1)} %add.393), channel_id=1, source_target_pairs={{0,16},{2,18},{4,20},{6,22},{8,24},{10,26},{12,28},{14,30},{16,0},... | collective-permute-start | bytes 83384 | tf_op jit(solution)/shard_map/ppermute | solution.py:94
  392.5 24.4 %collective-permute-start.31 = (bf16[256,1024]{1,0:T(8,128)(2,1)}, bf16[256,1024]{1,0:T(8,128)(2,1)S(1)}, u32[]{:S(2)}, u32[]{:S(2)}) collective-permute-start(bf16[256,1024]{1,0:T(8,128)(2,1)} %pad_maximum_fusion.22), channel_id=1, source_target_pairs={{0,8},{2,10},{4,12},{6,14},{8,0},{10,2},{12,4},{14,6},{16,24},{18,... | collective-permute-start | bytes 1572872 | tf_op jit(solution)/shard_map/ppermute | solution.py:94
  417.2 16.3 %collective-permute-start.34 = (bf16[512,1024]{1,0:T(8,128)(2,1)S(1)}, bf16[512,1024]{1,0:T(8,128)(2,1)S(1)}, u32[]{:S(2)}, u32[]{:S(2)}) collective-permute-start(bf16[512,1024]{1,0:T(8,128)(2,1)S(1)} %pad_maximum_fusion.12), channel_id=1, source_target_pairs={{0,2},{2,0},{4,6},{6,4},{8,10},{10,8},{12,14},{14,12},{16,18},{18,... | collective-permute-start | bytes 3145736 | tf_op jit(solution)/shard_map/ppermute | solution.py:94
  428.3 15.3 %collective-permute-start.33 = (bf16[128,1152]{1,0:T(8,128)(2,1)S(1)}, bf16[128,1152]{1,0:T(8,128)(2,1)S(1)}, u32[]{:S(2)}, u32[]{:S(2)}) collective-permute-start(bf16[128,1152]{1,0:T(8,128)(2,1)S(1)} %pad_maximum_fusion.24), channel_id=1, source_target_pairs={{0,16},{2,18},{4,20},{6,22},{8,24},{10,26},{12,28},{14,30},{16,0},... | collective-permute-start | bytes 884744 | tf_op jit(solution)/shard_map/ppermute | solution.py:94
  (117 other events, 1178.5 us)
Sparse Core Ops, SparseCore 0:
  171.5 86.6 reduce-scatter.1
  260.7 67.3 all-gather.1
